TPU v7x, 512 devices: a whole 4x4x16 slice. The times are simulated.
512 devices in a mesh: space: 8 (over y, x_lo), filt: 64 (over x_hi, z, core).
Axes of the slice: x: 4 (x_hi: 2, x_lo: 2; x = x_hi * 2 + x_lo), y: 4, z: 16, core: 2. Of those that a mesh axis runs over, the one named last changes fastest.
Arguments:
- quantized: bfloat16 [256, 8, 128, 128], P('filt', 'space'), may hold values from -6 to 6
- scales: float32 [256, 8], P('filt', 'space'), may hold values from 0.3 to 3
- weights: bfloat16 [256, 27, 256], P('filt'), may hold values from -0.078125 to 0.078125
- cotangent: bfloat16 [256, 8, 128, 128], P('filt', 'space'), may hold values from -6 to 6
Outputs:
- output: bfloat16 [256, 8, 128, 128], P('filt', 'space')
- input_grad: bfloat16 [256, 8, 128, 128], P('filt', 'space')
- weight_grad: float32 [256, 27, 256], P('filt')
All inputs are finite; a program needn't handle non-finite values.
Results may differ from a plain program's by a relative error of at most 0.0049.
Values may be sent and summed in bfloat16 or wider, within the bound.
No kernel may reach another device: no remote copies, remote signals or barrier semaphores. Data moves between devices by JAX's collectives and lax.ppermute only.
A program may use at most 64 MiB of HBM per device.

v0:
```python
import math

import jax
import jax.numpy as jnp
from jax import lax
from jax.sharding import PartitionSpec as P


def padded_2(cells, sides, width):
    for axis, dim in sides:
        count = lax.axis_size(axis)
        ends = count - 1
        head = lax.slice_in_dim(cells, 0, width, axis=dim)
        tail = lax.slice_in_dim(cells, cells.shape[dim] - width, cells.shape[dim], axis=dim)
        cells = jnp.concatenate(
            [
                lax.ppermute(tail, axis, [(i, (i + 1) % count) for i in range(ends)]),
                cells,
                lax.ppermute(head, axis, [((i + 1) % count, i) for i in range(ends)]),
            ],
            axis=dim,
        )
    return cells


def flatten_rim(rimmed):
    merged = rimmed.reshape(rimmed.shape[0], rimmed.shape[1], rimmed.shape[2] * rimmed.shape[3])
    return jnp.pad(merged, ((0, 0), (0, 0), (1, 1)))


def tap_window(padded, along_depth, along_rows, along_cols, depth_cells, row_cells, plane_cols):
    span = row_cells * plane_cols
    start = along_rows * plane_cols + along_cols
    window = padded[:, along_depth : along_depth + depth_cells, start : start + span]
    if along_cols != 1:
        columns = lax.broadcasted_iota(jnp.int32, (1, 1, span), 2) % plane_cols + (along_cols - 1)
        inside = (columns >= 0) & (columns < plane_cols)
        window = jnp.where(inside, window, jnp.zeros((), window.dtype))
    return window.reshape(padded.shape[0], -1)


def local(quantized, scales, weights, cotangent):
    in_local, depth_cells, plane_rows, plane_cols = quantized.shape
    out_local = cotangent.shape[0]
    filt_count = lax.axis_size("filt")
    space_count = lax.axis_size("space")
    row_cells = plane_rows // filt_count
    dequant = (quantized.astype(jnp.float32) * scales[:, :, None, None]).astype(jnp.bfloat16)
    combined = jnp.concatenate([dequant, cotangent], axis=0)
    filters = lax.all_gather(weights, "filt", axis=0, tiled=True)
    exchanged = lax.all_to_all(combined, "filt", split_axis=2, concat_axis=0, tiled=True)
    rimmed = padded_2(exchanged, (("space", 1), ("filt", 2)), 1)
    rim_shape = rimmed.shape[1:]
    grouped = rimmed.reshape((filt_count, in_local + out_local) + rim_shape)
    input_rim = flatten_rim(grouped[:, :in_local].reshape((filt_count * in_local,) + rim_shape))
    grad_rim = flatten_rim(grouped[:, in_local:].reshape((filt_count * out_local,) + rim_shape))
    cot_inner = tap_window(grad_rim, 1, 1, 1, depth_cells, row_cells, plane_cols)
    forward_sum = None
    backward_sum = None
    grad_taps = []
    for tap_index in range(27):
        along_depth = tap_index // 9
        along_rows = tap_index // 3 % 3
        along_cols = tap_index % 3
        ahead = tap_window(
            input_rim, along_depth, along_rows, along_cols, depth_cells, row_cells, plane_cols
        )
        behind = tap_window(
            grad_rim,
            2 - along_depth,
            2 - along_rows,
            2 - along_cols,
            depth_cells,
            row_cells,
            plane_cols,
        )
        tap_filter = filters[:, tap_index, :]
        forward_term = lax.dot_general(
            tap_filter, ahead, (((0,), (0,)), ((), ())), preferred_element_type=jnp.float32
        )
        backward_term = jnp.dot(tap_filter, behind, preferred_element_type=jnp.float32)
        grad_taps.append(
            lax.dot_general(
                ahead, cot_inner, (((1,), (1,)), ((), ())), preferred_element_type=jnp.float32
            )
        )
        forward_sum = forward_term if forward_sum is None else forward_sum + forward_term
        backward_sum = backward_term if backward_sum is None else backward_sum + backward_term
    output_cells = forward_sum.reshape(
        grad_rim.shape[0], depth_cells, row_cells, plane_cols
    ).astype(jnp.bfloat16)
    input_cells = backward_sum.reshape(
        input_rim.shape[0], depth_cells, row_cells, plane_cols
    ).astype(jnp.bfloat16)
    output, input_grad = (
        lax.all_to_all(output_cells, "filt", split_axis=0, concat_axis=2, tiled=True),
        lax.all_to_all(input_cells, "filt", split_axis=0, concat_axis=2, tiled=True),
    )
    grad_norm = 1.0 / math.sqrt(depth_cells * space_count * plane_rows * plane_cols)
    partial_grad = jnp.stack(grad_taps, axis=1) * grad_norm
    pieces = lax.all_to_all(partial_grad[None], "filt", split_axis=1, concat_axis=0, tiled=True)
    summed = jnp.sum(pieces, axis=0)
    weight_grad = lax.psum(summed, "space")
    return (output, input_grad, weight_grad)


def solution(mesh):
    placed = (
        P("filt", "space", None, None),
        P("filt", "space"),
        P("filt", None, None),
        P("filt", "space", None, None),
    )
    return jax.shard_map(
        local,
        mesh=mesh,
        in_specs=placed,
        out_specs=(
            P("filt", "space", None, None),
            P("filt", "space", None, None),
            P("filt", None, None),
        ),
        check_vma=False,
    )
```

profile of v0, /device:TPU:1, one launch (start us, length us, event | category | flops | bytes accessed | tf_op | source)
XLA Modules:
  0.0 702.6 jit_solution(9651337668184229448)
XLA Ops:
  8.0 1.0 multiply_convert_fusion
  10.2 43.2 %all_to_all.66 = bf16[8,1,128,128]{3,0,1,2:T(8,128)(2,1)S(1)} all-to-all(bf16[8,1,128,128]{3,0,1,2:T(8,128)(2,1)S(1)} %copy.169), channel_id=1, replica_groups=mesh['space'=8,'filt'=64] {'filt'}, dimensions={2} | all-to-all | bytes 524288 | tf_op jit(solution)/shard_map/all_to_all | solution.py:51
  53.3 1.3 collective-permute-start.1
  54.6 4.0 collective-permute-start
  58.7 4.9 collective-permute-done.1
  64.6 3.4 collective-permute-start.2
  67.9 1.9 collective-permute-start.3
  69.9 1.5 copy.172
  71.4 1.3 collective-permute-done.2
  72.6 4.4 collective-permute-done.3
  78.0 1.0 copy.243
  79.3 1.0 copy.215
  93.7 1.0 fusion.20
  94.6 0.9 fusion.19
  103.0 0.9 fusion.10
  105.8 114.1 %all-gather.2.cloned.1.call-done = bf16[256,27,256]{2,1,0:T(8,128)(2,1)} async-done(((bf16[4,27,256]{2,1,0:T(8,128)(2,1)}), bf16[256,27,256]{2,1,0:T(8,128)(2,1)}) %all-gather.2.cloned.1.call-update) | async-done | bytes 3538960 | tf_op jit(solution)/shard_map/all_gather | solution.py:50
  219.9 5.8 fusion.258
  226.1 4.7 fusion.257
  239.4 7.9 %all-to-all-start.1 = ((bf16[256,1,2,128]{3,2,1,0:T(2,128)(2,1)}), bf16[256,1,2,128]{3,2,1,0:T(2,128)(2,1)S(1)}, u32[]{:S(2)}, u32[]{:S(2)}) async-start(bf16[256,1,2,128]{3,2,1,0:T(2,128)(2,1)} %copy.200), calls=%async_computation.1 | async-start | bytes 262144 | tf_op jit(solution)/shard_map/all_to_all | solution.py:96
  247.3 3.6 broadcast_multiply_fusion
  250.9 9.9 %copy.207 = f32[1,256,27,256]{3,0,2,1:T(1,128)} copy(f32[1,256,27,256]{3,1,2,0:T(8,128)S(1)} %broadcast_multiply_fusion) | data formatting | bytes 14155776 | tf_op jit(solution)/shard_map/mul | solution.py:100
  260.8 5.1 all-to-all-done.1
  265.9 10.4 %all-to-all-start.3 = ((f32[1,256,27,256]{3,0,2,1:T(1,128)}), f32[1,256,27,256]{3,0,2,1:T(1,128)}, u32[]{:S(2)}, u32[]{:S(2)}) async-start(f32[1,256,27,256]{3,0,2,1:T(1,128)} %copy.207), calls=%async_computation.3 | async-start | bytes 14155776 | tf_op jit(solution)/shard_map/all_to_all | solution.py:101
  277.4 1.2 convolution_bitcast_fusion.34
  278.6 1.2 convolution_add_fusion.15
  287.2 300.3 %all-to-all-done.3 = f32[1,256,27,256]{3,0,2,1:T(1,128)} async-done(((f32[1,256,27,256]{3,0,2,1:T(1,128)}), f32[1,256,27,256]{3,0,2,1:T(1,128)}, u32[]{:S(2)}, u32[]{:S(2)}) %all-to-all-start.3) | async-done | bytes 7077920 | tf_op jit(solution)/shard_map/all_to_all | solution.py:101
  587.5 8.7 %all-to-all-start.2 = ((bf16[256,1,2,128]{3,2,1,0:T(2,128)(2,1)}), bf16[256,1,2,128]{3,2,1,0:T(2,128)(2,1)S(1)}, u32[]{:S(2)}, u32[]{:S(2)}) async-start(bf16[256,1,2,128]{3,2,1,0:T(2,128)(2,1)} %copy.204), calls=%async_computation.2 | async-start | bytes 262144 | tf_op jit(solution)/shard_map/all_to_all | solution.py:97
  596.3 7.6 %copy.214 = f32[1,256,27,256]{3,2,0,1:T(8,128)} copy(f32[1,256,27,256]{3,0,2,1:T(1,128)} %all-to-all-done.3) | data formatting | bytes 14155776
  603.8 4.7 reduce_sum.9
  609.4 5.5 all-to-all-done.2
  615.7 77.8 %all-reduce.4.cloned.1.call-done = f32[4,27,256]{2,1,0:T(8,128)} async-done(((f32[4,27,256]{2,1,0:T(8,128)}), f32[4,27,256]{2,1,0:T(8,128)}) %all-reduce.4.cloned.1.call-update) | async-done | bytes 110608 | tf_op jit(solution)/shard_map/psum | solution.py:103
  693.5 1.6 copy.212
  (176 shorter events, 44.3 us)
Async XLA Ops:
  8.0 211.9 %all-gather.2.cloned.1.call-start = ((), (), s32[]{:S(2)}) async-start(), calls=%async_computation.4 | async-start | bytes 4259840 | tf_op jit(solution)/shard_map/all_gather | solution.py:50
  53.3 10.2 %collective-permute-start.1 = (bf16[512,1,2,128]{3,0,2,1:T(8,128)(2,1)S(1)}, bf16[512,1,2,128]{3,0,2,1:T(8,128)(2,1)S(1)}, u32[]{:S(2)}, u32[]{:S(2)}) collective-permute-start(bf16[512,1,2,128]{3,0,2,1:T(8,128)(2,1)S(1)} %bitcast.549), channel_id=1, source_target_pairs={{64,0},{128,64},{192,128},{256,192},{320,256},{384,320},{448,384},... | collective-permute-start | bytes 786440 | tf_op jit(solution)/shard_map/ppermute | solution.py:19
  54.6 9.8 %collective-permute-start = (bf16[512,1,2,128]{3,0,2,1:T(8,128)(2,1)S(1)}, bf16[512,1,2,128]{3,0,2,1:T(8,128)(2,1)S(1)}, u32[]{:S(2)}, u32[]{:S(2)}) collective-permute-start(bf16[512,1,2,128]{3,0,2,1:T(8,128)(2,1)S(1)} %bitcast.550), channel_id=1, source_target_pairs={{0,64},{64,128},{128,192},{192,256},{256,320},{320,384},{384,448},... | collective-permute-start | bytes 786440 | tf_op jit(solution)/shard_map/ppermute | solution.py:17
  64.6 8.1 %collective-permute-start.2 = (bf16[512,3,1,128]{3,0,2,1:T(8,128)(2,1)S(1)}, bf16[512,3,1,128]{3,0,2,1:T(8,128)(2,1)S(1)}, u32[]{:S(2)}, u32[]{:S(2)}) collective-permute-start(bf16[512,3,1,128]{3,0,2,1:T(8,128)(2,1)S(1)} %get-tuple-element.50), channel_id=1, source_target_pairs={{0,1},{1,2},{2,3},{3,4},{4,5},{5,6},{6,7},{7,8},{8,9},{9,10},{10,1... | collective-permute-start | bytes 1179656 | tf_op jit(solution)/shard_map/ppermute | solution.py:17
  67.9 9.1 %collective-permute-start.3 = (bf16[512,3,1,128]{3,0,2,1:T(8,128)(2,1)S(1)}, bf16[512,3,1,128]{3,0,2,1:T(8,128)(2,1)S(1)}, u32[]{:S(2)}, u32[]{:S(2)}) collective-permute-start(bf16[512,3,1,128]{3,0,2,1:T(8,128)(2,1)S(1)} %get-tuple-element.51), channel_id=1, source_target_pairs={{1,0},{2,1},{3,2},{4,3},{5,4},{6,5},{7,6},{8,7},{9,8},{10,9},{11,1... | collective-permute-start | bytes 1179656 | tf_op jit(solution)/shard_map/ppermute | solution.py:19
  219.9 6.2 copy-start
  225.7 6.3 copy-start.31
  225.7 6.6 copy-start.29
  225.7 6.9 copy-start.27
  225.7 7.2 %copy-start.25 = (bf16[256,1,256]{2,1,0:T(2,128)(2,1)}, bf16[256,1,256]{2,1,0:T(2,128)(2,1)S(1)}, u32[]{:S(2)}) copy-start(bf16[256,1,256]{2,1,0:T(2,128)(2,1)S(1)} %get-tuple-element.42) | copy-start | bytes 393220
  225.7 7.5 %copy-start.23 = (bf16[256,1,256]{2,1,0:T(2,128)(2,1)}, bf16[256,1,256]{2,1,0:T(2,128)(2,1)S(1)}, u32[]{:S(2)}) copy-start(bf16[256,1,256]{2,1,0:T(2,128)(2,1)S(1)} %get-tuple-element.41) | copy-start | bytes 393220
  225.7 7.8 %copy-start.21 = (bf16[256,1,256]{2,1,0:T(2,128)(2,1)}, bf16[256,1,256]{2,1,0:T(2,128)(2,1)S(1)}, u32[]{:S(2)}) copy-start(bf16[256,1,256]{2,1,0:T(2,128)(2,1)S(1)} %get-tuple-element.40) | copy-start | bytes 393220
  225.7 12.9 %copy-start.33 = (bf16[256,1,256]{2,1,0:T(2,128)(2,1)}, bf16[256,1,256]{2,1,0:T(2,128)(2,1)S(1)}, u32[]{:S(2)}) copy-start(bf16[256,1,256]{2,1,0:T(2,128)(2,1)S(1)} %get-tuple-element.46) | copy-start | bytes 393220
  230.8 5.7 copy-start.7
  230.8 6.0 copy-start.5
  230.8 6.3 copy-start.3
  230.8 6.5 copy-start.1
  239.4 26.6 %all-to-all-start.1 = ((bf16[256,1,2,128]{3,2,1,0:T(2,128)(2,1)}), bf16[256,1,2,128]{3,2,1,0:T(2,128)(2,1)S(1)}, u32[]{:S(2)}, u32[]{:S(2)}) async-start(bf16[256,1,2,128]{3,2,1,0:T(2,128)(2,1)} %copy.200), calls=%async_computation.1 | async-start | bytes 262144 | tf_op jit(solution)/shard_map/all_to_all | solution.py:96
  260.8 18.9 %copy-start.32 = (bf16[256,1,256]{2,1,0:T(2,128)(2,1)S(1)}, bf16[256,1,256]{2,1,0:T(2,128)(2,1)}, u32[]{:S(2)}) copy-start(bf16[256,1,256]{2,1,0:T(2,128)(2,1)} %copy-done.31) | copy-start | bytes 393220
  260.8 19.3 %copy-start.30 = (bf16[256,1,256]{2,1,0:T(2,128)(2,1)S(1)}, bf16[256,1,256]{2,1,0:T(2,128)(2,1)}, u32[]{:S(2)}) copy-start(bf16[256,1,256]{2,1,0:T(2,128)(2,1)} %copy-done.29) | copy-start | bytes 393220
  260.8 19.6 %copy-start.28 = (bf16[256,1,256]{2,1,0:T(2,128)(2,1)S(1)}, bf16[256,1,256]{2,1,0:T(2,128)(2,1)}, u32[]{:S(2)}) copy-start(bf16[256,1,256]{2,1,0:T(2,128)(2,1)} %copy-done.27) | copy-start | bytes 393220
  265.9 321.6 %all-to-all-start.3 = ((f32[1,256,27,256]{3,0,2,1:T(1,128)}), f32[1,256,27,256]{3,0,2,1:T(1,128)}, u32[]{:S(2)}, u32[]{:S(2)}) async-start(f32[1,256,27,256]{3,0,2,1:T(1,128)} %copy.207), calls=%async_computation.3 | async-start | bytes 14155776 | tf_op jit(solution)/shard_map/all_to_all | solution.py:101
  276.4 5.2 copy-start.38
  276.4 5.6 copy-start.36
  276.4 5.9 copy-start.20
  276.4 6.1 copy-start.18
  276.4 6.4 copy-start.16
  276.7 6.4 copy-start.14
  276.8 6.7 copy-start.12
  277.1 6.7 copy-start.10
  587.5 27.3 %all-to-all-start.2 = ((bf16[256,1,2,128]{3,2,1,0:T(2,128)(2,1)}), bf16[256,1,2,128]{3,2,1,0:T(2,128)(2,1)S(1)}, u32[]{:S(2)}, u32[]{:S(2)}) async-start(bf16[256,1,2,128]{3,2,1,0:T(2,128)(2,1)} %copy.204), calls=%async_computation.2 | async-start | bytes 262144 | tf_op jit(solution)/shard_map/all_to_all | solution.py:97
  596.2 97.3 %all-reduce.4.cloned.1.call-start = ((), (), s32[]{:S(2)}) async-start(), calls=%async_computation.5 | async-start | bytes 262144 | tf_op jit(solution)/shard_map/psum | solution.py:103
  (16 other events, 75.5 us)
Sparse Core Ops, SparseCore 0:
  71.5 148.3 all-gather.1
Sparse Core Ops, SparseCore 1:
  608.6 84.8 all-reduce.3
where the time goes:
time: 707 us; the launch traced here: 703 us
  waiting for transfers between devices  514 us (73%)
  blocking collectives  43.2 us (6%)
  matrix products  42.3 us (6%)
  local copies, waits for them, and re-layouts  37.9 us (5%)
  starting transfers between devices  37.7 us (5%)
  between operations  16.6 us (2%)
  other arithmetic  10.6 us (1%)
    all_to_all x1, waiting for transfers between devices, local(): lax.all_to_all(partial_grad[None], 'filt', split_axis=1, concat_axis=0, t...  300 us
    all_gather x1, waiting for transfers between devices, local(): filters = lax.all_gather(weights, 'filt', axis=0, tiled=True)  114 us
    psum x1, waiting for transfers between devices, local(): weight_grad = lax.psum(summed, 'space')  77.8 us
    all_to_all x1, blocking collectives, local(): lax.all_to_all(combined, 'filt', split_axis=2, concat_axis=0, tiled=True)  43.2 us
    dot_general x27, matrix products, local(): lax.dot_general(ahead, cot_inner, (((1,), (1,)), ((), ())), preferred_ele...  25.1 us
  transfers between devices with their start and end apart: 9, of which 9 were waited for; matrix products, arithmetic and copies ran while one was open for 10% of the time, Pallas kernels for 0%

commit v1 on v0

v1 whole, which is shorter than its diff:
```python
import math

import jax
import jax.numpy as jnp
from jax import lax
from jax.experimental import pallas as pl
from jax.experimental.pallas import tpu as pltpu
from jax.sharding import PartitionSpec as P


F32 = jnp.float32
BF16 = jnp.bfloat16
PARAMS = pltpu.CompilerParams(vmem_limit_bytes=32 * 1024 * 1024)


def select_rows(rows, source, columns):
    row = lax.broadcasted_iota(jnp.int32, (rows, columns), 0)
    col = lax.broadcasted_iota(jnp.int32, (rows, columns), 1)
    return jnp.where(source(row) == col, 1.0, 0.0).astype(BF16)


def moved(matrix, cells):
    return jnp.dot(matrix, cells, preferred_element_type=F32).astype(BF16)


def y_first(n):
    return ((n >> 1) & 31) * 8 + (n & 1) * 4 + (n >> 6)


def y_last(n):
    return (n & 3) * 64 + (n >> 3) * 2 + ((n >> 2) & 1)


def j_first(n):
    return (n & 1) * 128 + ((n >> 1) & 15) * 8 + (n >> 5)


def j_last(n):
    return (n & 7) * 32 + ((n >> 3) & 15) * 2 + (n >> 7)


def rim_first(n):
    return ((n >> 4) & 1) * 128 + ((n >> 1) & 7) * 16 + (n & 1) * 8 + (n >> 5) + 1


def rim_last(n):
    return jnp.where(((n & 7) >= 1) & ((n & 7) <= 6), ((n & 7) - 1) * 16 + (n >> 3), -1)


def forward_kernel(half_ref, cells_ref, mine_ref, theirs_ref, keep_ref, send_ref, dequant_ref, filter_ref, planes):
    first = half_ref[0] == 0
    by_j = select_rows(256, j_first, 256)
    for block in range(4):
        part = pl.ds(block * 128, 128)
        mine, theirs = mine_ref[part], theirs_ref[part]
        pair = jnp.concatenate([jnp.where(first, mine, theirs), jnp.where(first, theirs, mine)], axis=0)
        lanes = moved(by_j, pair)
        for j in range(7):
            filter_ref[block * 32 : block * 32 + 32, j * 128 : j * 128 + 128] = lanes[j * 32 : j * 32 + 32]
    turned = jnp.concatenate([filter_ref[:, j * 128 : j * 128 + 128].T for j in range(7)], axis=0)
    stacked = jnp.concatenate([turned[a * 288 : a * 288 + 288] for a in range(3)], axis=1)

    by_y = select_rows(256, y_first, 256)
    planes[0] = jnp.zeros((128, 512), BF16)
    planes[9] = jnp.zeros((128, 512), BF16)

    def arrange(z, _):
        for part in range(2):
            rows = moved(by_y, cells_ref[z, part * 256 : part * 256 + 256])
            for y in range(4):
                piece = rows[y * 64 : y * 64 + 64]
                planes[z + 1, part * 64 : part * 64 + 64, y * 128 : y * 128 + 128] = piece
                dequant_ref[z, part * 64 : part * 64 + 64, y * 128 : y * 128 + 128] = piece
        return 0

    lax.fori_loop(0, 8, arrange, 0)
    column = lax.broadcasted_iota(jnp.int32, (32, 128), 1)

    def plane(z, _):
        near = jnp.concatenate([planes[z], planes[z + 1], planes[z + 2]], axis=0)
        terms = jnp.dot(stacked, near, preferred_element_type=F32)
        for row in range(6):
            sums = []
            for e in range(3):
                total = None
                for b in range(3):
                    y = row + b - 2
                    if 0 <= y < 4:
                        at = b * 96 + e * 32
                        term = terms[at : at + 32, y * 128 : y * 128 + 128]
                        total = term if total is None else total + term
                sums.append(total)
            left = jnp.where(column >= 1, pltpu.roll(sums[0], 1, 1), 0.0)
            right = jnp.where(column <= 126, pltpu.roll(sums[2], 127, 1), 0.0)
            result = sums[1] + left + right
            keep_ref[z, row] = result[:16]
            send_ref[z, row] = result[16:]
        return 0

    lax.fori_loop(0, 8, plane, 0)


def backward_kernel(mine_ref, theirs_ref, dequant_ref, filter_ref, grad_ref, filter_grad_ref, shifted, image, total):
    by_rim = select_rows(192, rim_first, 256)
    before = select_rows(128, lambda n: n - 1, 128)
    after = select_rows(128, lambda n: n + 1, 128)
    shifted[0] = jnp.zeros((96, 768), BF16)
    shifted[9] = jnp.zeros((96, 768), BF16)
    image[864:896] = jnp.zeros((32, 512), BF16)
    total[...] = jnp.zeros((128, 896), F32)

    def arrange(z, _):
        rows = moved(by_rim, jnp.concatenate([mine_ref[z], theirs_ref[z]], axis=0))
        for e, cells in ((0, moved(rows, before)), (1, rows), (2, moved(rows, after))):
            for y in range(6):
                shifted[z + 1, e * 32 : e * 32 + 32, y * 128 : y * 128 + 128] = cells[y * 32 : y * 32 + 32]
        return 0

    lax.fori_loop(0, 8, arrange, 0)
    back_y = select_rows(256, y_last, 256)

    def plane(z, _):
        for a in range(3):
            for b in range(3):
                at = (a * 3 + b) * 96
                image[at : at + 96] = shifted[z + 2 - a, :, (2 - b) * 128 : (2 - b) * 128 + 512]
        grad = jnp.dot(filter_ref[...], image[...], preferred_element_type=F32).astype(BF16)
        for part in range(2):
            rows = jnp.concatenate(
                [grad[part * 64 : part * 64 + 64, y * 128 : y * 128 + 128] for y in range(4)], axis=0
            )
            grad_ref[z, part * 256 : part * 256 + 256] = moved(back_y, rows)
        total[...] += lax.dot_general(
            dequant_ref[z], image[...], (((1,), (1,)), ((), ())), preferred_element_type=F32
        )
        return 0

    lax.fori_loop(0, 8, plane, 0)
    back_j = select_rows(256, j_last, 256)
    for block in range(4):
        rows = [total[block * 32 : block * 32 + 32, j * 128 : j * 128 + 128].astype(BF16) for j in range(7)]
        rows = moved(back_j, jnp.concatenate(rows + [jnp.zeros((32, 128), BF16)], axis=0))
        filter_grad_ref[0, block * 128 : block * 128 + 128] = rows[:128]
        filter_grad_ref[1, block * 128 : block * 128 + 128] = rows[128:]


def sum_kernel(keep_ref, other_ref, out_ref):
    back_rim = select_rows(128, rim_last, 96)
    for z in range(8):
        rows = (keep_ref[z] + other_ref[z]).astype(BF16).reshape(96, 128)
        out_ref[z] = moved(back_rim, rows)


def windows(rows):
    lead = rows.shape[:-2]
    padded = jnp.pad(rows, [(0, 0)] * len(lead) + [(2, 2), (0, 0)]).reshape(lead + (33, 4, 128))
    return jnp.concatenate([padded[..., :32, :, :], padded[..., 1:, :, :]], axis=-2)


def overlapped(parts):
    lead = parts.shape[:-3]
    keep = [(0, 0)] * len(lead)
    first = jnp.pad(parts[..., :4, :], keep + [(0, 1), (0, 0), (0, 0)])
    second = jnp.pad(parts[..., 4:, :], keep + [(1, 0), (0, 0), (0, 0)])
    return (first + second).reshape(lead + (132, 128))[..., 2:130, :]


def local(quantized, scales, weights, cotangent):
    rank = lax.axis_index("filt")
    slab = lax.axis_index("space")
    x_hi = rank // 32
    swap_core = [(n, n ^ 1) for n in range(64)]
    swap_x = [(n, n ^ 32) for n in range(64)]

    dequant = (quantized.astype(F32) * scales[:, :, None, None]).astype(BF16)
    cells = dequant.reshape(2, 2, 32, 4, 128).transpose(2, 0, 1, 3, 4).reshape(64, 8, 128)
    rims = windows(cotangent.reshape(2, 2, 128, 128)).transpose(2, 0, 1, 3, 4).reshape(64, 16, 128)
    own = lax.dynamic_slice_in_dim(weights, slab * 32, 32, axis=2).reshape(2, 2, 27, 8, 2, 2)
    own = own.transpose(0, 1, 2, 4, 3, 5)
    own = jnp.stack([own[0], own[1][:, :, ::-1]], axis=1).reshape(2, 2, 864)
    own = jnp.pad(own, ((0, 0), (0, 0), (0, 160))).reshape(2, 1, 2, 8, 128)
    own = jnp.broadcast_to(own, (2, 16, 2, 8, 128)).reshape(64, 8, 128)
    got = lax.all_to_all(jnp.concatenate([cells, rims, own], axis=1), "filt", 0, 0, tiled=True)

    filters = got[:, 24:].reshape(512, 128)
    other_filters = lax.ppermute(filters, "filt", swap_x)
    cells = jnp.broadcast_to(got[:, :8].reshape(1, 512, 128), (8, 512, 128))
    rims = got[:, 8:24].reshape(8, 128, 128)
    got = lax.all_to_all(jnp.concatenate([cells, rims], axis=1), "space", 0, 0, tiled=True)
    other_rims = lax.ppermute(got[:, 512:], "filt", swap_core)

    keep, send, cells, filters = pl.pallas_call(
        forward_kernel,
        grid=(1,),
        out_shape=(
            jax.ShapeDtypeStruct((8, 6, 16, 128), F32),
            jax.ShapeDtypeStruct((8, 6, 16, 128), F32),
            jax.ShapeDtypeStruct((8, 128, 512), BF16),
            jax.ShapeDtypeStruct((128, 896), BF16),
        ),
        in_specs=[
            pl.BlockSpec(memory_space=pltpu.SMEM),
            pl.BlockSpec((8, 512, 128), lambda n: (0, 0, 0)),
            pl.BlockSpec((512, 128), lambda n: (0, 0)),
            pl.BlockSpec((512, 128), lambda n: (0, 0)),
        ],
        out_specs=(
            pl.BlockSpec((8, 6, 16, 128), lambda n: (0, 0, 0, 0)),
            pl.BlockSpec((8, 6, 16, 128), lambda n: (0, 0, 0, 0)),
            pl.BlockSpec((8, 128, 512), lambda n: (0, 0, 0)),
            pl.BlockSpec((128, 896), lambda n: (0, 0)),
        ),
        scratch_shapes=[pltpu.VMEM((10, 128, 512), BF16)],
        compiler_params=PARAMS,
        cost_estimate=pl.CostEstimate(flops=2 * 8 * 288 * 384 * 512, bytes_accessed=4 << 20, transcendentals=0),
        name="forward",
    )(x_hi.reshape(1).astype(jnp.int32), got, filters, other_filters)
    other = lax.ppermute(send, "filt", swap_core)

    grad, filter_grad = pl.pallas_call(
        backward_kernel,
        grid=(1,),
        out_shape=(
            jax.ShapeDtypeStruct((8, 512, 128), BF16),
            jax.ShapeDtypeStruct((2, 512, 128), BF16),
        ),
        in_specs=[
            pl.BlockSpec((8, 128, 128), lambda n: (0, 4, 0)),
            pl.BlockSpec((8, 128, 128), lambda n: (0, 0, 0)),
            pl.BlockSpec((8, 128, 512), lambda n: (0, 0, 0)),
            pl.BlockSpec((128, 896), lambda n: (0, 0)),
        ],
        out_specs=(
            pl.BlockSpec((8, 512, 128), lambda n: (0, 0, 0)),
            pl.BlockSpec((2, 512, 128), lambda n: (0, 0, 0)),
        ),
        scratch_shapes=[
            pltpu.VMEM((10, 96, 768), BF16),
            pltpu.VMEM((896, 512), BF16),
            pltpu.VMEM((128, 896), F32),
        ],
        compiler_params=PARAMS,
        cost_estimate=pl.CostEstimate(flops=4 * 8 * 896 * 128 * 512, bytes_accessed=4 << 20, transcendentals=0),
        name="backward",
    )(got, other_rims, cells, filters)

    filter_keep = jnp.where(x_hi == 0, filter_grad[0], filter_grad[1])
    filter_send = jnp.where(x_hi == 0, filter_grad[1], filter_grad[0])
    filter_other = lax.ppermute(filter_send, "filt", swap_x)

    out = pl.pallas_call(
        sum_kernel,
        out_shape=jax.ShapeDtypeStruct((8, 128, 128), BF16),
        compiler_params=PARAMS,
        name="sum",
    )(keep, other)

    got = lax.all_to_all(jnp.concatenate([grad, out], axis=1), "space", 0, 0, tiled=True)
    grad = jnp.sum(got[:, :512].astype(F32), axis=0).astype(BF16).reshape(64, 8, 128)
    out = got[:, 512:].reshape(64, 16, 128)
    filter_grad = (filter_keep.astype(F32) + filter_other.astype(F32)).astype(BF16).reshape(64, 8, 128)
    got = lax.all_to_all(jnp.concatenate([grad, out, filter_grad], axis=1), "filt", 0, 0, tiled=True)

    got = got.reshape(32, 2, 32, 128)
    grad = got[:, :, :8].reshape(32, 2, 2, 4, 128).transpose(1, 2, 0, 3, 4).reshape(4, 1, 128, 128)
    out = got[:, :, 8:24].reshape(32, 2, 2, 8, 128).transpose(1, 2, 0, 3, 4).astype(F32)
    out = overlapped(out).astype(BF16).reshape(4, 1, 128, 128)

    norm = 1.0 / math.sqrt(131072)
    summed = jnp.sum(got[:, :, 24:].reshape(2, 16, 2, 8, 128).astype(F32), axis=1) * norm
    summed = summed.transpose(1, 0, 2, 3).reshape(1, 32, 128)
    gathered = lax.all_to_all(jnp.broadcast_to(summed, (8, 32, 128)), "space", 0, 0, tiled=True)
    gathered = gathered.reshape(8, 2, 2, 1024)[..., :864].reshape(8, 2, 2, 27, 2, 8, 2)
    gathered = jnp.stack([gathered[:, 0], gathered[:, 1][:, :, :, ::-1]], axis=1)
    filter_grad = gathered.transpose(1, 2, 3, 0, 5, 4, 6).reshape(4, 27, 256)
    return (out, grad, filter_grad)


def solution(mesh):
    placed = (
        P("filt", "space", None, None),
        P("filt", "space"),
        P("filt", None, None),
        P("filt", "space", None, None),
    )
    return jax.shard_map(
        local,
        mesh=mesh,
        in_specs=placed,
        out_specs=(
            P("filt", "space", None, None),
            P("filt", "space", None, None),
            P("filt", None, None),
        ),
        check_vma=False,
    )
```

time: 707 us -> 184 us (0.26)
  waiting for transfers between devices: 514 us -> 36 us
  blocking collectives: 43.2 us -> 94 us
  matrix products: 42.3 us -> 0 us
  local copies, waits for them, and re-layouts: 37.9 us -> 10.7 us
  between operations: 16.6 us -> 1.08 us
  Pallas kernels: 0 us -> 15.1 us
  starting transfers between devices: 37.7 us -> 23.7 us
  other arithmetic: 10.6 us -> 3.35 us
    all_to_all x3, waiting for transfers between devices: 311 us -> 20.3 us  [the longest x1 16.7 us: local(): lax.all_to_all(jnp.concatenate([cells, rims], axis=1), 'space', 0, 0, til...]
    all_gather x1 -> x0, waiting for transfers between devices: 114 us -> none  [local(): filters = lax.all_gather(weights, 'filt', axis=0, tiled=True)]
    psum x1 -> x0, waiting for transfers between devices: 77.8 us -> none  [local(): weight_grad = lax.psum(summed, 'space')]
    all_to_all x1 -> x2, blocking collectives: 43.2 us -> 94 us  [the longest x1 52.6 us: local(): lax.all_to_all(jnp.concatenate([cells, rims, own], axis=1), 'filt', 0, 0,...]
    dot_general x81 -> x0, matrix products: 42.3 us -> none  [the longest x27 25.1 us: local(): lax.dot_general(ahead, cot_inner, (((1,), (1,)), ((), ())), preferred_ele...]
    pallas_call x0 -> x3, Pallas kernels: none -> 15.1 us  [the longest x1 9.44 us: local(): pl.pallas_call(backward_kernel, grid=(1,), out_shape=(jax.ShapeDtypeStruc...]
    all_to_all x3, starting transfers between devices: 27 us -> 13.2 us  [the longest x1 5.45 us: local(): lax.all_to_all(jnp.broadcast_to(summed, (8, 32, 128)), 'space', 0, 0, til...]
    unnamed x83 -> x8, local copies, waits for them, and re-layouts: 12.9 us -> 1.78 us
  transfers between devices with their start and end apart: 9 -> 7, of which waited for: 9 -> 3; matrix products, arithmetic and copies ran while one was open for 10% -> 1% of each run, Pallas kernels for 0% -> 8%
where the time goes in v1:
time: 184 us
  blocking collectives  94 us (51%)
  waiting for transfers between devices  36 us (20%)
  starting transfers between devices  23.7 us (13%)
  Pallas kernels  15.1 us (8%)
  local copies, waits for them, and re-layouts  10.7 us (6%)
  other arithmetic  3.35 us (2%)
    all_to_all x1, blocking collectives, local(): lax.all_to_all(jnp.concatenate([cells, rims, own], axis=1), 'filt', 0, 0,...  52.6 us
    all_to_all x1, blocking collectives, local(): lax.all_to_all(jnp.concatenate([grad, out, filter_grad], axis=1), 'filt',...  41.4 us
    all_to_all x1, waiting for transfers between devices, local(): lax.all_to_all(jnp.concatenate([cells, rims], axis=1), 'space', 0, 0, til...  16.7 us
    ppermute x1, waiting for transfers between devices, local(): filter_other = lax.ppermute(filter_send, 'filt', swap_x)  15.7 us
    pallas_call x1, Pallas kernels, local(): pl.pallas_call(backward_kernel, grid=(1,), out_shape=(jax.ShapeDtypeStruc...  9.44 us
    all_to_all x1, starting transfers between devices, local(): lax.all_to_all(jnp.broadcast_to(summed, (8, 32, 128)), 'space', 0, 0, til...  5.45 us
    pallas_call x1, Pallas kernels, local(): pl.pallas_call(forward_kernel, grid=(1,), out_shape=(jax.ShapeDtypeStruct...  5.42 us
    all_to_all x1, starting transfers between devices, local(): lax.all_to_all(jnp.concatenate([cells, rims], axis=1), 'space', 0, 0, til...  4.22 us
  transfers between devices with their start and end apart: 7, of which 3 were waited for; matrix products, arithmetic and copies ran while one was open for 1% of the time, Pallas kernels for 8%

profile of v1, /device:TPU:1, one launch (start us, length us, event | category | flops | bytes accessed | tf_op | source)
XLA Modules:
  0.0 183.9 jit_solution(1940017415584092269)
XLA Ops:
  0.7 0.8 copy-done
  1.7 0.3 copy.41
  2.1 0.3 stack.15
  2.4 0.3 copy.40
  3.0 1.0 copy.37
  4.3 0.3 maximum_bitcast_fusion.1
  5.0 52.6 %all_to_all.25 = bf16[64,32,128]{2,1,0:T(8,128)(2,1)S(1)} all-to-all(bf16[64,32,128]{2,1,0:T(8,128)(2,1)S(1)} %pad_maximum_fusion.2), channel_id=1, replica_groups=mesh['space'=8,'filt'=64] {'filt'}, dimensions={0} | all-to-all | bytes 1048576 | tf_op jit(solution)/shard_map/all_to_all | solution.py:183
  57.8 1.2 pad_maximum_fusion
  58.9 4.2 %all-to-all-start.1 = ((bf16[8,640,128]{2,1,0:T(8,128)(2,1)}), bf16[8,640,128]{2,1,0:T(8,128)(2,1)S(1)}, u32[]{:S(2)}, u32[]{:S(2)}) async-start(bf16[8,640,128]{2,1,0:T(8,128)(2,1)} %pad_maximum_fusion), calls=%async_computation.1 | async-start | bytes 2621440 | tf_op jit(solution)/shard_map/all_to_all | solution.py:189
  63.2 2.3 %collective-permute-start.1 = (bf16[512,128]{1,0:T(8,128)(2,1)S(1)}, bf16[512,128]{1,0:T(8,128)(2,1)S(1)}, u32[]{:S(2)}, u32[]{:S(2)}) collective-permute-start(bf16[512,128]{1,0:T(8,128)(2,1)S(1)} %get-tuple-element.28.mine_ref), channel_id=1, source_target_pairs={{0,32},{1,33},{2,34},{3,35},{4,36},{5,37},{6,38},{7,39},{8,40},{9,... | collective-permute-start | bytes 393224 | tf_op jit(solution)/shard_map/ppermute | solution.py:186
  65.4 16.7 %all-to-all-done.1.cells_ref.mine_ref = bf16[8,640,128]{2,1,0:T(8,128)(2,1)S(1)} async-done(((bf16[8,640,128]{2,1,0:T(8,128)(2,1)}), bf16[8,640,128]{2,1,0:T(8,128)(2,1)S(1)}, u32[]{:S(2)}, u32[]{:S(2)}) %all-to-all-start.1) | async-done | bytes 1310752 | tf_op jit(solution)/shard_map/all_to_all | solution.py:189
  82.1 1.9 %collective-permute-start = (bf16[8,128,128]{2,1,0:T(8,128)(2,1)S(1)}, bf16[8,128,128]{2,1,0:T(8,128)(2,1)S(1)}, u32[]{:S(2)}, u32[]{:S(2)}) collective-permute-start(bf16[8,128,128]{2,1,0:T(8,128)(2,1)S(1)} %slice.93), channel_id=1, source_target_pairs={{0,1},{1,0},{2,3},{3,2},{4,5},{5,4},{6,7},{7,6},{8,9},{9,8},{10,11... | collective-permute-start | bytes 786440 | tf_op jit(solution)/shard_map/ppermute | solution.py:190
  84.1 5.4 %forward.1 = (f32[8,6,16,128]{3,2,1,0:T(8,128)S(1)}, f32[8,6,16,128]{3,2,1,0:T(8,128)S(1)}, bf16[8,128,512]{2,1,0:T(8,128)(2,1)S(1)}, bf16[128,896]{1,0:T(8,128)(2,1)S(1)}) custom-call(s32[1]{0:T(128)} %bitcast.15.half_ref, bf16[8,640,128]{2,1,0:T(8,128)(2,1)S(1)} %all-to-all-done.1.cells_ref.mine_ref, bf16[512,128]{1,0:T(8,128)(2,1)S(1)} %get-tuple-element.28.mine_ref, ...), custom_call_target="tpu_custom_call" | custom-call | flops 905969664 | bytes 4194304 | tf_op jit(solution)/shard_map/forward/pallas_call | solution.py:192
  89.5 2.4 %collective-permute-start.2 = (f32[8,6,16,128]{3,2,1,0:T(8,128)S(1)}, f32[8,6,16,128]{3,2,1,0:T(8,128)S(1)}, u32[]{:S(2)}, u32[]{:S(2)}) collective-permute-start(f32[8,6,16,128]{3,2,1,0:T(8,128)S(1)} %get-tuple-element.13), channel_id=1, source_target_pairs={{0,1},{1,0},{2,3},{3,2},{4,5},{5,4},{6,7},{7,6},{8,9},{9,8},{10,11... | collective-permute-start | bytes 1179656 | tf_op jit(solution)/shard_map/ppermute | solution.py:218
  91.9 9.4 %backward.1 = (bf16[8,512,128]{2,1,0:T(8,128)(2,1)S(1)}, bf16[2,512,128]{2,1,0:T(8,128)(2,1)S(1)}) custom-call(bf16[8,640,128]{2,1,0:T(8,128)(2,1)S(1)} %all-to-all-done.1.cells_ref.mine_ref, bf16[8,128,128]{2,1,0:T(8,128)(2,1)S(1)} %collective-permute-done.theirs_ref, bf16[8,128,512]{2,1,0:T(8,128)(2,1)S(1)} %get-tuple-element.9.dequant_ref, ...), custom_call_target="tpu_custom_call" | custom-call | flops 1879048192 | bytes 4194304 | tf_op jit(solution)/shard_map/backward/pallas_call | solution.py:220
  101.6 1.2 pad_maximum_fusion.1
  102.8 3.6 %all-to-all-start.2 = ((bf16[8,640,128]{2,1,0:T(8,128)(2,1)}), bf16[8,640,128]{2,1,0:T(8,128)(2,1)S(1)}, u32[]{:S(2)}, u32[]{:S(2)}) async-start(bf16[8,640,128]{2,1,0:T(8,128)(2,1)} %pad_maximum_fusion.1), calls=%async_computation.2 | async-start | bytes 2621440 | tf_op jit(solution)/shard_map/all_to_all | solution.py:258
  106.4 3.8 %collective-permute-start.3 = (bf16[512,128]{1,0:T(8,128)(2,1)S(1)}, bf16[512,128]{1,0:T(8,128)(2,1)S(1)}, u32[]{:S(2)}, u32[]{:S(2)}) collective-permute-start(bf16[512,128]{1,0:T(8,128)(2,1)S(1)} %select_bitcast_fusion), channel_id=1, source_target_pairs={{0,32},{1,33},{2,34},{3,35},{4,36},{5,37},{6,38},{7,39},{8,40},{9,... | collective-permute-start | bytes 393224 | tf_op jit(solution)/shard_map/ppermute | solution.py:249
  110.2 15.7 %collective-permute-done.3 = bf16[512,128]{1,0:T(8,128)(2,1)S(1)} collective-permute-done((bf16[512,128]{1,0:T(8,128)(2,1)S(1)}, bf16[512,128]{1,0:T(8,128)(2,1)S(1)}, u32[]{:S(2)}, u32[]{:S(2)}) %collective-permute-start.3) | collective-permute-done | bytes 131104 | tf_op jit(solution)/shard_map/ppermute | solution.py:249
  126.2 41.4 %all_to_all.26 = bf16[64,32,128]{2,1,0:T(8,128)(2,1)S(1)} all-to-all(bf16[64,32,128]{2,1,0:T(8,128)(2,1)S(1)} %pad_maximum_fusion.3), channel_id=1, replica_groups=mesh['space'=8,'filt'=64] {'filt'}, dimensions={0} | all-to-all | bytes 1048576 | tf_op jit(solution)/shard_map/all_to_all | solution.py:262
  167.8 0.7 broadcast_in_dim.27
  168.4 5.4 %all-to-all-start.4 = ((f32[8,32,128]{2,1,0:T(8,128)}), f32[8,32,128]{2,1,0:T(8,128)S(1)}, u32[]{:S(2)}, u32[]{:S(2)}) async-start(f32[8,32,128]{2,1,0:T(8,128)} %broadcast_in_dim.27), calls=%async_computation.4 | async-start | bytes 262144 | tf_op jit(solution)/shard_map/all_to_all | solution.py:272
  173.9 0.3 copy.58
  174.4 0.7 copy.44
  175.1 0.7 copy.46
  175.9 3.7 %all-to-all-done.4 = f32[8,32,128]{2,1,0:T(8,128)S(1)} async-done(((f32[8,32,128]{2,1,0:T(8,128)}), f32[8,32,128]{2,1,0:T(8,128)S(1)}, u32[]{:S(2)}, u32[]{:S(2)}) %all-to-all-start.4) | async-done | bytes 131104 | tf_op jit(solution)/shard_map/all_to_all | solution.py:272
  179.5 0.6 copy.55
  180.3 0.9 fusion.6
  181.3 0.8 copy.50
  182.0 0.8 copy.49
  182.8 0.3 copy.51
  183.1 0.8 copy.54
  (46 shorter events, 2.4 us)
Async XLA Ops:
  0.6 0.8 copy-start
  2.3 2.4 %copy-start.1 = (bf16[4,1,128,128]{3,2,1,0:T(8,128)(2,1)S(1)}, bf16[4,1,128,128]{3,2,1,0:T(8,128)(2,1)}, u32[]{:S(2)}) copy-start(bf16[4,1,128,128]{3,2,1,0:T(8,128)(2,1)} %param.4) | copy-start | bytes 393220
  2.3 2.4 %copy-start.2 = (f32[4,1]{0,1:T(1,128)S(1)}, f32[4,1]{0,1:T(1,128)}, u32[]{:S(2)}) copy-start(f32[4,1]{0,1:T(1,128)} %param.5) | copy-start | bytes 52
  58.9 23.2 %all-to-all-start.1 = ((bf16[8,640,128]{2,1,0:T(8,128)(2,1)}), bf16[8,640,128]{2,1,0:T(8,128)(2,1)S(1)}, u32[]{:S(2)}, u32[]{:S(2)}) async-start(bf16[8,640,128]{2,1,0:T(8,128)(2,1)} %pad_maximum_fusion), calls=%async_computation.1 | async-start | bytes 2621440 | tf_op jit(solution)/shard_map/all_to_all | solution.py:189
  63.2 20.9 %collective-permute-start.1 = (bf16[512,128]{1,0:T(8,128)(2,1)S(1)}, bf16[512,128]{1,0:T(8,128)(2,1)S(1)}, u32[]{:S(2)}, u32[]{:S(2)}) collective-permute-start(bf16[512,128]{1,0:T(8,128)(2,1)S(1)} %get-tuple-element.28.mine_ref), channel_id=1, source_target_pairs={{0,32},{1,33},{2,34},{3,35},{4,36},{5,37},{6,38},{7,39},{8,40},{9,... | collective-permute-start | bytes 393224 | tf_op jit(solution)/shard_map/ppermute | solution.py:186
  82.1 9.8 %collective-permute-start = (bf16[8,128,128]{2,1,0:T(8,128)(2,1)S(1)}, bf16[8,128,128]{2,1,0:T(8,128)(2,1)S(1)}, u32[]{:S(2)}, u32[]{:S(2)}) collective-permute-start(bf16[8,128,128]{2,1,0:T(8,128)(2,1)S(1)} %slice.93), channel_id=1, source_target_pairs={{0,1},{1,0},{2,3},{3,2},{4,5},{5,4},{6,7},{7,6},{8,9},{9,8},{10,11... | collective-permute-start | bytes 786440 | tf_op jit(solution)/shard_map/ppermute | solution.py:190
  89.5 11.9 %collective-permute-start.2 = (f32[8,6,16,128]{3,2,1,0:T(8,128)S(1)}, f32[8,6,16,128]{3,2,1,0:T(8,128)S(1)}, u32[]{:S(2)}, u32[]{:S(2)}) collective-permute-start(f32[8,6,16,128]{3,2,1,0:T(8,128)S(1)} %get-tuple-element.13), channel_id=1, source_target_pairs={{0,1},{1,0},{2,3},{3,2},{4,5},{5,4},{6,7},{7,6},{8,9},{9,8},{10,11... | collective-permute-start | bytes 1179656 | tf_op jit(solution)/shard_map/ppermute | solution.py:218
  102.8 23.2 %all-to-all-start.2 = ((bf16[8,640,128]{2,1,0:T(8,128)(2,1)}), bf16[8,640,128]{2,1,0:T(8,128)(2,1)S(1)}, u32[]{:S(2)}, u32[]{:S(2)}) async-start(bf16[8,640,128]{2,1,0:T(8,128)(2,1)} %pad_maximum_fusion.1), calls=%async_computation.2 | async-start | bytes 2621440 | tf_op jit(solution)/shard_map/all_to_all | solution.py:258
  106.4 19.5 %collective-permute-start.3 = (bf16[512,128]{1,0:T(8,128)(2,1)S(1)}, bf16[512,128]{1,0:T(8,128)(2,1)S(1)}, u32[]{:S(2)}, u32[]{:S(2)}) collective-permute-start(bf16[512,128]{1,0:T(8,128)(2,1)S(1)} %select_bitcast_fusion), channel_id=1, source_target_pairs={{0,32},{1,33},{2,34},{3,35},{4,36},{5,37},{6,38},{7,39},{8,40},{9,... | collective-permute-start | bytes 393224 | tf_op jit(solution)/shard_map/ppermute | solution.py:249
  168.4 11.1 %all-to-all-start.4 = ((f32[8,32,128]{2,1,0:T(8,128)}), f32[8,32,128]{2,1,0:T(8,128)S(1)}, u32[]{:S(2)}, u32[]{:S(2)}) async-start(f32[8,32,128]{2,1,0:T(8,128)} %broadcast_in_dim.27), calls=%async_computation.4 | async-start | bytes 262144 | tf_op jit(solution)/shard_map/all_to_all | solution.py:272

commit v2 on v1

v2 whole, which is shorter than its diff:
```python
import math

import jax
import jax.numpy as jnp
from jax import lax
from jax.experimental import pallas as pl
from jax.experimental.pallas import tpu as pltpu
from jax.sharding import PartitionSpec as P


F32 = jnp.float32
BF16 = jnp.bfloat16
PARAMS = pltpu.CompilerParams(vmem_limit_bytes=32 * 1024 * 1024)
UNROLL = 2


def select_rows(rows, source, columns):
    row = lax.broadcasted_iota(jnp.int32, (rows, columns), 0)
    col = lax.broadcasted_iota(jnp.int32, (rows, columns), 1)
    return jnp.where(source(row) == col, 1.0, 0.0).astype(BF16)


def moved(matrix, cells):
    return jnp.dot(matrix, cells, preferred_element_type=F32).astype(BF16)


def y_first(n):
    return ((n >> 1) & 31) * 8 + (n & 1) * 4 + (n >> 6)


def y_last(n):
    return (n & 3) * 64 + (n >> 3) * 2 + ((n >> 2) & 1)


def n_first(n):
    return (n & 1) * 128 + ((n >> 1) & 31) * 4 + (n >> 6)


def n_last(n):
    return (n & 3) * 64 + ((n >> 2) & 31) * 2 + (n >> 7)


def rim_first(core):
    return lambda n: (((n >> 1) & 1) ^ core) * 128 + ((n >> 2) & 7) * 16 + (n & 1) * 8 + (n >> 5) + 1


def rim_last(n):
    return jnp.where(((n & 7) >= 1) & ((n & 7) <= 6), ((n & 7) - 1) * 16 + (n >> 3), -1)


def own_first(core):
    return lambda n: (n & 96) + ((n >> 1) & 7) * 4 + (((n >> 4) & 1) ^ core) * 2 + (n & 1)


def slot(rank, quarter):
    x = ((rank >> 1) & 3) ^ quarter
    return ((x & 1) << 1) | (x >> 1)


def forward_kernel(rank_ref, cells_ref, slots_ref, keep_ref, send_ref, planes_ref, filter_ref):
    rank = rank_ref[0]
    by_n = select_rows(256, n_first, 256)
    for h in range(2):
        for part in range(2):
            pair = [slots_ref[slot(rank, 2 * i + h), part * 128 : part * 128 + 128] for i in range(2)]
            lanes = moved(by_n, jnp.concatenate(pair, axis=0))
            for n in range(4 - h):
                at = (4 * h + n) * 128
                filter_ref[part * 64 : part * 64 + 64, at : at + 128] = lanes[n * 64 : n * 64 + 64]
    order = select_rows(128, own_first(rank & 1), 128)
    turned = [
        lax.dot_general(
            order,
            filter_ref[:, j * 128 : j * 128 + 128],
            (((1,), (1,)), ((), ())),
            preferred_element_type=F32,
        ).astype(BF16)
        for j in range(7)
    ]
    turned = jnp.concatenate(turned, axis=0)
    stacked = jnp.concatenate([turned[a * 288 : a * 288 + 288] for a in range(3)], axis=1)

    by_y = select_rows(256, y_first, 256)
    planes_ref[0] = jnp.zeros((128, 512), BF16)
    planes_ref[9] = jnp.zeros((128, 512), BF16)

    def arrange(z, _):
        for part in range(2):
            rows = moved(by_y, cells_ref[z, part * 256 : part * 256 + 256])
            for y in range(4):
                piece = rows[y * 64 : y * 64 + 64]
                planes_ref[z + 1, part * 64 : part * 64 + 64, y * 128 : y * 128 + 128] = piece
        return 0

    lax.fori_loop(0, 8, arrange, 0, unroll=UNROLL)
    column = lax.broadcasted_iota(jnp.int32, (32, 128), 1)

    def plane(z, _):
        near = jnp.concatenate([planes_ref[z], planes_ref[z + 1], planes_ref[z + 2]], axis=0)
        terms = jnp.dot(stacked, near, preferred_element_type=F32)
        for row in range(6):
            sums = []
            for e in range(3):
                total = None
                for b in range(3):
                    y = row + b - 2
                    if 0 <= y < 4:
                        at = b * 96 + e * 32
                        term = terms[at : at + 32, y * 128 : y * 128 + 128]
                        total = term if total is None else total + term
                sums.append(total)
            left = jnp.where(column >= 1, pltpu.roll(sums[0], 1, 1), 0.0)
            right = jnp.where(column <= 126, pltpu.roll(sums[2], 127, 1), 0.0)
            result = sums[1] + left + right
            keep_ref[z, row] = result[:16]
            send_ref[z, row] = result[16:]
        return 0

    lax.fori_loop(0, 8, plane, 0, unroll=UNROLL)


def fill_image(image, shifted_ref, z):
    for a in range(3):
        for b in range(3):
            at = (a * 3 + b) * 96
            image[at : at + 96] = shifted_ref[z + 2 - a, :, (2 - b) * 128 : (2 - b) * 128 + 512]


def backward_kernel(rank_ref, mine_ref, theirs_ref, filter_ref, grad_ref, shifted_ref, image):
    by_rim = select_rows(192, rim_first(rank_ref[0] & 1), 256)
    before = select_rows(128, lambda n: n - 1, 128)
    after = select_rows(128, lambda n: n + 1, 128)
    shifted_ref[0] = jnp.zeros((96, 768), BF16)
    shifted_ref[9] = jnp.zeros((96, 768), BF16)
    image[864:896] = jnp.zeros((32, 512), BF16)

    def arrange(z, _):
        rows = moved(by_rim, jnp.concatenate([mine_ref[z], theirs_ref[z]], axis=0))
        for e, cells in ((0, moved(rows, before)), (1, rows), (2, moved(rows, after))):
            for y in range(6):
                shifted_ref[z + 1, e * 32 : e * 32 + 32, y * 128 : y * 128 + 128] = cells[y * 32 : y * 32 + 32]
        return 0

    lax.fori_loop(0, 8, arrange, 0, unroll=UNROLL)
    back_y = select_rows(256, y_last, 256)

    def plane(z, _):
        fill_image(image, shifted_ref, z)
        grad = jnp.dot(filter_ref[...], image[...], preferred_element_type=F32).astype(BF16)
        for part in range(2):
            rows = jnp.concatenate(
                [grad[part * 64 : part * 64 + 64, y * 128 : y * 128 + 128] for y in range(4)], axis=0
            )
            grad_ref[z, part * 256 : part * 256 + 256] = moved(back_y, rows)
        return 0

    lax.fori_loop(0, 8, plane, 0, unroll=UNROLL)


def filter_grad_kernel(rank_ref, planes_ref, shifted_ref, slots_ref, image, total):
    image[864:896] = jnp.zeros((32, 512), BF16)
    total[...] = jnp.zeros((128, 896), F32)

    def plane(z, _):
        fill_image(image, shifted_ref, z)
        total[...] += lax.dot_general(
            planes_ref[z + 1], image[...], (((1,), (1,)), ((), ())), preferred_element_type=F32
        )
        return 0

    lax.fori_loop(0, 8, plane, 0, unroll=UNROLL)
    back_n = select_rows(256, n_last, 256)
    for h in range(2):
        for part in range(2):
            rows = [
                total[part * 64 : part * 64 + 64, j * 128 : j * 128 + 128].astype(BF16)
                if j < 7
                else jnp.zeros((64, 128), BF16)
                for j in range(4 * h, 4 * h + 4)
            ]
            rows = moved(back_n, jnp.concatenate(rows, axis=0))
            for i in range(2):
                place = slot(rank_ref[0], 2 * i + h)
                slots_ref[place, part * 128 : part * 128 + 128] = rows[i * 128 : i * 128 + 128]


def sum_kernel(keep_ref, other_ref, out_ref):
    back_rim = select_rows(128, rim_last, 96)
    for z in range(8):
        rows = (keep_ref[z] + other_ref[z]).astype(BF16).reshape(96, 128)
        out_ref[z] = moved(back_rim, rows)


def finish_kernel(parts_ref, out_ref, by_tap):
    column = lax.broadcasted_iota(jnp.int32, (8, 128), 1) // 32
    norm = 1.0 / math.sqrt(131072)
    for channel in range(4):
        for half in range(2):
            parts = [parts_ref[half * 4 + n, channel] for n in range(4)]
            for tap in range(4):
                rows = jnp.zeros((8, 128), F32)
                for n in range(4):
                    turned = parts[n] if n == tap else pltpu.roll(parts[n], (n - tap) % 4 * 32, 1)
                    rows = jnp.where(column == n, turned, rows)
                by_tap[channel * 2 + half, pl.ds(tap, 8, stride=4)] = rows * norm
            out_ref[channel, :, half * 128 : half * 128 + 128] = by_tap[channel * 2 + half, :27]


def windows(rows):
    lead = rows.shape[:-2]
    padded = jnp.pad(rows, [(0, 0)] * len(lead) + [(2, 2), (0, 0)]).reshape(lead + (33, 4, 128))
    return jnp.concatenate([padded[..., :32, :, :], padded[..., 1:, :, :]], axis=-2)


def overlapped(parts):
    lead = parts.shape[:-3]
    keep = [(0, 0)] * len(lead)
    first = jnp.pad(parts[..., 1:4, :], keep + [(0, 1), (1, 0), (0, 0)])
    second = jnp.pad(parts[..., 4:7, :], keep + [(1, 0), (0, 1), (0, 0)])
    return (first + second).reshape(lead + (132, 128))[..., 2:130, :]


def with_corners(rims, rows):
    return jnp.concatenate([rows[..., :1, :], rims[..., 1:7, :], rows[..., 1:, :]], axis=-2)


def corners(rims):
    return jnp.concatenate([rims[..., :1, :], rims[..., 7:, :]], axis=-2)


def whole(*shape):
    return pl.BlockSpec(shape, lambda n: (0,) * len(shape))


SCALAR = pl.BlockSpec(memory_space=pltpu.SMEM)


def call(kernel, name, ins, outs, scratch, flops):
    return pl.pallas_call(
        kernel,
        grid=(1,),
        in_specs=ins,
        out_shape=[jax.ShapeDtypeStruct(shape, dtype) for shape, dtype in outs],
        out_specs=[whole(*shape) for shape, _ in outs],
        scratch_shapes=[pltpu.VMEM(shape, dtype) for shape, dtype in scratch],
        compiler_params=PARAMS,
        cost_estimate=pl.CostEstimate(flops=flops, bytes_accessed=4 << 20, transcendentals=0),
        name=name,
    )


def swapped(array, axis, bit):
    count = lax.axis_size(axis)
    return lax.ppermute(array, axis, [(n, n ^ bit) for n in range(count)])


def local(quantized, scales, weights, cotangent):
    rank = lax.axis_index("filt").reshape(1).astype(jnp.int32)
    slab = lax.axis_index("space").reshape(1).astype(jnp.int32)

    dequant = (quantized.astype(F32) * scales[:, :, None, None]).astype(BF16)
    cells = dequant.reshape(2, 2, 32, 4, 128).transpose(2, 0, 1, 3, 4).reshape(64, 8, 128)
    rims = windows(cotangent.reshape(2, 2, 128, 128)).transpose(2, 0, 1, 3, 4).reshape(8, 4, 2, 2, 8, 128)
    own = lax.dynamic_slice_in_dim(weights, slab[0] * 32, 32, axis=2).reshape(4, 864)
    own = jnp.pad(own, ((0, 0), (0, 160))).reshape(2, 4, 2, 2, 128).transpose(1, 0, 2, 3, 4)
    own = jnp.broadcast_to(own[None], (8, 4, 2, 2, 2, 128))
    rims = with_corners(rims, own).reshape(64, 16, 128)
    got = lax.all_to_all(jnp.concatenate([cells, rims], axis=1), "filt", 0, 0, tiled=True)

    filters = corners(got[:, 8:24].reshape(64, 2, 8, 128)).reshape(1, 256, 128)
    for bit in (4, 2):
        filters = jnp.concatenate([filters, swapped(filters, "filt", bit)], axis=0)

    cells = jnp.broadcast_to(got[:, :8].reshape(1, 512, 128), (8, 512, 128))
    rims = got[:, 8:24].reshape(8, 128, 128)
    got = lax.all_to_all(jnp.concatenate([cells, rims], axis=1), "space", 0, 0, tiled=True)
    other_rims = swapped(got[:, 512:], "filt", 1)

    keep, send, planes, filters = call(
        forward_kernel,
        "forward",
        [SCALAR, whole(8, 512, 128), whole(4, 256, 128)],
        [((8, 6, 16, 128), F32), ((8, 6, 16, 128), F32), ((10, 128, 512), BF16), ((128, 896), BF16)],
        [],
        2 * 8 * 288 * 384 * 512,
    )(rank, got, filters)
    other = swapped(send, "filt", 1)
    grad, shifted = call(
        backward_kernel,
        "backward",
        [SCALAR, pl.BlockSpec((8, 128, 128), lambda n: (0, 4, 0)), whole(8, 128, 128), whole(128, 896)],
        [((8, 512, 128), BF16), ((10, 96, 768), BF16)],
        [((896, 512), BF16)],
        2 * 8 * 896 * 128 * 512,
    )(rank, got, other_rims, filters)

    out = pl.pallas_call(
        sum_kernel,
        out_shape=jax.ShapeDtypeStruct((8, 128, 128), BF16),
        compiler_params=PARAMS,
        name="sum",
    )(keep, other)
    both = jnp.concatenate([grad, out], axis=1)
    both, planes, shifted = lax.optimization_barrier((both, planes, shifted))

    (terms,) = call(
        filter_grad_kernel,
        "filter_grad",
        [SCALAR, whole(10, 128, 512), whole(10, 96, 768)],
        [((4, 256, 128), BF16)],
        [((896, 512), BF16), ((128, 896), F32)],
        2 * 8 * 896 * 128 * 512,
    )(rank, planes, shifted)

    got = lax.all_to_all(both, "space", 0, 0, tiled=True)

    terms = (terms[:2].astype(F32) + swapped(terms[2:], "filt", 2).astype(F32)).astype(BF16)
    terms = (terms[0].astype(F32) + swapped(terms[1], "filt", 4).astype(F32)).astype(BF16)

    grad = jnp.sum(got[:, :512].astype(F32), axis=0).astype(BF16).reshape(64, 8, 128)
    out = with_corners(got[:, 512:].reshape(64, 2, 8, 128), terms.reshape(64, 2, 2, 128)).reshape(64, 16, 128)
    got = lax.all_to_all(jnp.concatenate([grad, out], axis=1), "filt", 0, 0, tiled=True)

    got = got.reshape(32, 2, 24, 128)
    grad = got[:, :, :8].reshape(32, 2, 2, 4, 128).transpose(1, 2, 0, 3, 4).reshape(4, 1, 128, 128)
    rims = got[:, :, 8:24].reshape(32, 2, 2, 8, 128)
    terms = jnp.sum(corners(rims).reshape(8, 4, 2, 4, 128).astype(F32), axis=0)
    terms = terms.reshape(2, 2, 2, 4, 128).transpose(2, 0, 1, 3, 4).reshape(1, 4, 8, 128)
    terms = lax.all_to_all(jnp.broadcast_to(terms, (8, 4, 8, 128)), "space", 0, 0, tiled=True)
    filter_grad = pl.pallas_call(
        finish_kernel,
        out_shape=jax.ShapeDtypeStruct((4, 27, 256), F32),
        scratch_shapes=[pltpu.VMEM((8, 32, 128), F32)],
        compiler_params=PARAMS,
        name="finish",
    )(terms)

    out = overlapped(rims.transpose(1, 2, 0, 3, 4).astype(F32)).astype(BF16).reshape(4, 1, 128, 128)
    return (out, grad, filter_grad)


def solution(mesh):
    placed = (
        P("filt", "space", None, None),
        P("filt", "space"),
        P("filt", None, None),
        P("filt", "space", None, None),
    )
    return jax.shard_map(
        local,
        mesh=mesh,
        in_specs=placed,
        out_specs=(
            P("filt", "space", None, None),
            P("filt", "space", None, None),
            P("filt", None, None),
        ),
        check_vma=False,
    )
```

time: 184 us -> 168 us (0.913)
  blocking collectives: 94 us -> 83.1 us
  waiting for transfers between devices: 36 us -> 26.7 us
  starting transfers between devices: 23.7 us -> 29.5 us
  other arithmetic: 3.35 us -> 6.25 us
  Pallas kernels: 15.1 us -> 12.7 us
  local copies, waits for them, and re-layouts: 10.7 us -> 8.38 us
    all_to_all x1, waiting for transfers between devices: 16.7 us -> 3.41 us  [local(): lax.all_to_all(jnp.concatenate([cells, rims], axis=1), 'space', 0, 0, til...]
    all_to_all x2, blocking collectives: 94 us -> 83.1 us  [the longest x1 48.2 us: local(): lax.all_to_all(jnp.concatenate([cells, rims], axis=1), 'filt', 0, 0, tile...]
    ppermute x4 -> x6, starting transfers between devices: 10.4 us -> 16.9 us  [swapped(): return lax.ppermute(array, axis, [(n, n ^ bit) for n in range(count)])]
    pallas_call x2 -> x4, Pallas kernels: 14.9 us -> 12.5 us  [the longest x1 5.16 us: local(): call(backward_kernel, 'backward', [SCALAR, pl.BlockSpec((8, 128, 128), la...]
    all_to_all x2, waiting for transfers between devices: 3.66 us -> 5.89 us  [the longest x1 4.65 us: local(): lax.all_to_all(jnp.broadcast_to(terms, (8, 4, 8, 128)), 'space', 0, 0, ti...]
    concatenate x2 -> x7, other arithmetic: 0.13 us -> 2.09 us  [the longest x1 1.15 us: local(): both = jnp.concatenate([grad, out], axis=1)]
    ppermute x4 -> x6, waiting for transfers between devices: 15.7 us -> 17.4 us  [swapped(): return lax.ppermute(array, axis, [(n, n ^ bit) for n in range(count)])]
  transfers between devices with their start and end apart: 7 -> 9, of which waited for: 3 -> 8; matrix products, arithmetic and copies ran while one was open for 1% -> 1% of each run, Pallas kernels for 8% -> 5%
where the time goes in v2:
time: 168 us
  blocking collectives  83.1 us (49%)
  starting transfers between devices  29.5 us (18%)
  waiting for transfers between devices  26.7 us (16%)
  Pallas kernels  12.7 us (8%)
  local copies, waits for them, and re-layouts  8.38 us (5%)
  other arithmetic  6.25 us (4%)
    all_to_all x1, blocking collectives, local(): lax.all_to_all(jnp.concatenate([cells, rims], axis=1), 'filt', 0, 0, tile...  48.2 us
    all_to_all x1, blocking collectives, local(): lax.all_to_all(jnp.concatenate([grad, out], axis=1), 'filt', 0, 0, tiled=...  34.9 us
    ppermute x6, waiting for transfers between devices, swapped(): return lax.ppermute(array, axis, [(n, n ^ bit) for n in range(count)])  17.4 us
    ppermute x6, starting transfers between devices, swapped(): return lax.ppermute(array, axis, [(n, n ^ bit) for n in range(count)])  16.9 us
    pallas_call x1, Pallas kernels, local(): call(backward_kernel, 'backward', [SCALAR, pl.BlockSpec((8, 128, 128), la...  5.16 us
    all_to_all x1, waiting for transfers between devices, local(): lax.all_to_all(jnp.broadcast_to(terms, (8, 4, 8, 128)), 'space', 0, 0, ti...  4.65 us
    all_to_all x1, starting transfers between devices, local(): got = lax.all_to_all(both, 'space', 0, 0, tiled=True)  4.4 us
    all_to_all x1, starting transfers between devices, local(): lax.all_to_all(jnp.concatenate([cells, rims], axis=1), 'space', 0, 0, til...  4.22 us
  transfers between devices with their start and end apart: 9, of which 8 were waited for; matrix products, arithmetic and copies ran while one was open for 1% of the time, Pallas kernels for 5%

profile of v2, /device:TPU:1, one launch (start us, length us, event | category | flops | bytes accessed | tf_op | source)
XLA Modules:
  0.0 167.7 jit_solution(13328396468110639756)
XLA Ops:
  0.7 0.8 copy-done
  1.7 1.0 multiply_convert_fusion
  2.8 1.0 copy.55
  5.1 48.2 %all_to_all.25 = bf16[64,24,128]{2,1,0:T(8,128)(2,1)S(1)} all-to-all(bf16[64,24,128]{2,1,0:T(8,128)(2,1)S(1)} %pad_maximum_fusion.2), channel_id=1, replica_groups=mesh['space'=8,'filt'=64] {'filt'}, dimensions={0} | all-to-all | bytes 786432 | tf_op jit(solution)/shard_map/all_to_all | solution.py:268
  53.5 1.2 pad_maximum_fusion
  54.7 4.2 %all-to-all-start.1 = ((bf16[8,640,128]{2,1,0:T(8,128)(2,1)}), bf16[8,640,128]{2,1,0:T(8,128)(2,1)S(1)}, u32[]{:S(2)}, u32[]{:S(2)}) async-start(bf16[8,640,128]{2,1,0:T(8,128)(2,1)} %pad_maximum_fusion), calls=%async_computation.1 | async-start | bytes 2621440 | tf_op jit(solution)/shard_map/all_to_all | solution.py:276
  59.2 3.4 %collective-permute-start.1 = (bf16[1,256,128]{2,1,0:T(8,128)(2,1)S(1)}, bf16[1,256,128]{2,1,0:T(8,128)(2,1)S(1)}, u32[]{:S(2)}, u32[]{:S(2)}) collective-permute-start(bf16[1,256,128]{2,1,0:T(8,128)(2,1)S(1)} %bitcast.68), channel_id=1, source_target_pairs={{0,4},{1,5},{2,6},{3,7},{4,0},{5,1},{6,2},{7,3},{8,12},{9,13},{10,... | collective-permute-start | bytes 196616 | tf_op jit(solution)/shard_map/ppermute | solution.py:254
  62.6 4.5 %collective-permute-done.1 = bf16[1,256,128]{2,1,0:T(8,128)(2,1)S(1)} collective-permute-done((bf16[1,256,128]{2,1,0:T(8,128)(2,1)S(1)}, bf16[1,256,128]{2,1,0:T(8,128)(2,1)S(1)}, u32[]{:S(2)}, u32[]{:S(2)}) %collective-permute-start.1) | collective-permute-done | bytes 65568 | tf_op jit(solution)/shard_map/ppermute | solution.py:254
  67.1 1.9 %collective-permute-start.2 = (bf16[2,256,128]{2,1,0:T(8,128)(2,1)S(1)}, bf16[2,256,128]{2,1,0:T(8,128)(2,1)S(1)}, u32[]{:S(2)}, u32[]{:S(2)}) collective-permute-start(bf16[2,256,128]{2,1,0:T(8,128)(2,1)S(1)} %pad_maximum_fusion.7), channel_id=1, source_target_pairs={{0,2},{1,3},{2,0},{3,1},{4,6},{5,7},{6,4},{7,5},{8,10},{9,11},{10,... | collective-permute-start | bytes 393224 | tf_op jit(solution)/shard_map/ppermute | solution.py:254
  69.1 4.8 %collective-permute-done.2 = bf16[2,256,128]{2,1,0:T(8,128)(2,1)S(1)} collective-permute-done((bf16[2,256,128]{2,1,0:T(8,128)(2,1)S(1)}, bf16[2,256,128]{2,1,0:T(8,128)(2,1)S(1)}, u32[]{:S(2)}, u32[]{:S(2)}) %collective-permute-start.2) | collective-permute-done | bytes 131104 | tf_op jit(solution)/shard_map/ppermute | solution.py:254
  74.0 3.4 %all-to-all-done.1.cells_ref.mine_ref = bf16[8,640,128]{2,1,0:T(8,128)(2,1)S(1)} async-done(((bf16[8,640,128]{2,1,0:T(8,128)(2,1)}), bf16[8,640,128]{2,1,0:T(8,128)(2,1)S(1)}, u32[]{:S(2)}, u32[]{:S(2)}) %all-to-all-start.1) | async-done | bytes 1310752 | tf_op jit(solution)/shard_map/all_to_all | solution.py:276
  77.4 3.9 %forward.1 = (f32[8,6,16,128]{3,2,1,0:T(8,128)S(1)}, f32[8,6,16,128]{3,2,1,0:T(8,128)S(1)}, bf16[10,128,512]{2,1,0:T(8,128)(2,1)S(1)}, bf16[128,896]{1,0:T(8,128)(2,1)S(1)}) custom-call(s32[1]{0:T(128)} %bitcast.rank_ref, bf16[8,640,128]{2,1,0:T(8,128)(2,1)S(1)} %all-to-all-done.1.cells_ref.mine_ref, bf16[4,256,128]{2,1,0:T(8,128)(2,1)S(1)} %pad_maximum_fusion.6.slots_ref), custom_call_target="tpu_custom_call" | custom-call | flops 905969664 | bytes 4194304 | tf_op jit(solution)/shard_map/forward/pallas_call | solution.py:279
  81.3 1.1 copy-done.1
  82.4 2.3 %collective-permute-start.3 = (f32[8,6,16,128]{3,2,1,0:T(8,128)S(1)}, f32[8,6,16,128]{3,2,1,0:T(8,128)S(1)}, u32[]{:S(2)}, u32[]{:S(2)}) collective-permute-start(f32[8,6,16,128]{3,2,1,0:T(8,128)S(1)} %get-tuple-element.15), channel_id=1, source_target_pairs={{0,1},{1,0},{2,3},{3,2},{4,5},{5,4},{6,7},{7,6},{8,9},{9,8},{10,11... | collective-permute-start | bytes 1179656 | tf_op jit(solution)/shard_map/ppermute | solution.py:254
  84.7 2.0 %collective-permute-start = (bf16[8,128,128]{2,1,0:T(8,128)(2,1)S(1)}, bf16[8,128,128]{2,1,0:T(8,128)(2,1)S(1)}, u32[]{:S(2)}, u32[]{:S(2)}) collective-permute-start(bf16[8,128,128]{2,1,0:T(8,128)(2,1)S(1)} %slice.121), channel_id=1, source_target_pairs={{0,1},{1,0},{2,3},{3,2},{4,5},{5,4},{6,7},{7,6},{8,9},{9,8},{10,11... | collective-permute-start | bytes 786440 | tf_op jit(solution)/shard_map/ppermute | solution.py:254
  86.7 1.4 collective-permute-done.theirs_ref
  88.1 5.2 %backward.1 = (bf16[8,512,128]{2,1,0:T(8,128)(2,1)S(1)}, bf16[10,96,768]{2,1,0:T(8,128)(2,1)S(1)}) custom-call(s32[1]{0:T(128)} %bitcast.rank_ref, bf16[8,640,128]{2,1,0:T(8,128)(2,1)S(1)} %all-to-all-done.1.cells_ref.mine_ref, bf16[8,128,128]{2,1,0:T(8,128)(2,1)S(1)} %collective-permute-done.theirs_ref, bf16[128,896]{1,0:T(8,128)(2,1)S(1)} %get-tuple-element.12.filter_ref), custom_call_target="tpu_custom_call" | custom-call | flops 939524096 | bytes 4194304 | tf_op jit(solution)/shard_map/backward/pallas_call | solution.py:288
  93.5 1.1 pad_maximum_fusion.1
  94.7 4.4 %all-to-all-start.2 = ((bf16[8,640,128]{2,1,0:T(8,128)(2,1)}), bf16[8,640,128]{2,1,0:T(8,128)(2,1)}, u32[]{:S(2)}, u32[]{:S(2)}) async-start(bf16[8,640,128]{2,1,0:T(8,128)(2,1)} %pad_maximum_fusion.1), calls=%async_computation.2 | async-start | bytes 2621440 | tf_op jit(solution)/shard_map/all_to_all | solution.py:315
  99.1 3.2 %filter_grad.1 = bf16[4,256,128]{2,1,0:T(8,128)(2,1)S(1)} custom-call(s32[1]{0:T(128)} %bitcast.rank_ref, bf16[10,128,512]{2,1,0:T(8,128)(2,1)S(1)} %copy-done.2, bf16[10,96,768]{2,1,0:T(8,128)(2,1)S(1)} %get-tuple-element.20.shifted_ref), custom_call_target="tpu_custom_call" | custom-call | flops 939524096 | bytes 4194304 | tf_op jit(solution)/shard_map/filter_grad/pallas_call | solution.py:306
  102.3 3.8 %collective-permute-start.4 = (bf16[2,256,128]{2,1,0:T(8,128)(2,1)S(1)}, bf16[2,256,128]{2,1,0:T(8,128)(2,1)S(1)}, u32[]{:S(2)}, u32[]{:S(2)}) collective-permute-start(bf16[2,256,128]{2,1,0:T(8,128)(2,1)S(1)} %slice.126), channel_id=1, source_target_pairs={{0,2},{1,3},{2,0},{3,1},{4,6},{5,7},{6,4},{7,5},{8,10},{9,11},{10,... | collective-permute-start | bytes 393224 | tf_op jit(solution)/shard_map/ppermute | solution.py:254
  106.1 3.8 %collective-permute-done.4 = bf16[2,256,128]{2,1,0:T(8,128)(2,1)S(1)} collective-permute-done((bf16[2,256,128]{2,1,0:T(8,128)(2,1)S(1)}, bf16[2,256,128]{2,1,0:T(8,128)(2,1)S(1)}, u32[]{:S(2)}, u32[]{:S(2)}) %collective-permute-start.4) | collective-permute-done | bytes 131104 | tf_op jit(solution)/shard_map/ppermute | solution.py:254
  109.9 3.5 %collective-permute-start.5 = (bf16[256,128]{1,0:T(8,128)(2,1)S(1)}, bf16[256,128]{1,0:T(8,128)(2,1)S(1)}, u32[]{:S(2)}, u32[]{:S(2)}) collective-permute-start(bf16[256,128]{1,0:T(8,128)(2,1)S(1)} %slice_bitcast_fusion.2), channel_id=1, source_target_pairs={{0,4},{1,5},{2,6},{3,7},{4,0},{5,1},{6,2},{7,3},{8,12},{9,13},{10,... | collective-permute-start | bytes 196616 | tf_op jit(solution)/shard_map/ppermute | solution.py:254
  113.4 2.8 %collective-permute-done.5 = bf16[256,128]{1,0:T(8,128)(2,1)S(1)} collective-permute-done((bf16[256,128]{1,0:T(8,128)(2,1)S(1)}, bf16[256,128]{1,0:T(8,128)(2,1)S(1)}, u32[]{:S(2)}, u32[]{:S(2)}) %collective-permute-start.5) | collective-permute-done | bytes 65568 | tf_op jit(solution)/shard_map/ppermute | solution.py:254
  116.4 1.2 all-to-all-done.2
  117.6 1.0 slice.130
  118.9 1.4 slice_reduce_fusion
  120.3 34.9 %all_to_all.26 = bf16[64,24,128]{2,1,0:T(8,128)(2,1)S(1)} all-to-all(bf16[64,24,128]{2,1,0:T(8,128)(2,1)S(1)} %pad_maximum_fusion.3), channel_id=1, replica_groups=mesh['space'=8,'filt'=64] {'filt'}, dimensions={0} | all-to-all | bytes 786432 | tf_op jit(solution)/shard_map/all_to_all | solution.py:322
  155.4 0.7 copy.62
  157.0 4.0 %all-to-all-start.4 = ((f32[8,4,8,128]{3,2,1,0:T(8,128)}), f32[8,4,8,128]{3,2,1,0:T(8,128)S(1)}, u32[]{:S(2)}, u32[]{:S(2)}) async-start(f32[8,4,8,128]{3,2,1,0:T(8,128)} %broadcast_in_dim.28), calls=%async_computation.4 | async-start | bytes 262144 | tf_op jit(solution)/shard_map/all_to_all | solution.py:329
  162.1 4.7 %all-to-all-done.4.parts_ref = f32[8,4,8,128]{3,2,1,0:T(8,128)S(1)} async-done(((f32[8,4,8,128]{3,2,1,0:T(8,128)}), f32[8,4,8,128]{3,2,1,0:T(8,128)S(1)}, u32[]{:S(2)}, u32[]{:S(2)}) %all-to-all-start.4) | async-done | bytes 131104 | tf_op jit(solution)/shard_map/all_to_all | solution.py:329
  167.0 0.7 copy.68
  (55 shorter events, 5.0 us)
Async XLA Ops:
  0.6 0.8 copy-start
  54.7 22.6 %all-to-all-start.1 = ((bf16[8,640,128]{2,1,0:T(8,128)(2,1)}), bf16[8,640,128]{2,1,0:T(8,128)(2,1)S(1)}, u32[]{:S(2)}, u32[]{:S(2)}) async-start(bf16[8,640,128]{2,1,0:T(8,128)(2,1)} %pad_maximum_fusion), calls=%async_computation.1 | async-start | bytes 2621440 | tf_op jit(solution)/shard_map/all_to_all | solution.py:276
  59.2 7.9 %collective-permute-start.1 = (bf16[1,256,128]{2,1,0:T(8,128)(2,1)S(1)}, bf16[1,256,128]{2,1,0:T(8,128)(2,1)S(1)}, u32[]{:S(2)}, u32[]{:S(2)}) collective-permute-start(bf16[1,256,128]{2,1,0:T(8,128)(2,1)S(1)} %bitcast.68), channel_id=1, source_target_pairs={{0,4},{1,5},{2,6},{3,7},{4,0},{5,1},{6,2},{7,3},{8,12},{9,13},{10,... | collective-permute-start | bytes 196616 | tf_op jit(solution)/shard_map/ppermute | solution.py:254
  67.1 6.8 %collective-permute-start.2 = (bf16[2,256,128]{2,1,0:T(8,128)(2,1)S(1)}, bf16[2,256,128]{2,1,0:T(8,128)(2,1)S(1)}, u32[]{:S(2)}, u32[]{:S(2)}) collective-permute-start(bf16[2,256,128]{2,1,0:T(8,128)(2,1)S(1)} %pad_maximum_fusion.7), channel_id=1, source_target_pairs={{0,2},{1,3},{2,0},{3,1},{4,6},{5,7},{6,4},{7,5},{8,10},{9,11},{10,... | collective-permute-start | bytes 393224 | tf_op jit(solution)/shard_map/ppermute | solution.py:254
  81.3 1.1 copy-start.1
  82.4 10.9 %collective-permute-start.3 = (f32[8,6,16,128]{3,2,1,0:T(8,128)S(1)}, f32[8,6,16,128]{3,2,1,0:T(8,128)S(1)}, u32[]{:S(2)}, u32[]{:S(2)}) collective-permute-start(f32[8,6,16,128]{3,2,1,0:T(8,128)S(1)} %get-tuple-element.15), channel_id=1, source_target_pairs={{0,1},{1,0},{2,3},{3,2},{4,5},{5,4},{6,7},{7,6},{8,9},{9,8},{10,11... | collective-permute-start | bytes 1179656 | tf_op jit(solution)/shard_map/ppermute | solution.py:254
  84.7 3.4 %collective-permute-start = (bf16[8,128,128]{2,1,0:T(8,128)(2,1)S(1)}, bf16[8,128,128]{2,1,0:T(8,128)(2,1)S(1)}, u32[]{:S(2)}, u32[]{:S(2)}) collective-permute-start(bf16[8,128,128]{2,1,0:T(8,128)(2,1)S(1)} %slice.121), channel_id=1, source_target_pairs={{0,1},{1,0},{2,3},{3,2},{4,5},{5,4},{6,7},{7,6},{8,9},{9,8},{10,11... | collective-permute-start | bytes 786440 | tf_op jit(solution)/shard_map/ppermute | solution.py:254
  94.7 4.4 %copy-start.2 = (bf16[10,128,512]{2,1,0:T(8,128)(2,1)S(1)}, bf16[10,128,512]{2,1,0:T(8,128)(2,1)}, u32[]{:S(2)}) copy-start(bf16[10,128,512]{2,1,0:T(8,128)(2,1)} %copy-done.1) | copy-start | bytes 3932164
  94.7 23.0 %all-to-all-start.2 = ((bf16[8,640,128]{2,1,0:T(8,128)(2,1)}), bf16[8,640,128]{2,1,0:T(8,128)(2,1)}, u32[]{:S(2)}, u32[]{:S(2)}) async-start(bf16[8,640,128]{2,1,0:T(8,128)(2,1)} %pad_maximum_fusion.1), calls=%async_computation.2 | async-start | bytes 2621440 | tf_op jit(solution)/shard_map/all_to_all | solution.py:315
  102.3 7.6 %collective-permute-start.4 = (bf16[2,256,128]{2,1,0:T(8,128)(2,1)S(1)}, bf16[2,256,128]{2,1,0:T(8,128)(2,1)S(1)}, u32[]{:S(2)}, u32[]{:S(2)}) collective-permute-start(bf16[2,256,128]{2,1,0:T(8,128)(2,1)S(1)} %slice.126), channel_id=1, source_target_pairs={{0,2},{1,3},{2,0},{3,1},{4,6},{5,7},{6,4},{7,5},{8,10},{9,11},{10,... | collective-permute-start | bytes 393224 | tf_op jit(solution)/shard_map/ppermute | solution.py:254
  109.9 6.3 %collective-permute-start.5 = (bf16[256,128]{1,0:T(8,128)(2,1)S(1)}, bf16[256,128]{1,0:T(8,128)(2,1)S(1)}, u32[]{:S(2)}, u32[]{:S(2)}) collective-permute-start(bf16[256,128]{1,0:T(8,128)(2,1)S(1)} %slice_bitcast_fusion.2), channel_id=1, source_target_pairs={{0,4},{1,5},{2,6},{3,7},{4,0},{5,1},{6,2},{7,3},{8,12},{9,13},{10,... | collective-permute-start | bytes 196616 | tf_op jit(solution)/shard_map/ppermute | solution.py:254
  157.0 9.8 %all-to-all-start.4 = ((f32[8,4,8,128]{3,2,1,0:T(8,128)}), f32[8,4,8,128]{3,2,1,0:T(8,128)S(1)}, u32[]{:S(2)}, u32[]{:S(2)}) async-start(f32[8,4,8,128]{3,2,1,0:T(8,128)} %broadcast_in_dim.28), calls=%async_computation.4 | async-start | bytes 262144 | tf_op jit(solution)/shard_map/all_to_all | solution.py:329

commit v3 on v2

v3 whole, which is shorter than its diff:
```python
import math

import jax
import jax.numpy as jnp
from jax import lax
from jax.experimental import pallas as pl
from jax.experimental.pallas import tpu as pltpu
from jax.sharding import PartitionSpec as P


F32 = jnp.float32
BF16 = jnp.bfloat16
PARAMS = pltpu.CompilerParams(vmem_limit_bytes=16 * 1024 * 1024)
UNROLL = 4


def select_rows(rows, source, columns):
    row = lax.broadcasted_iota(jnp.int32, (rows, 128), 0)[:, :1]
    col = lax.broadcasted_iota(jnp.int32, (rows, columns), 1)
    return jnp.where(source(row) == col, 1.0, 0.0).astype(BF16)


def moved(matrix, cells):
    return jnp.dot(matrix, cells, preferred_element_type=F32).astype(BF16)


def by_24(n):
    part = (n * 2731) >> 16
    return part, n - part * 24


def by_32(n):
    return n >> 5, (n >> 1) & 15, n & 1


def pack_first(n):
    part, m = by_24(n)
    r, core = part >> 1, part & 1
    i, w = (m - 8) >> 3, m & 7
    rim = 64 + i * 64 + r * 4 + w + 14
    corner = 192 + (r & 3) * 4 + i * 2 + (w >> 2)
    inner = (w >= 1) & (w <= 6)
    return core * 208 + jnp.where(m < 8, (m >> 2) * 32 + r * 4 + (m & 3), jnp.where(inner, rim, corner))


def message_row(n):
    cell = (n & 15) * 24 + (n >> 6) * 4 + ((n >> 4) & 3)
    w, g, i = by_32(n - 128)
    rim = g * 24 + i * 8 + w + 9
    g, corner = (n - 320) >> 2, (n - 320) & 3
    return jnp.where(n < 128, cell, jnp.where(n < 320, rim, g * 24 + 8 + (corner >> 1) * 8 + (corner & 1) * 7))


def matrix_row(n):
    g, m = by_24(n)
    i, w = (m - 8) >> 3, m & 7
    cell = (m >> 2) * 64 + (m & 3) * 16 + g
    rim = 128 + (w - 1) * 32 + g * 2 + i
    inner = (w >= 1) & (w <= 6)
    return jnp.where(m < 8, cell, jnp.where(inner, rim, 320 + g * 4 + i * 2 + (w >> 2)))


def slot(rank, quarter):
    x = ((rank >> 1) & 3) ^ quarter
    return ((x & 1) << 1) | (x >> 1)


def first_kernel(scales_ref, cells_ref, rims_ref, own_ref, out_ref, raw, cells, rims, sems):
    copies = [
        pltpu.make_async_copy(cells_ref, raw, sems.at[0]),
        pltpu.make_async_copy(rims_ref, rims.at[:, 16:144], sems.at[1]),
    ]
    for copy in copies:
        copy.start()
    order = select_rows(384, pack_first, 416)
    for n in range(4):
        rims[n, :16] = jnp.zeros((16, 128), BF16)
        rims[n, 144:] = jnp.zeros((16, 128), BF16)
    for copy in copies:
        copy.wait()
    for n in range(4):
        cells[n] = (raw[n].astype(F32) * scales_ref[0, n]).astype(BF16)
    for block in range(4):
        at = block * 32
        parts = []
        for core in range(2):
            parts += [cells[2 * core + i, at : at + 32] for i in range(2)]
            parts += [rims[2 * core + i, at : at + 64] for i in range(2)]
            parts.append(own_ref[core])
        out_ref[block * 384 : block * 384 + 384] = moved(order, jnp.concatenate(parts, axis=0))


def middle_kernel(got_ref, out_ref, corners_ref):
    order = select_rows(384, message_row, 384)
    for block in range(4):
        rows = moved(order, got_ref[block * 384 : block * 384 + 384])
        for i in range(2):
            for y in range(4):
                piece = rows[i * 64 + y * 16 : i * 64 + y * 16 + 16]
                for place in range(4):
                    out_ref[2 * place + i, y * 64 + block * 16 : y * 64 + block * 16 + 16] = piece
            out_ref[2 * block + i, 256:448] = rows[128:320]
        corners_ref[block * 64 : block * 64 + 64] = rows[320:384]


def filter_kernel(rank_ref, slots_ref, filter_ref, stacked_ref):
    rank = rank_ref[0]
    by_n = select_rows(256, lambda n: (n & 63) * 4 + (n >> 6), 256)
    for h in range(2):
        for part in range(2):
            lanes = moved(by_n, slots_ref[slot(rank, 2 * ((rank & 1) ^ part) + h)])
            for n in range(4 - h):
                at = (4 * h + n) * 128
                filter_ref[part * 64 : part * 64 + 64, at : at + 128] = lanes[n * 64 : n * 64 + 64]
    same = select_rows(128, lambda n: n, 128)
    turned = [
        lax.dot_general(
            same,
            filter_ref[:, j * 128 : j * 128 + 128],
            (((1,), (1,)), ((), ())),
            preferred_element_type=F32,
        ).astype(BF16)
        for j in range(7)
    ]
    turned = jnp.concatenate(turned, axis=0)
    for a in range(3):
        stacked_ref[:, a * 128 : a * 128 + 128] = turned[a * 288 : a * 288 + 288]


def plane_of(mine_ref, theirs_ref, z):
    halves = [
        jnp.concatenate([ref[z, y * 64 : y * 64 + 64] for y in range(4)], axis=1) for ref in (mine_ref, theirs_ref)
    ]
    return jnp.concatenate(halves, axis=0)


def forward_kernel(mine_ref, theirs_ref, stacked_ref, out_ref, planes):
    planes[0] = jnp.zeros((128, 512), BF16)
    planes[9] = jnp.zeros((128, 512), BF16)
    for z in range(8):
        planes[z + 1] = plane_of(mine_ref, theirs_ref, z)
    column = lax.broadcasted_iota(jnp.int32, (32, 128), 1)

    def plane(z, _):
        near = jnp.concatenate([planes[z], planes[z + 1], planes[z + 2]], axis=0)
        terms = jnp.dot(stacked_ref[...], near, preferred_element_type=F32)
        for row in range(6):
            sums = []
            for e in range(3):
                total = None
                for b in range(3):
                    y = row + b - 2
                    if 0 <= y < 4:
                        at = b * 96 + e * 32
                        term = terms[at : at + 32, y * 128 : y * 128 + 128]
                        total = term if total is None else total + term
                sums.append(total)
            left = jnp.where(column >= 1, pltpu.roll(sums[0], 1, 1), 0.0)
            right = jnp.where(column <= 126, pltpu.roll(sums[2], 127, 1), 0.0)
            out_ref[z, 256 + row * 32 : 256 + row * 32 + 32] = (sums[1] + left + right).astype(BF16)
        return 0

    lax.fori_loop(0, 8, plane, 0, unroll=UNROLL)


def fill_image(image, shifted, z):
    for a in range(3):
        for b in range(3):
            at = (a * 3 + b) * 96
            image[at : at + 96] = shifted[z + 2 - a, :, (2 - b) * 128 : (2 - b) * 128 + 512]


def shift(got_ref, shifted):
    before = select_rows(128, lambda n: n - 1, 128)
    after = select_rows(128, lambda n: n + 1, 128)
    shifted[0] = jnp.zeros((96, 768), BF16)
    shifted[9] = jnp.zeros((96, 768), BF16)

    def plane(z, _):
        rows = got_ref[z, 256:448]
        for e, cells in ((0, moved(rows, before)), (1, rows), (2, moved(rows, after))):
            for y in range(6):
                shifted[z + 1, e * 32 : e * 32 + 32, y * 128 : y * 128 + 128] = cells[y * 32 : y * 32 + 32]
        return 0

    lax.fori_loop(0, 8, plane, 0, unroll=UNROLL)


def backward_kernel(got_ref, filter_ref, keep_ref, send_ref, shifted, image):
    shift(got_ref, shifted)
    image[864:896] = jnp.zeros((32, 512), BF16)

    def plane(z, _):
        fill_image(image, shifted, z)
        grad = jnp.dot(filter_ref[...], image[...], preferred_element_type=F32)
        for y in range(4):
            keep_ref[z, y * 64 : y * 64 + 64] = grad[:64, y * 128 : y * 128 + 128]
            send_ref[z, y * 64 : y * 64 + 64] = grad[64:, y * 128 : y * 128 + 128].astype(BF16)
        return 0

    lax.fori_loop(0, 8, plane, 0, unroll=UNROLL)


def sum_kernel(keep_ref, other_ref, out_ref, result_ref, rows_ref, sem):
    rows_ref[...] = (keep_ref[...] + other_ref[...].astype(F32)).astype(BF16)
    copy = pltpu.make_async_copy(rows_ref, result_ref.at[:, 0:256], sem)
    copy.start()
    copy.wait()


def filter_grad_kernel(rank_ref, got_ref, theirs_ref, slots_ref, shifted, image, total):
    shift(got_ref, shifted)
    image[864:896] = jnp.zeros((32, 512), BF16)
    total[...] = jnp.zeros((128, 896), F32)

    def plane(z, _):
        fill_image(image, shifted, z)
        total[...] += lax.dot_general(
            plane_of(got_ref, theirs_ref, z), image[...], (((1,), (1,)), ((), ())), preferred_element_type=F32
        )
        return 0

    lax.fori_loop(0, 8, plane, 0, unroll=UNROLL)
    back_n = select_rows(256, lambda n: (n & 3) * 64 + (n >> 2), 256)
    rank = rank_ref[0]
    for h in range(2):
        for part in range(2):
            rows = [
                total[part * 64 : part * 64 + 64, j * 128 : j * 128 + 128].astype(BF16)
                if j < 7
                else jnp.zeros((64, 128), BF16)
                for j in range(4 * h, 4 * h + 4)
            ]
            place = slot(rank, 2 * ((rank & 1) ^ part) + h)
            slots_ref[place] = moved(back_n, jnp.concatenate(rows, axis=0))


def last_kernel(got_ref, mine_ref, theirs_ref, out_ref, grads):
    order = select_rows(384, matrix_row, 384)
    for i in range(2):
        grad = got_ref[i, :256].astype(F32)
        for n in range(1, 4):
            grad = grad + got_ref[2 * n + i, :256].astype(F32)
        grads[i] = grad.astype(BF16)
    for block in range(4):
        parts = []
        for i in range(2):
            parts += [grads[i, y * 64 + block * 16 : y * 64 + block * 16 + 16] for y in range(4)]
        rims = [got_ref[2 * block + i, 256:448].astype(F32) for i in range(2)]
        parts.append((rims[0] + rims[1]).astype(BF16))
        part = slice(block * 64, block * 64 + 64)
        parts.append((mine_ref[part].astype(F32) + theirs_ref[part].astype(F32)).astype(BF16))
        out_ref[block * 384 : block * 384 + 384] = moved(order, jnp.concatenate(parts, axis=0))


def finish_kernel(parts_ref, out_ref, by_tap):
    row = lax.broadcasted_iota(jnp.int32, (256, 128), 0)
    lane = lax.broadcasted_iota(jnp.int32, (256, 128), 1)
    low = lax.broadcasted_iota(jnp.int32, (8, 128), 1) < 64
    norm = 1.0 / math.sqrt(131072)
    rows = []
    for c in range(2):
        for x in range(2):
            for y in range(4):
                rows.append(jnp.concatenate([parts_ref[2 * y + x, 2 * c + k] for k in range(2)], axis=1))
    rows = jnp.concatenate(rows, axis=0) * norm
    for pair in range(2):
        source = ((lane >> 1) & 1) * 128 + (2 * pair + (lane >> 6)) * 32 + ((lane >> 2) & 15) * 2 + (lane & 1)
        spread = jnp.where(source == row, 1.0, 0.0).astype(F32)
        wide = jnp.dot(rows, spread, preferred_element_type=F32, precision=lax.Precision.HIGHEST)
        for channel in range(4):
            for half in range(2):
                at = (channel * 4 + half * 2) * 8
                even, odd = wide[at : at + 8], wide[at + 8 : at + 16]
                by_tap[channel * 2 + half, pl.ds(2 * pair, 8, stride=4)] = jnp.where(low, even, pltpu.roll(odd, 64, 1))
                by_tap[channel * 2 + half, pl.ds(2 * pair + 1, 8, stride=4)] = jnp.where(
                    low, pltpu.roll(even, 64, 1), odd
                )
    for channel in range(4):
        for half in range(2):
            out_ref[:, channel, half * 128 : half * 128 + 128] = by_tap[channel * 2 + half, :27]


def overlapped(parts):
    lead = parts.shape[:-3]
    keep = [(0, 0)] * len(lead)
    first = jnp.pad(parts[..., 1:4, :], keep + [(0, 1), (1, 0), (0, 0)])
    second = jnp.pad(parts[..., 4:7, :], keep + [(1, 0), (0, 1), (0, 0)])
    return (first + second).reshape(lead + (132, 128))[..., 2:130, :]


def corners(rims):
    return jnp.concatenate([rims[..., :1, :], rims[..., 7:, :]], axis=-2)


def whole(*shape):
    return pl.BlockSpec(shape, lambda n: (0,) * len(shape))


SCALAR = pl.BlockSpec(memory_space=pltpu.SMEM)
ANY = pl.BlockSpec(memory_space=pl.ANY)
HBM = pl.BlockSpec(memory_space=pltpu.HBM)
DMA = pltpu.SemaphoreType.DMA


def call(kernel, name, ins, outs, scratch, flops, out_specs=None, aliases={}):
    return pl.pallas_call(
        kernel,
        grid=(1,),
        in_specs=ins,
        out_shape=[jax.ShapeDtypeStruct(shape, dtype) for shape, dtype in outs],
        out_specs=out_specs or [whole(*shape) for shape, _ in outs],
        scratch_shapes=[pltpu.VMEM(*s) if isinstance(s, tuple) else s for s in scratch],
        input_output_aliases=aliases,
        compiler_params=PARAMS,
        cost_estimate=pl.CostEstimate(flops=flops, bytes_accessed=4 << 20, transcendentals=0),
        name=name,
    )


def swapped(array, axis, bit):
    count = lax.axis_size(axis)
    return lax.ppermute(array, axis, [(n, n ^ bit) for n in range(count)])


def local(quantized, scales, weights, cotangent):
    rank = lax.axis_index("filt").reshape(1).astype(jnp.int32)
    slab = lax.axis_index("space")

    own = lax.dynamic_slice_in_dim(weights, slab // 2 * 64, 64, axis=2).reshape(2, 2, 27, 16, 2, 2)
    own = lax.dynamic_index_in_dim(own, slab % 2, axis=1, keepdims=False).transpose(3, 0, 1, 2, 4).reshape(2, 2, 864)
    own = jnp.pad(own, ((0, 0), (0, 0), (0, 160))).reshape(2, 16, 128)
    (both,) = call(
        first_kernel,
        "first",
        [SCALAR, HBM, HBM, whole(2, 16, 128)],
        [((1536, 128), BF16)],
        [((4, 128, 128), BF16), ((4, 128, 128), BF16), ((4, 160, 128), BF16), DMA((2,))],
        2 * 4 * 384 * 416 * 128,
    )(scales.reshape(1, 4), quantized.reshape(4, 128, 128), cotangent.reshape(4, 128, 128), own)
    got = lax.all_to_all(both.reshape(64, 24, 128), "filt", 0, 0, tiled=True)

    both, filters = call(
        middle_kernel,
        "middle",
        [whole(1536, 128)],
        [((8, 448, 128), BF16), ((256, 128), BF16)],
        [],
        2 * 4 * 384 * 384 * 128,
    )(got.reshape(1536, 128))
    got = lax.all_to_all(both, "space", 0, 0, tiled=True)
    filters = filters[None]
    for bit in (4, 2):
        filters = jnp.concatenate([filters, swapped(filters, "filt", bit)], axis=0)
    filters, got = lax.optimization_barrier((filters, got))
    filters, stacked = call(
        filter_kernel,
        "filters",
        [SCALAR, whole(4, 256, 128)],
        [((128, 896), BF16), ((288, 384), BF16)],
        [],
        2 * 4 * 256 * 256 * 128,
    )(rank, filters)

    theirs = swapped(got[:, :256], "filt", 1)
    keep, send = call(
        backward_kernel,
        "backward",
        [whole(8, 448, 128), whole(128, 896)],
        [((8, 256, 128), F32), ((8, 256, 128), BF16)],
        [((10, 96, 768), BF16), ((896, 512), BF16)],
        2 * 8 * 896 * 128 * 512,
    )(got, filters)
    send, theirs = lax.optimization_barrier((send, theirs))
    other = swapped(send, "filt", 1)
    cells = pl.BlockSpec((8, 256, 128), lambda n: (0, 0, 0))
    (out,) = call(
        forward_kernel,
        "forward",
        [cells, whole(8, 256, 128), whole(288, 384)],
        [((8, 448, 128), BF16)],
        [((10, 128, 512), BF16)],
        2 * 8 * 288 * 384 * 512,
    )(got, theirs, stacked)
    (both,) = call(
        sum_kernel,
        "sum",
        [whole(8, 256, 128), whole(8, 256, 128), ANY],
        [((8, 448, 128), BF16)],
        [((8, 256, 128), BF16), DMA],
        8 * 256 * 128,
        [ANY],
        {2: 0},
    )(keep, other, out)
    both, cells, theirs = lax.optimization_barrier((both, got, theirs))

    (terms,) = call(
        filter_grad_kernel,
        "filter_grad",
        [SCALAR, whole(8, 448, 128), whole(8, 256, 128)],
        [((4, 256, 128), BF16)],
        [((10, 96, 768), BF16), ((896, 512), BF16), ((128, 896), F32)],
        2 * 8 * 896 * 128 * 512,
    )(rank, cells, theirs)

    got = lax.all_to_all(both, "space", 0, 0, tiled=True)
    terms = (terms[:2].astype(F32) + swapped(terms[2:], "filt", 2).astype(F32)).astype(BF16)
    (both,) = call(
        last_kernel,
        "last",
        [whole(8, 448, 128), whole(256, 128), whole(256, 128)],
        [((1536, 128), BF16)],
        [((2, 256, 128), BF16)],
        2 * 4 * 384 * 384 * 128,
    )(got, terms[0], swapped(terms[1], "filt", 4))
    got = lax.all_to_all(both.reshape(64, 24, 128), "filt", 0, 0, tiled=True)

    got = got.reshape(32, 2, 24, 128)
    rims = got[:, :, 8:24].reshape(32, 2, 2, 8, 128)
    terms = jnp.sum(corners(rims).reshape(8, 2, 2, 2, 4, 128).astype(F32), axis=0)
    terms = terms.transpose(0, 2, 1, 3, 4).reshape(1, 4, 8, 128)
    terms, got = lax.optimization_barrier((jnp.broadcast_to(terms, (8, 4, 8, 128)), got))
    terms = lax.all_to_all(terms, "space", 0, 0, tiled=True)
    filter_grad = pl.pallas_call(
        finish_kernel,
        out_shape=jax.ShapeDtypeStruct((27, 4, 256), F32),
        scratch_shapes=[pltpu.VMEM((8, 32, 128), F32)],
        compiler_params=PARAMS,
        name="finish",
    )(terms).transpose(1, 0, 2)

    grad = got[:, :, :8].reshape(32, 2, 2, 4, 128).transpose(1, 2, 0, 3, 4).reshape(4, 1, 128, 128)
    rims = got[:, :, 8:24].reshape(32, 2, 2, 8, 128)
    out = overlapped(rims.transpose(1, 2, 0, 3, 4).astype(F32)).astype(BF16).reshape(4, 1, 128, 128)
    return (out, grad, filter_grad)


def solution(mesh):
    placed = (
        P("filt", "space", None, None),
        P("filt", "space"),
        P("filt", None, None),
        P("filt", "space", None, None),
    )
    return jax.shard_map(
        local,
        mesh=mesh,
        in_specs=placed,
        out_specs=(
            P("filt", "space", None, None),
            P("filt", "space", None, None),
            P("filt", None, None),
        ),
        check_vma=False,
    )
```

time: 168 us -> 157 us (0.935)
  waiting for transfers between devices: 26.7 us -> 20.8 us
  other arithmetic: 6.25 us -> 0.44 us
  local copies, waits for them, and re-layouts: 8.38 us -> 5.53 us
  Pallas kernels: 12.7 us -> 15 us
    all_to_all x1 -> x2, starting transfers between devices: 4.4 us -> 10.3 us  [local(): got = lax.all_to_all(both, 'space', 0, 0, tiled=True)]
    all_to_all x2 -> x1, waiting for transfers between devices: 8.06 us -> 3.73 us  [local(): terms = lax.all_to_all(terms, 'space', 0, 0, tiled=True)]
    all_to_all x2 -> x1, starting transfers between devices: 8.23 us -> 4.67 us  [local(): terms = lax.all_to_all(terms, 'space', 0, 0, tiled=True)]
    concatenate x6 -> x0, other arithmetic: 3.15 us -> none  [the longest x2 1.22 us: local(): jnp.concatenate([cells, rims], axis=1)]
    ppermute x6, starting transfers between devices: 16.9 us -> 14.1 us  [swapped(): return lax.ppermute(array, axis, [(n, n ^ bit) for n in range(count)])]
    pallas_call x5 -> x9, Pallas kernels: 12.7 us -> 15 us  [the longest x1 3.5 us: local(): call(filter_grad_kernel, 'filter_grad', [SCALAR, whole(8, 448, 128), whol...]
  transfers between devices with their start and end apart: 9 -> 9, of which waited for: 8 -> 5; matrix products, arithmetic and copies ran while one was open for 1% -> 1% of each run, Pallas kernels for 5% -> 6%
where the time goes in v3:
time: 157 us; the launch traced here: 156 us
  blocking collectives  84.4 us (54%)
  starting transfers between devices  29.1 us (19%)
  waiting for transfers between devices  20.8 us (13%)
  Pallas kernels  15 us (10%)
  local copies, waits for them, and re-layouts  5.53 us (4%)
    all_to_all x2, blocking collectives, local(): got = lax.all_to_all(both.reshape(64, 24, 128), 'filt', 0, 0, tiled=True)  84.4 us
    ppermute x6, waiting for transfers between devices, swapped(): return lax.ppermute(array, axis, [(n, n ^ bit) for n in range(count)])  17.1 us
    ppermute x6, starting transfers between devices, swapped(): return lax.ppermute(array, axis, [(n, n ^ bit) for n in range(count)])  14.1 us
    all_to_all x2, starting transfers between devices, local(): got = lax.all_to_all(both, 'space', 0, 0, tiled=True)  10.3 us
    all_to_all x1, starting transfers between devices, local(): terms = lax.all_to_all(terms, 'space', 0, 0, tiled=True)  4.67 us
    all_to_all x1, waiting for transfers between devices, local(): terms = lax.all_to_all(terms, 'space', 0, 0, tiled=True)  3.73 us
    pallas_call x1, Pallas kernels, local(): call(filter_grad_kernel, 'filter_grad', [SCALAR, whole(8, 448, 128), whol...  3.5 us
  transfers between devices with their start and end apart: 9, of which 5 were waited for; matrix products, arithmetic and copies ran while one was open for 1% of the time, Pallas kernels for 6%

profile of v3, /device:TPU:1, one launch (start us, length us, event | category | flops | bytes accessed | tf_op | source)
XLA Modules:
  0.0 156.2 jit_solution(15707927745096162554)
XLA Ops:
  0.7 0.8 copy-done
  1.7 0.6 copy.40
  2.3 0.5 reshape.67
  2.8 0.4 copy-done.1
  3.5 1.7 %first.1 = bf16[1536,128]{1,0:T(8,128)(2,1)S(1)} custom-call(f32[1,4]{1,0:T(1,128)S(1)} %bitcast.50, bf16[4,128,128]{2,1,0:T(8,128)(2,1)S(1)} %bitcast.48, bf16[4,128,128]{2,1,0:T(8,128)(2,1)S(1)} %bitcast.49, bf16[2,16,128]{2,1,0:T(8,128)(2,1)S(1)} %reshape.68.own_ref), custom_call_target="tpu_custom_call" | custom-call | flops 163577856 | bytes 4194304 | tf_op jit(solution)/shard_map/first/pallas_call | solution.py:333
  5.3 48.2 %all_to_all.25 = bf16[64,24,128]{2,1,0:T(8,128)(2,1)S(1)} all-to-all(bf16[64,24,128]{2,1,0:T(8,128)(2,1)S(1)} %bitcast.42), channel_id=1, replica_groups=mesh['space'=8,'filt'=64] {'filt'}, dimensions={0} | all-to-all | bytes 786432 | tf_op jit(solution)/shard_map/all_to_all | solution.py:341
  53.4 1.4 middle.1
  54.8 4.2 %all-to-all-start.1 = ((bf16[8,448,128]{2,1,0:T(8,128)(2,1)}), bf16[8,448,128]{2,1,0:T(8,128)(2,1)S(1)}, u32[]{:S(2)}, u32[]{:S(2)}) async-start(bf16[8,448,128]{2,1,0:T(8,128)(2,1)} %get-tuple-element.19), calls=%async_computation.1 | async-start | bytes 1835008 | tf_op jit(solution)/shard_map/all_to_all | solution.py:351
  59.1 3.4 %collective-permute-start = (bf16[1,256,128]{2,1,0:T(8,128)(2,1)S(1)}, bf16[1,256,128]{2,1,0:T(8,128)(2,1)S(1)}, u32[]{:S(2)}, u32[]{:S(2)}) collective-permute-start(bf16[1,256,128]{2,1,0:T(8,128)(2,1)S(1)} %bitcast.45), channel_id=1, source_target_pairs={{0,4},{1,5},{2,6},{3,7},{4,0},{5,1},{6,2},{7,3},{8,12},{9,13},{10,... | collective-permute-start | bytes 196616 | tf_op jit(solution)/shard_map/ppermute | solution.py:323
  62.4 4.5 %collective-permute-done = bf16[1,256,128]{2,1,0:T(8,128)(2,1)S(1)} collective-permute-done((bf16[1,256,128]{2,1,0:T(8,128)(2,1)S(1)}, bf16[1,256,128]{2,1,0:T(8,128)(2,1)S(1)}, u32[]{:S(2)}, u32[]{:S(2)}) %collective-permute-start) | collective-permute-done | bytes 65568 | tf_op jit(solution)/shard_map/ppermute | solution.py:323
  67.0 1.9 %collective-permute-start.1 = (bf16[2,256,128]{2,1,0:T(8,128)(2,1)S(1)}, bf16[2,256,128]{2,1,0:T(8,128)(2,1)S(1)}, u32[]{:S(2)}, u32[]{:S(2)}) collective-permute-start(bf16[2,256,128]{2,1,0:T(8,128)(2,1)S(1)} %pad_maximum_fusion.1), channel_id=1, source_target_pairs={{0,2},{1,3},{2,0},{3,1},{4,6},{5,7},{6,4},{7,5},{8,10},{9,11},{10,... | collective-permute-start | bytes 393224 | tf_op jit(solution)/shard_map/ppermute | solution.py:323
  68.9 4.6 %collective-permute-done.1 = bf16[2,256,128]{2,1,0:T(8,128)(2,1)S(1)} collective-permute-done((bf16[2,256,128]{2,1,0:T(8,128)(2,1)S(1)}, bf16[2,256,128]{2,1,0:T(8,128)(2,1)S(1)}, u32[]{:S(2)}, u32[]{:S(2)}) %collective-permute-start.1) | collective-permute-done | bytes 131104 | tf_op jit(solution)/shard_map/ppermute | solution.py:323
  73.6 2.0 %collective-permute-start.2 = (bf16[8,256,128]{2,1,0:T(8,128)(2,1)S(1)}, bf16[8,256,128]{2,1,0:T(8,128)(2,1)S(1)}, u32[]{:S(2)}, u32[]{:S(2)}) collective-permute-start(bf16[8,256,128]{2,1,0:T(8,128)(2,1)S(1)} %slice.40), channel_id=1, source_target_pairs={{0,1},{1,0},{2,3},{3,2},{4,5},{5,4},{6,7},{7,6},{8,9},{9,8},{10,11... | collective-permute-start | bytes 1572872 | tf_op jit(solution)/shard_map/ppermute | solution.py:323
  75.6 0.5 filters.1
  76.1 2.3 %backward.1 = (f32[8,256,128]{2,1,0:T(8,128)S(1)}, bf16[8,256,128]{2,1,0:T(8,128)(2,1)S(1)}) custom-call(bf16[8,448,128]{2,1,0:T(8,128)(2,1)S(1)} %all-to-all-done.1.got_ref.mine_ref, bf16[128,896]{1,0:T(8,128)(2,1)S(1)} %get-tuple-element.22.filter_ref), custom_call_target="tpu_custom_call" | custom-call | flops 939524096 | bytes 4194304 | tf_op jit(solution)/shard_map/backward/pallas_call | solution.py:366
  78.4 2.3 %collective-permute-start.3 = (bf16[8,256,128]{2,1,0:T(8,128)(2,1)S(1)}, bf16[8,256,128]{2,1,0:T(8,128)(2,1)S(1)}, u32[]{:S(2)}, u32[]{:S(2)}) collective-permute-start(bf16[8,256,128]{2,1,0:T(8,128)(2,1)S(1)} %get-tuple-element.25), channel_id=1, source_target_pairs={{0,1},{1,0},{2,3},{3,2},{4,5},{5,4},{6,7},{7,6},{8,9},{9,8},{10,11... | collective-permute-start | bytes 1572872 | tf_op jit(solution)/shard_map/ppermute | solution.py:323
  80.7 2.8 %forward.1.out_ref = bf16[8,448,128]{2,1,0:T(8,128)(2,1)} custom-call(bf16[8,448,128]{2,1,0:T(8,128)(2,1)S(1)} %all-to-all-done.1.got_ref.mine_ref, bf16[8,256,128]{2,1,0:T(8,128)(2,1)S(1)} %collective-permute-done.2.theirs_ref, bf16[288,384]{1,0:T(8,128)(2,1)S(1)} %get-tuple-element.27.stacked_ref), custom_call_target="tpu_custom_call" | custom-call | flops 905969664 | bytes 4194304 | tf_op jit(solution)/shard_map/forward/pallas_call | solution.py:377
  83.5 0.9 sum.1
  84.4 6.1 %all-to-all-start.2 = ((bf16[8,448,128]{2,1,0:T(8,128)(2,1)}), bf16[8,448,128]{2,1,0:T(8,128)(2,1)S(1)}, u32[]{:S(2)}, u32[]{:S(2)}) async-start(bf16[8,448,128]{2,1,0:T(8,128)(2,1)} %sum.1), calls=%async_computation.2 | async-start | bytes 1835008 | tf_op jit(solution)/shard_map/all_to_all | solution.py:406
  90.5 3.5 %filter_grad.1 = bf16[4,256,128]{2,1,0:T(8,128)(2,1)S(1)} custom-call(s32[1]{0:T(128)} %bitcast.10.rank_ref, bf16[8,448,128]{2,1,0:T(8,128)(2,1)S(1)} %all-to-all-done.1.got_ref.mine_ref, bf16[8,256,128]{2,1,0:T(8,128)(2,1)S(1)} %collective-permute-done.2.theirs_ref), custom_call_target="tpu_custom_call" | custom-call | flops 939524096 | bytes 4194304 | tf_op jit(solution)/shard_map/filter_grad/pallas_call | solution.py:397
  94.1 1.9 %collective-permute-start.4 = (bf16[2,256,128]{2,1,0:T(8,128)(2,1)S(1)}, bf16[2,256,128]{2,1,0:T(8,128)(2,1)S(1)}, u32[]{:S(2)}, u32[]{:S(2)}) collective-permute-start(bf16[2,256,128]{2,1,0:T(8,128)(2,1)S(1)} %slice.54), channel_id=1, source_target_pairs={{0,2},{1,3},{2,0},{3,1},{4,6},{5,7},{6,4},{7,5},{8,10},{9,11},{10,... | collective-permute-start | bytes 393224 | tf_op jit(solution)/shard_map/ppermute | solution.py:323
  96.0 4.2 %collective-permute-done.4 = bf16[2,256,128]{2,1,0:T(8,128)(2,1)S(1)} collective-permute-done((bf16[2,256,128]{2,1,0:T(8,128)(2,1)S(1)}, bf16[2,256,128]{2,1,0:T(8,128)(2,1)S(1)}, u32[]{:S(2)}, u32[]{:S(2)}) %collective-permute-start.4) | collective-permute-done | bytes 131104 | tf_op jit(solution)/shard_map/ppermute | solution.py:323
  100.3 2.6 %collective-permute-start.5 = (bf16[256,128]{1,0:T(8,128)(2,1)S(1)}, bf16[256,128]{1,0:T(8,128)(2,1)S(1)}, u32[]{:S(2)}, u32[]{:S(2)}) collective-permute-start(bf16[256,128]{1,0:T(8,128)(2,1)S(1)} %get-tuple-element.46), channel_id=1, source_target_pairs={{0,4},{1,5},{2,6},{3,7},{4,0},{5,1},{6,2},{7,3},{8,12},{9,13},{10,... | collective-permute-start | bytes 196616 | tf_op jit(solution)/shard_map/ppermute | solution.py:323
  102.8 3.8 %collective-permute-done.5.theirs_ref = bf16[256,128]{1,0:T(8,128)(2,1)S(1)} collective-permute-done((bf16[256,128]{1,0:T(8,128)(2,1)S(1)}, bf16[256,128]{1,0:T(8,128)(2,1)S(1)}, u32[]{:S(2)}, u32[]{:S(2)}) %collective-permute-start.5) | collective-permute-done | bytes 65568 | tf_op jit(solution)/shard_map/ppermute | solution.py:323
  106.6 0.7 last.1
  107.3 36.2 %all_to_all.26 = bf16[64,24,128]{2,1,0:T(8,128)(2,1)S(1)} all-to-all(bf16[64,24,128]{2,1,0:T(8,128)(2,1)S(1)} %bitcast.43), channel_id=1, replica_groups=mesh['space'=8,'filt'=64] {'filt'}, dimensions={0} | all-to-all | bytes 786432 | tf_op jit(solution)/shard_map/all_to_all | solution.py:416
  143.9 0.7 broadcast_in_dim.12
  144.6 4.7 %all-to-all-start.4 = ((f32[8,4,8,128]{3,2,1,0:T(8,128)}), f32[8,4,8,128]{3,2,1,0:T(8,128)S(1)}, u32[]{:S(2)}, u32[]{:S(2)}) async-start(f32[8,4,8,128]{3,2,1,0:T(8,128)} %broadcast_in_dim.12), calls=%async_computation.4 | async-start | bytes 262144 | tf_op jit(solution)/shard_map/all_to_all | solution.py:423
  149.3 0.7 copy.37
  150.6 0.7 copy.35
  151.3 3.7 %all-to-all-done.4.parts_ref = f32[8,4,8,128]{3,2,1,0:T(8,128)S(1)} async-done(((f32[8,4,8,128]{3,2,1,0:T(8,128)}), f32[8,4,8,128]{3,2,1,0:T(8,128)S(1)}, u32[]{:S(2)}, u32[]{:S(2)}) %all-to-all-start.4) | async-done | bytes 131104 | tf_op jit(solution)/shard_map/all_to_all | solution.py:423
  155.0 1.1 finish.1
  (33 shorter events, 1.7 us)
Async XLA Ops:
  0.6 0.8 copy-start
  2.3 0.9 copy-start.1
  2.3 1.0 copy-start.2
  2.8 0.7 copy-start.3
  54.8 18.7 %all-to-all-start.1 = ((bf16[8,448,128]{2,1,0:T(8,128)(2,1)}), bf16[8,448,128]{2,1,0:T(8,128)(2,1)S(1)}, u32[]{:S(2)}, u32[]{:S(2)}) async-start(bf16[8,448,128]{2,1,0:T(8,128)(2,1)} %get-tuple-element.19), calls=%async_computation.1 | async-start | bytes 1835008 | tf_op jit(solution)/shard_map/all_to_all | solution.py:351
  59.1 7.9 %collective-permute-start = (bf16[1,256,128]{2,1,0:T(8,128)(2,1)S(1)}, bf16[1,256,128]{2,1,0:T(8,128)(2,1)S(1)}, u32[]{:S(2)}, u32[]{:S(2)}) collective-permute-start(bf16[1,256,128]{2,1,0:T(8,128)(2,1)S(1)} %bitcast.45), channel_id=1, source_target_pairs={{0,4},{1,5},{2,6},{3,7},{4,0},{5,1},{6,2},{7,3},{8,12},{9,13},{10,... | collective-permute-start | bytes 196616 | tf_op jit(solution)/shard_map/ppermute | solution.py:323
  67.0 6.5 %collective-permute-start.1 = (bf16[2,256,128]{2,1,0:T(8,128)(2,1)S(1)}, bf16[2,256,128]{2,1,0:T(8,128)(2,1)S(1)}, u32[]{:S(2)}, u32[]{:S(2)}) collective-permute-start(bf16[2,256,128]{2,1,0:T(8,128)(2,1)S(1)} %pad_maximum_fusion.1), channel_id=1, source_target_pairs={{0,2},{1,3},{2,0},{3,1},{4,6},{5,7},{6,4},{7,5},{8,10},{9,11},{10,... | collective-permute-start | bytes 393224 | tf_op jit(solution)/shard_map/ppermute | solution.py:323
  73.6 4.8 %collective-permute-start.2 = (bf16[8,256,128]{2,1,0:T(8,128)(2,1)S(1)}, bf16[8,256,128]{2,1,0:T(8,128)(2,1)S(1)}, u32[]{:S(2)}, u32[]{:S(2)}) collective-permute-start(bf16[8,256,128]{2,1,0:T(8,128)(2,1)S(1)} %slice.40), channel_id=1, source_target_pairs={{0,1},{1,0},{2,3},{3,2},{4,5},{5,4},{6,7},{7,6},{8,9},{9,8},{10,11... | collective-permute-start | bytes 1572872 | tf_op jit(solution)/shard_map/ppermute | solution.py:323
  78.4 5.1 %collective-permute-start.3 = (bf16[8,256,128]{2,1,0:T(8,128)(2,1)S(1)}, bf16[8,256,128]{2,1,0:T(8,128)(2,1)S(1)}, u32[]{:S(2)}, u32[]{:S(2)}) collective-permute-start(bf16[8,256,128]{2,1,0:T(8,128)(2,1)S(1)} %get-tuple-element.25), channel_id=1, source_target_pairs={{0,1},{1,0},{2,3},{3,2},{4,5},{5,4},{6,7},{7,6},{8,9},{9,8},{10,11... | collective-permute-start | bytes 1572872 | tf_op jit(solution)/shard_map/ppermute | solution.py:323
  84.4 22.2 %all-to-all-start.2 = ((bf16[8,448,128]{2,1,0:T(8,128)(2,1)}), bf16[8,448,128]{2,1,0:T(8,128)(2,1)S(1)}, u32[]{:S(2)}, u32[]{:S(2)}) async-start(bf16[8,448,128]{2,1,0:T(8,128)(2,1)} %sum.1), calls=%async_computation.2 | async-start | bytes 1835008 | tf_op jit(solution)/shard_map/all_to_all | solution.py:406
  94.1 6.1 %collective-permute-start.4 = (bf16[2,256,128]{2,1,0:T(8,128)(2,1)S(1)}, bf16[2,256,128]{2,1,0:T(8,128)(2,1)S(1)}, u32[]{:S(2)}, u32[]{:S(2)}) collective-permute-start(bf16[2,256,128]{2,1,0:T(8,128)(2,1)S(1)} %slice.54), channel_id=1, source_target_pairs={{0,2},{1,3},{2,0},{3,1},{4,6},{5,7},{6,4},{7,5},{8,10},{9,11},{10,... | collective-permute-start | bytes 393224 | tf_op jit(solution)/shard_map/ppermute | solution.py:323
  100.3 6.3 %collective-permute-start.5 = (bf16[256,128]{1,0:T(8,128)(2,1)S(1)}, bf16[256,128]{1,0:T(8,128)(2,1)S(1)}, u32[]{:S(2)}, u32[]{:S(2)}) collective-permute-start(bf16[256,128]{1,0:T(8,128)(2,1)S(1)} %get-tuple-element.46), channel_id=1, source_target_pairs={{0,4},{1,5},{2,6},{3,7},{4,0},{5,1},{6,2},{7,3},{8,12},{9,13},{10,... | collective-permute-start | bytes 196616 | tf_op jit(solution)/shard_map/ppermute | solution.py:323
  144.6 10.4 %all-to-all-start.4 = ((f32[8,4,8,128]{3,2,1,0:T(8,128)}), f32[8,4,8,128]{3,2,1,0:T(8,128)S(1)}, u32[]{:S(2)}, u32[]{:S(2)}) async-start(f32[8,4,8,128]{3,2,1,0:T(8,128)} %broadcast_in_dim.12), calls=%async_computation.4 | async-start | bytes 262144 | tf_op jit(solution)/shard_map/all_to_all | solution.py:423

commit v4 on v3

--- a/solution.py
+++ b/solution.py
@@ -60,12 +60,29 @@
     return jnp.where(m < 8, cell, jnp.where(inner, rim, 320 + g * 4 + i * 2 + (w >> 2)))
 
 
-def slot(rank, quarter):
-    x = ((rank >> 1) & 3) ^ quarter
-    return ((x & 1) << 1) | (x >> 1)
-
-
-def first_kernel(scales_ref, cells_ref, rims_ref, own_ref, out_ref, raw, cells, rims, sems):
+def quarter_of(rank):
+    return (rank >> 1) & 3
+
+
+def own_rows(slab, weights_ref):
+    lane = lax.broadcasted_iota(jnp.int32, (16, 128), 1) >> 5
+    weights = jnp.concatenate([weights_ref[tap] for tap in range(27)], axis=0)
+    result = []
+    for core in range(2):
+        source = lambda n: (slab >> 1) * 64 + ((n >> 1) & 15) * 4 + core * 2 + (n & 1)
+        row = lax.broadcasted_iota(jnp.int32, (256, 128), 0)
+        col = lax.broadcasted_iota(jnp.int32, (256, 128), 1)
+        pick = jnp.where(source(col) == row, 1.0, 0.0).astype(BF16)
+        picked = moved(weights, pick)
+        rows = jnp.zeros((16, 128), F32)
+        for tap in range(4):
+            order = select_rows(16, lambda n: (4 * (n & 7) + tap) * 4 + (n >> 3) * 2 + (slab & 1), 108)
+            rows = jnp.where(lane == tap, jnp.dot(order, picked, preferred_element_type=F32), rows)
+        result.append(rows.astype(BF16))
+    return result
+
+
+def first_kernel(slab_ref, scales_ref, cells_ref, rims_ref, weights_ref, out_ref, raw, cells, rims, sems):
     copies = [
         pltpu.make_async_copy(cells_ref, raw, sems.at[0]),
         pltpu.make_async_copy(rims_ref, rims.at[:, 16:144], sems.at[1]),
@@ -73,6 +90,7 @@
     for copy in copies:
         copy.start()
     order = select_rows(384, pack_first, 416)
+    own = own_rows(slab_ref[0], weights_ref)
     for n in range(4):
         rims[n, :16] = jnp.zeros((16, 128), BF16)
         rims[n, 144:] = jnp.zeros((16, 128), BF16)
@@ -86,7 +104,7 @@
         for core in range(2):
             parts += [cells[2 * core + i, at : at + 32] for i in range(2)]
             parts += [rims[2 * core + i, at : at + 64] for i in range(2)]
-            parts.append(own_ref[core])
+            parts.append(own[core])
         out_ref[block * 384 : block * 384 + 384] = moved(order, jnp.concatenate(parts, axis=0))
 
 
@@ -103,12 +121,14 @@
         corners_ref[block * 64 : block * 64 + 64] = rows[320:384]
 
 
-def filter_kernel(rank_ref, slots_ref, filter_ref, stacked_ref):
+def filter_kernel(rank_ref, own_ref, first_ref, second_ref, third_ref, filter_ref, stacked_ref, quarters):
     rank = rank_ref[0]
+    for n, ref in enumerate((own_ref, first_ref, second_ref, third_ref)):
+        quarters[quarter_of(rank) ^ n] = ref[...]
     by_n = select_rows(256, lambda n: (n & 63) * 4 + (n >> 6), 256)
     for h in range(2):
         for part in range(2):
-            lanes = moved(by_n, slots_ref[slot(rank, 2 * ((rank & 1) ^ part) + h)])
+            lanes = moved(by_n, quarters[2 * ((rank & 1) ^ part) + h])
             for n in range(4 - h):
                 at = (4 * h + n) * 128
                 filter_ref[part * 64 : part * 64 + 64, at : at + 128] = lanes[n * 64 : n * 64 + 64]
@@ -134,7 +154,7 @@
     return jnp.concatenate(halves, axis=0)
 
 
-def forward_kernel(mine_ref, theirs_ref, stacked_ref, out_ref, planes):
+def forward_kernel(mine_ref, theirs_ref, stacked_ref, out_ref, planes, rows, sems):
     planes[0] = jnp.zeros((128, 512), BF16)
     planes[9] = jnp.zeros((128, 512), BF16)
     for z in range(8):
@@ -157,10 +177,17 @@
                 sums.append(total)
             left = jnp.where(column >= 1, pltpu.roll(sums[0], 1, 1), 0.0)
             right = jnp.where(column <= 126, pltpu.roll(sums[2], 127, 1), 0.0)
-            out_ref[z, 256 + row * 32 : 256 + row * 32 + 32] = (sums[1] + left + right).astype(BF16)
+            rows[z, row * 32 : row * 32 + 32] = (sums[1] + left + right).astype(BF16)
         return 0
 
-    lax.fori_loop(0, 8, plane, 0, unroll=UNROLL)
+    copies = []
+    for half in range(2):
+        lax.fori_loop(half * 4, half * 4 + 4, plane, 0, unroll=UNROLL)
+        part = slice(half * 4, half * 4 + 4)
+        copies.append(pltpu.make_async_copy(rows.at[part], out_ref.at[part, 256:448], sems.at[half]))
+        copies[-1].start()
+    for copy in copies:
+        copy.wait()
 
 
 def fill_image(image, shifted, z):
@@ -201,41 +228,42 @@
     lax.fori_loop(0, 8, plane, 0, unroll=UNROLL)
 
 
-def sum_kernel(keep_ref, other_ref, out_ref, result_ref, rows_ref, sem):
-    rows_ref[...] = (keep_ref[...] + other_ref[...].astype(F32)).astype(BF16)
-    copy = pltpu.make_async_copy(rows_ref, result_ref.at[:, 0:256], sem)
-    copy.start()
-    copy.wait()
-
-
-def filter_grad_kernel(rank_ref, got_ref, theirs_ref, slots_ref, shifted, image, total):
+def sum_kernel(keep_ref, other_ref, out_ref, result_ref, rows_ref, sems):
+    copies = []
+    for half in range(2):
+        part = slice(half * 4, half * 4 + 4)
+        rows_ref[part] = (keep_ref[part] + other_ref[part].astype(F32)).astype(BF16)
+        copies.append(pltpu.make_async_copy(rows_ref.at[part], result_ref.at[part, 0:256], sems.at[half]))
+        copies[-1].start()
+    for copy in copies:
+        copy.wait()
+
+
+def filter_grad_kernel(
+    rank_ref, got_ref, theirs_ref, own_ref, first_ref, second_ref, third_ref, shifted, image, total
+):
     shift(got_ref, shifted)
-    image[864:896] = jnp.zeros((32, 512), BF16)
-    total[...] = jnp.zeros((128, 896), F32)
-
-    def plane(z, _):
-        fill_image(image, shifted, z)
-        total[...] += lax.dot_general(
-            plane_of(got_ref, theirs_ref, z), image[...], (((1,), (1,)), ((), ())), preferred_element_type=F32
-        )
-        return 0
-
-    lax.fori_loop(0, 8, plane, 0, unroll=UNROLL)
-    back_n = select_rows(256, lambda n: (n & 3) * 64 + (n >> 2), 256)
+    image[864:896] = jnp.zeros((32, 2048), BF16)
+    total[...] = jnp.zeros((1024, 128), F32)
+    for half in range(2):
+        for z in range(4):
+            fill_image(image.at[:, z * 512 : z * 512 + 512], shifted, half * 4 + z)
+        cells = jnp.concatenate([plane_of(got_ref, theirs_ref, half * 4 + z) for z in range(4)], axis=1)
+        total[:896] += lax.dot_general(image[...], cells, (((1,), (1,)), ((), ())), preferred_element_type=F32)
     rank = rank_ref[0]
-    for h in range(2):
-        for part in range(2):
-            rows = [
-                total[part * 64 : part * 64 + 64, j * 128 : j * 128 + 128].astype(BF16)
-                if j < 7
-                else jnp.zeros((64, 128), BF16)
-                for j in range(4 * h, 4 * h + 4)
-            ]
-            place = slot(rank, 2 * ((rank & 1) ^ part) + h)
-            slots_ref[place] = moved(back_n, jnp.concatenate(rows, axis=0))
-
-
-def last_kernel(got_ref, mine_ref, theirs_ref, out_ref, grads):
+    for n, ref in enumerate((own_ref, first_ref, second_ref, third_ref)):
+        quarter = quarter_of(rank) ^ n
+        part = ((quarter >> 1) ^ (rank & 1)) * 64
+        order = select_rows(256, lambda n: (n & 3) * 128 + part + (n >> 2), 512)
+        lanes = [
+            total[pl.ds(pl.multiple_of((4 * (quarter & 1) + m) * 128, 128), 128)].astype(BF16) for m in range(4)
+        ]
+        ref[...] = lax.dot_general(
+            order, jnp.concatenate(lanes, axis=1), (((1,), (1,)), ((), ())), preferred_element_type=F32
+        ).astype(BF16)
+
+
+def last_kernel(got_ref, own_ref, first_ref, second_ref, third_ref, out_ref, grads):
     order = select_rows(384, matrix_row, 384)
     for i in range(2):
         grad = got_ref[i, :256].astype(F32)
@@ -249,8 +277,23 @@
         rims = [got_ref[2 * block + i, 256:448].astype(F32) for i in range(2)]
         parts.append((rims[0] + rims[1]).astype(BF16))
         part = slice(block * 64, block * 64 + 64)
-        parts.append((mine_ref[part].astype(F32) + theirs_ref[part].astype(F32)).astype(BF16))
+        terms = [ref[part].astype(F32) for ref in (own_ref, first_ref, second_ref, third_ref)]
+        parts.append(sum(terms[1:], terms[0]).astype(BF16))
         out_ref[block * 384 : block * 384 + 384] = moved(order, jnp.concatenate(parts, axis=0))
+
+
+def tail_kernel(got_ref, out_ref):
+    row = lax.broadcasted_iota(jnp.int32, (32, 1536), 0)
+    col = lax.broadcasted_iota(jnp.int32, (32, 1536), 1)
+    sender, m = by_24(col)
+    corner = (m >= 8) & (((m & 7) == 0) | ((m & 7) == 7))
+    n = ((m - 8) >> 3) * 2 + ((m & 7) >> 2)
+    quarter = quarter_of(sender)
+    target = (quarter >> 1) * 16 + (sender & 1) * 8 + (quarter & 1) * 4 + n
+    order = jnp.where(corner & (target == row), 1.0, 0.0).astype(BF16)
+    rows = jnp.dot(order, got_ref[...], preferred_element_type=F32)
+    for n in range(8):
+        out_ref[n] = rows
 
 
 def finish_kernel(parts_ref, out_ref, by_tap):
@@ -289,10 +332,6 @@
     return (first + second).reshape(lead + (132, 128))[..., 2:130, :]
 
 
-def corners(rims):
-    return jnp.concatenate([rims[..., :1, :], rims[..., 7:, :]], axis=-2)
-
-
 def whole(*shape):
     return pl.BlockSpec(shape, lambda n: (0,) * len(shape))
 
@@ -303,7 +342,7 @@
 DMA = pltpu.SemaphoreType.DMA
 
 
-def call(kernel, name, ins, outs, scratch, flops, out_specs=None, aliases={}):
+def call(kernel, name, ins, outs, scratch, flops, out_specs=None, aliases={}, mib=16):
     return pl.pallas_call(
         kernel,
         grid=(1,),
@@ -312,7 +351,7 @@
         out_specs=out_specs or [whole(*shape) for shape, _ in outs],
         scratch_shapes=[pltpu.VMEM(*s) if isinstance(s, tuple) else s for s in scratch],
         input_output_aliases=aliases,
-        compiler_params=PARAMS,
+        compiler_params=pltpu.CompilerParams(vmem_limit_bytes=mib * 1024 * 1024),
         cost_estimate=pl.CostEstimate(flops=flops, bytes_accessed=4 << 20, transcendentals=0),
         name=name,
     )
@@ -325,19 +364,23 @@
 
 def local(quantized, scales, weights, cotangent):
     rank = lax.axis_index("filt").reshape(1).astype(jnp.int32)
-    slab = lax.axis_index("space")
-
-    own = lax.dynamic_slice_in_dim(weights, slab // 2 * 64, 64, axis=2).reshape(2, 2, 27, 16, 2, 2)
-    own = lax.dynamic_index_in_dim(own, slab % 2, axis=1, keepdims=False).transpose(3, 0, 1, 2, 4).reshape(2, 2, 864)
-    own = jnp.pad(own, ((0, 0), (0, 0), (0, 160))).reshape(2, 16, 128)
+    slab = lax.axis_index("space").reshape(1).astype(jnp.int32)
+
     (both,) = call(
         first_kernel,
         "first",
-        [SCALAR, HBM, HBM, whole(2, 16, 128)],
+        [SCALAR, SCALAR, HBM, HBM, whole(27, 4, 256)],
         [((1536, 128), BF16)],
         [((4, 128, 128), BF16), ((4, 128, 128), BF16), ((4, 160, 128), BF16), DMA((2,))],
         2 * 4 * 384 * 416 * 128,
-    )(scales.reshape(1, 4), quantized.reshape(4, 128, 128), cotangent.reshape(4, 128, 128), own)
+        mib=56,
+    )(
+        slab,
+        scales.reshape(1, 4),
+        quantized.reshape(4, 128, 128),
+        cotangent.reshape(4, 128, 128),
+        weights.transpose(1, 0, 2),
+    )
     got = lax.all_to_all(both.reshape(64, 24, 128), "filt", 0, 0, tiled=True)
 
     both, filters = call(
@@ -349,19 +392,17 @@
         2 * 4 * 384 * 384 * 128,
     )(got.reshape(1536, 128))
     got = lax.all_to_all(both, "space", 0, 0, tiled=True)
-    filters = filters[None]
-    for bit in (4, 2):
-        filters = jnp.concatenate([filters, swapped(filters, "filt", bit)], axis=0)
-    filters, got = lax.optimization_barrier((filters, got))
+    filters = [filters] + [swapped(filters, "filt", 2 * n) for n in range(1, 4)]
     filters, stacked = call(
         filter_kernel,
         "filters",
-        [SCALAR, whole(4, 256, 128)],
+        [SCALAR] + [whole(256, 128)] * 4,
         [((128, 896), BF16), ((288, 384), BF16)],
-        [],
+        [((4, 256, 128), BF16)],
         2 * 4 * 256 * 256 * 128,
-    )(rank, filters)
-
+    )(rank, *filters)
+
+    filters, stacked, got = lax.optimization_barrier((filters, stacked, got))
     theirs = swapped(got[:, :256], "filt", 1)
     keep, send = call(
         backward_kernel,
@@ -379,48 +420,48 @@
         "forward",
         [cells, whole(8, 256, 128), whole(288, 384)],
         [((8, 448, 128), BF16)],
-        [((10, 128, 512), BF16)],
+        [((10, 128, 512), BF16), ((8, 192, 128), BF16), DMA((2,))],
         2 * 8 * 288 * 384 * 512,
+        [ANY],
     )(got, theirs, stacked)
     (both,) = call(
         sum_kernel,
         "sum",
         [whole(8, 256, 128), whole(8, 256, 128), ANY],
         [((8, 448, 128), BF16)],
-        [((8, 256, 128), BF16), DMA],
+        [((8, 256, 128), BF16), DMA((2,))],
         8 * 256 * 128,
         [ANY],
         {2: 0},
     )(keep, other, out)
     both, cells, theirs = lax.optimization_barrier((both, got, theirs))
 
-    (terms,) = call(
+    terms = call(
         filter_grad_kernel,
         "filter_grad",
         [SCALAR, whole(8, 448, 128), whole(8, 256, 128)],
-        [((4, 256, 128), BF16)],
-        [((10, 96, 768), BF16), ((896, 512), BF16), ((128, 896), F32)],
+        [((256, 128), BF16)] * 4,
+        [((10, 96, 768), BF16), ((896, 2048), BF16), ((1024, 128), F32)],
         2 * 8 * 896 * 128 * 512,
     )(rank, cells, theirs)
 
     got = lax.all_to_all(both, "space", 0, 0, tiled=True)
-    terms = (terms[:2].astype(F32) + swapped(terms[2:], "filt", 2).astype(F32)).astype(BF16)
+    terms = [terms[0]] + [swapped(terms[n], "filt", 2 * n) for n in range(1, 4)]
     (both,) = call(
         last_kernel,
         "last",
-        [whole(8, 448, 128), whole(256, 128), whole(256, 128)],
+        [whole(8, 448, 128)] + [whole(256, 128)] * 4,
         [((1536, 128), BF16)],
         [((2, 256, 128), BF16)],
         2 * 4 * 384 * 384 * 128,
-    )(got, terms[0], swapped(terms[1], "filt", 4))
+    )(got, *terms)
     got = lax.all_to_all(both.reshape(64, 24, 128), "filt", 0, 0, tiled=True)
 
-    got = got.reshape(32, 2, 24, 128)
-    rims = got[:, :, 8:24].reshape(32, 2, 2, 8, 128)
-    terms = jnp.sum(corners(rims).reshape(8, 2, 2, 2, 4, 128).astype(F32), axis=0)
-    terms = terms.transpose(0, 2, 1, 3, 4).reshape(1, 4, 8, 128)
-    terms, got = lax.optimization_barrier((jnp.broadcast_to(terms, (8, 4, 8, 128)), got))
-    terms = lax.all_to_all(terms, "space", 0, 0, tiled=True)
+    (terms,) = call(
+        tail_kernel, "tail", [whole(1536, 128)], [((8, 32, 128), F32)], [], 2 * 32 * 1536 * 128
+    )(got.reshape(1536, 128))
+    terms, got = lax.optimization_barrier((terms, got.reshape(32, 2, 24, 128)))
+    terms = lax.all_to_all(terms, "space", 0, 0, tiled=True).reshape(8, 4, 8, 128)
     filter_grad = pl.pallas_call(
         finish_kernel,
         out_shape=jax.ShapeDtypeStruct((27, 4, 256), F32),

time: 157 us -> 153 us (0.975)
  waiting for transfers between devices: 20.8 us -> 11.5 us
  starting transfers between devices: 29.1 us -> 36.6 us
  local copies, waits for them, and re-layouts: 5.53 us -> 1.95 us
  Pallas kernels: 15 us -> 16.6 us
    ppermute x6 -> x8, waiting for transfers between devices: 17.1 us -> 7.13 us  [swapped(): return lax.ppermute(array, axis, [(n, n ^ bit) for n in range(count)])]
    ppermute x6 -> x8, starting transfers between devices: 14.1 us -> 22.9 us  [swapped(): return lax.ppermute(array, axis, [(n, n ^ bit) for n in range(count)])]
    pallas_call x3 -> x4, Pallas kernels: 2.94 us -> 5.25 us  [the longest x1 3.15 us: local(): call(first_kernel, 'first', [SCALAR, SCALAR, HBM, HBM, whole(27, 4, 256)]...]
    all_to_all x2, starting transfers between devices: 10.3 us -> 8.68 us  [local(): got = lax.all_to_all(both, 'space', 0, 0, tiled=True)]
    unnamed x9 -> x0, local copies, waits for them, and re-layouts: 1.6 us -> none
  transfers between devices with their start and end apart: 9 -> 11, of which waited for: 5 -> 6; matrix products, arithmetic and copies ran while one was open for 1% -> 1% of each run, Pallas kernels for 6% -> 5%
where the time goes in v4:
time: 153 us
  blocking collectives  85.1 us (56%)
  starting transfers between devices  36.6 us (24%)
  Pallas kernels  16.6 us (11%)
  waiting for transfers between devices  11.5 us (8%)
  local copies, waits for them, and re-layouts  1.95 us (1%)
    all_to_all x2, blocking collectives, local(): got = lax.all_to_all(both.reshape(64, 24, 128), 'filt', 0, 0, tiled=True)  85.1 us
    ppermute x8, starting transfers between devices, swapped(): return lax.ppermute(array, axis, [(n, n ^ bit) for n in range(count)])  22.9 us
    all_to_all x2, starting transfers between devices, local(): got = lax.all_to_all(both, 'space', 0, 0, tiled=True)  8.68 us
    ppermute x8, waiting for transfers between devices, swapped(): return lax.ppermute(array, axis, [(n, n ^ bit) for n in range(count)])  7.13 us
    all_to_all x1, starting transfers between devices, local(): lax.all_to_all(terms, 'space', 0, 0, tiled=True).reshape(8, 4, 8, 128)  5.07 us
    all_to_all x1, waiting for transfers between devices, local(): lax.all_to_all(terms, 'space', 0, 0, tiled=True).reshape(8, 4, 8, 128)  3.73 us
    pallas_call x1, Pallas kernels, local(): call(filter_grad_kernel, 'filter_grad', [SCALAR, whole(8, 448, 128), whol...  3.55 us
    pallas_call x1, Pallas kernels, local(): call(first_kernel, 'first', [SCALAR, SCALAR, HBM, HBM, whole(27, 4, 256)]...  3.15 us
  transfers between devices with their start and end apart: 11, of which 6 were waited for; matrix products, arithmetic and copies ran while one was open for 1% of the time, Pallas kernels for 5%

profile of v4, /device:TPU:1, one launch (start us, length us, event | category | flops | bytes accessed | tf_op | source)
XLA Modules:
  0.0 152.8 jit_solution(10945087272724898528)
XLA Ops:
  0.6 3.1 %first.1 = bf16[1536,128]{1,0:T(8,128)(2,1)} custom-call(s32[1]{0:T(128)} %bitcast.1.slab_ref, f32[1,4]{1,0:T(1,128)} %bitcast.45, bf16[4,128,128]{2,1,0:T(8,128)(2,1)} %bitcast.41, bf16[4,128,128]{2,1,0:T(8,128)(2,1)} %bitcast.42, bf16[27,4,256]{2,1,0:T(4,128)(2,1)} %bitcast.44), custom_call_target="tpu_custom_call" | custom-call | flops 163577856 | bytes 4194304 | tf_op jit(solution)/shard_map/first/pallas_call | solution.py:369
  3.8 48.4 %all_to_all.25 = bf16[64,24,128]{2,1,0:T(8,128)(2,1)S(1)} all-to-all(bf16[64,24,128]{2,1,0:T(8,128)(2,1)} %bitcast.36), channel_id=1, replica_groups=mesh['space'=8,'filt'=64] {'filt'}, dimensions={0} | all-to-all | bytes 786432 | tf_op jit(solution)/shard_map/all_to_all | solution.py:384
  52.2 1.4 middle.1
  53.6 4.2 %all-to-all-start.1 = ((bf16[8,448,128]{2,1,0:T(8,128)(2,1)}), bf16[8,448,128]{2,1,0:T(8,128)(2,1)S(1)}, u32[]{:S(2)}, u32[]{:S(2)}) async-start(bf16[8,448,128]{2,1,0:T(8,128)(2,1)} %get-tuple-element.26), calls=%async_computation.1 | async-start | bytes 1835008 | tf_op jit(solution)/shard_map/all_to_all | solution.py:394
  57.8 3.7 %collective-permute-start.2 = (bf16[256,128]{1,0:T(8,128)(2,1)S(1)}, bf16[256,128]{1,0:T(8,128)(2,1)S(1)}, u32[]{:S(2)}, u32[]{:S(2)}) collective-permute-start(bf16[256,128]{1,0:T(8,128)(2,1)S(1)} %get-tuple-element.23.own_ref), channel_id=1, source_target_pairs={{0,6},{1,7},{2,4},{3,5},{4,2},{5,3},{6,0},{7,1},{8,14},{9,15},{10,... | collective-permute-start | bytes 196616 | tf_op jit(solution)/shard_map/ppermute | solution.py:362
  61.5 2.5 %collective-permute-start.1 = (bf16[256,128]{1,0:T(8,128)(2,1)S(1)}, bf16[256,128]{1,0:T(8,128)(2,1)S(1)}, u32[]{:S(2)}, u32[]{:S(2)}) collective-permute-start(bf16[256,128]{1,0:T(8,128)(2,1)S(1)} %get-tuple-element.23.own_ref), channel_id=1, source_target_pairs={{0,4},{1,5},{2,6},{3,7},{4,0},{5,1},{6,2},{7,3},{8,12},{9,13},{10,... | collective-permute-start | bytes 196616 | tf_op jit(solution)/shard_map/ppermute | solution.py:362
  64.0 3.1 %collective-permute-start = (bf16[256,128]{1,0:T(8,128)(2,1)S(1)}, bf16[256,128]{1,0:T(8,128)(2,1)S(1)}, u32[]{:S(2)}, u32[]{:S(2)}) collective-permute-start(bf16[256,128]{1,0:T(8,128)(2,1)S(1)} %get-tuple-element.23.own_ref), channel_id=1, source_target_pairs={{0,2},{1,3},{2,0},{3,1},{4,6},{5,7},{6,4},{7,5},{8,10},{9,11},{10,... | collective-permute-start | bytes 196616 | tf_op jit(solution)/shard_map/ppermute | solution.py:362
  67.1 2.3 %collective-permute-done.1.second_ref = bf16[256,128]{1,0:T(8,128)(2,1)S(1)} collective-permute-done((bf16[256,128]{1,0:T(8,128)(2,1)S(1)}, bf16[256,128]{1,0:T(8,128)(2,1)S(1)}, u32[]{:S(2)}, u32[]{:S(2)}) %collective-permute-start.1) | collective-permute-done | bytes 65568 | tf_op jit(solution)/shard_map/ppermute | solution.py:362
  69.4 1.4 collective-permute-done.first_ref
  70.8 0.5 filters.1
  71.3 0.7 all-to-all-done.1.got_ref.mine_ref
  72.0 2.3 %collective-permute-start.3 = (bf16[8,256,128]{2,1,0:T(8,128)(2,1)S(1)}, bf16[8,256,128]{2,1,0:T(8,128)(2,1)S(1)}, u32[]{:S(2)}, u32[]{:S(2)}) collective-permute-start(bf16[8,256,128]{2,1,0:T(8,128)(2,1)S(1)} %slice.19), channel_id=1, source_target_pairs={{0,1},{1,0},{2,3},{3,2},{4,5},{5,4},{6,7},{7,6},{8,9},{9,8},{10,11... | collective-permute-start | bytes 1572872 | tf_op jit(solution)/shard_map/ppermute | solution.py:362
  74.3 2.2 %backward.1 = (f32[8,256,128]{2,1,0:T(8,128)S(1)}, bf16[8,256,128]{2,1,0:T(8,128)(2,1)S(1)}) custom-call(bf16[8,448,128]{2,1,0:T(8,128)(2,1)S(1)} %all-to-all-done.1.got_ref.mine_ref, bf16[128,896]{1,0:T(8,128)(2,1)S(1)} %get-tuple-element.28.filter_ref), custom_call_target="tpu_custom_call" | custom-call | flops 939524096 | bytes 4194304 | tf_op jit(solution)/shard_map/backward/pallas_call | solution.py:407
  76.5 2.1 %collective-permute-start.4 = (bf16[8,256,128]{2,1,0:T(8,128)(2,1)S(1)}, bf16[8,256,128]{2,1,0:T(8,128)(2,1)S(1)}, u32[]{:S(2)}, u32[]{:S(2)}) collective-permute-start(bf16[8,256,128]{2,1,0:T(8,128)(2,1)S(1)} %get-tuple-element.31), channel_id=1, source_target_pairs={{0,1},{1,0},{2,3},{3,2},{4,5},{5,4},{6,7},{7,6},{8,9},{9,8},{10,11... | collective-permute-start | bytes 1572872 | tf_op jit(solution)/shard_map/ppermute | solution.py:362
  78.6 2.2 %forward.1.out_ref = bf16[8,448,128]{2,1,0:T(8,128)(2,1)} custom-call(bf16[8,448,128]{2,1,0:T(8,128)(2,1)S(1)} %all-to-all-done.1.got_ref.mine_ref, bf16[8,256,128]{2,1,0:T(8,128)(2,1)S(1)} %collective-permute-done.3.theirs_ref, bf16[288,384]{1,0:T(8,128)(2,1)S(1)} %get-tuple-element.33.stacked_ref), custom_call_target="tpu_custom_call" | custom-call | flops 905969664 | bytes 4194304 | tf_op jit(solution)/shard_map/forward/pallas_call | solution.py:418
  80.8 0.9 sum.1
  81.7 4.5 %all-to-all-start.2 = ((bf16[8,448,128]{2,1,0:T(8,128)(2,1)}), bf16[8,448,128]{2,1,0:T(8,128)(2,1)S(1)}, u32[]{:S(2)}, u32[]{:S(2)}) async-start(bf16[8,448,128]{2,1,0:T(8,128)(2,1)} %sum.1), calls=%async_computation.2 | async-start | bytes 1835008 | tf_op jit(solution)/shard_map/all_to_all | solution.py:448
  86.1 3.5 %filter_grad.1 = (bf16[256,128]{1,0:T(8,128)(2,1)S(1)}, bf16[256,128]{1,0:T(8,128)(2,1)S(1)}, bf16[256,128]{1,0:T(8,128)(2,1)S(1)}, bf16[256,128]{1,0:T(8,128)(2,1)S(1)}) custom-call(s32[1]{0:T(128)} %bitcast.rank_ref, bf16[8,448,128]{2,1,0:T(8,128)(2,1)S(1)} %all-to-all-done.1.got_ref.mine_ref, bf16[8,256,128]{2,1,0:T(8,128)(2,1)S(1)} %collective-permute-done.3.theirs_ref), custom_call_target="tpu_custom_call" | custom-call | flops 939524096 | bytes 4194304 | tf_op jit(solution)/shard_map/filter_grad/pallas_call | solution.py:439
  89.7 2.8 %collective-permute-start.5 = (bf16[256,128]{1,0:T(8,128)(2,1)S(1)}, bf16[256,128]{1,0:T(8,128)(2,1)S(1)}, u32[]{:S(2)}, u32[]{:S(2)}) collective-permute-start(bf16[256,128]{1,0:T(8,128)(2,1)S(1)} %get-tuple-element.38), channel_id=1, source_target_pairs={{0,2},{1,3},{2,0},{3,1},{4,6},{5,7},{6,4},{7,5},{8,10},{9,11},{10,... | collective-permute-start | bytes 196616 | tf_op jit(solution)/shard_map/ppermute | solution.py:362
  92.5 3.1 %collective-permute-start.6 = (bf16[256,128]{1,0:T(8,128)(2,1)S(1)}, bf16[256,128]{1,0:T(8,128)(2,1)S(1)}, u32[]{:S(2)}, u32[]{:S(2)}) collective-permute-start(bf16[256,128]{1,0:T(8,128)(2,1)S(1)} %get-tuple-element.39), channel_id=1, source_target_pairs={{0,4},{1,5},{2,6},{3,7},{4,0},{5,1},{6,2},{7,3},{8,12},{9,13},{10,... | collective-permute-start | bytes 196616 | tf_op jit(solution)/shard_map/ppermute | solution.py:362
  95.6 3.4 %collective-permute-start.7 = (bf16[256,128]{1,0:T(8,128)(2,1)S(1)}, bf16[256,128]{1,0:T(8,128)(2,1)S(1)}, u32[]{:S(2)}, u32[]{:S(2)}) collective-permute-start(bf16[256,128]{1,0:T(8,128)(2,1)S(1)} %get-tuple-element.40), channel_id=1, source_target_pairs={{0,6},{1,7},{2,4},{3,5},{4,2},{5,3},{6,0},{7,1},{8,14},{9,15},{10,... | collective-permute-start | bytes 196616 | tf_op jit(solution)/shard_map/ppermute | solution.py:362
  99.0 0.5 collective-permute-done.6.second_ref
  99.5 2.9 %collective-permute-done.7.third_ref = bf16[256,128]{1,0:T(8,128)(2,1)S(1)} collective-permute-done((bf16[256,128]{1,0:T(8,128)(2,1)S(1)}, bf16[256,128]{1,0:T(8,128)(2,1)S(1)}, u32[]{:S(2)}, u32[]{:S(2)}) %collective-permute-start.7) | collective-permute-done | bytes 65568 | tf_op jit(solution)/shard_map/ppermute | solution.py:362
  102.4 0.7 last.1
  103.1 36.7 %all_to_all.26 = bf16[64,24,128]{2,1,0:T(8,128)(2,1)S(1)} all-to-all(bf16[64,24,128]{2,1,0:T(8,128)(2,1)S(1)} %bitcast.32), channel_id=1, replica_groups=mesh['space'=8,'filt'=64] {'filt'}, dimensions={0} | all-to-all | bytes 786432 | tf_op jit(solution)/shard_map/all_to_all | solution.py:458
  139.8 0.9 tail.1
  140.8 5.1 %all-to-all-start.4 = ((f32[8,32,128]{2,1,0:T(8,128)}), f32[8,32,128]{2,1,0:T(8,128)S(1)}, u32[]{:S(2)}, u32[]{:S(2)}) async-start(f32[8,32,128]{2,1,0:T(8,128)} %tail.1), calls=%async_computation.4 | async-start | bytes 262144 | tf_op jit(solution)/shard_map/all_to_all | solution.py:464
  145.9 0.7 copy.13
  146.6 0.3 copy.17
  147.2 0.7 copy.11
  147.9 3.7 %all-to-all-done.4 = f32[8,32,128]{2,1,0:T(8,128)S(1)} async-done(((f32[8,32,128]{2,1,0:T(8,128)}), f32[8,32,128]{2,1,0:T(8,128)S(1)}, u32[]{:S(2)}, u32[]{:S(2)}) %all-to-all-start.4) | async-done | bytes 131104 | tf_op jit(solution)/shard_map/all_to_all | solution.py:464
  151.6 1.1 finish.1
  (12 shorter events, 0.5 us)
Async XLA Ops:
  53.6 18.4 %all-to-all-start.1 = ((bf16[8,448,128]{2,1,0:T(8,128)(2,1)}), bf16[8,448,128]{2,1,0:T(8,128)(2,1)S(1)}, u32[]{:S(2)}, u32[]{:S(2)}) async-start(bf16[8,448,128]{2,1,0:T(8,128)(2,1)} %get-tuple-element.26), calls=%async_computation.1 | async-start | bytes 1835008 | tf_op jit(solution)/shard_map/all_to_all | solution.py:394
  57.8 9.3 %collective-permute-start.2 = (bf16[256,128]{1,0:T(8,128)(2,1)S(1)}, bf16[256,128]{1,0:T(8,128)(2,1)S(1)}, u32[]{:S(2)}, u32[]{:S(2)}) collective-permute-start(bf16[256,128]{1,0:T(8,128)(2,1)S(1)} %get-tuple-element.23.own_ref), channel_id=1, source_target_pairs={{0,6},{1,7},{2,4},{3,5},{4,2},{5,3},{6,0},{7,1},{8,14},{9,15},{10,... | collective-permute-start | bytes 196616 | tf_op jit(solution)/shard_map/ppermute | solution.py:362
  61.5 7.9 %collective-permute-start.1 = (bf16[256,128]{1,0:T(8,128)(2,1)S(1)}, bf16[256,128]{1,0:T(8,128)(2,1)S(1)}, u32[]{:S(2)}, u32[]{:S(2)}) collective-permute-start(bf16[256,128]{1,0:T(8,128)(2,1)S(1)} %get-tuple-element.23.own_ref), channel_id=1, source_target_pairs={{0,4},{1,5},{2,6},{3,7},{4,0},{5,1},{6,2},{7,3},{8,12},{9,13},{10,... | collective-permute-start | bytes 196616 | tf_op jit(solution)/shard_map/ppermute | solution.py:362
  64.0 6.9 %collective-permute-start = (bf16[256,128]{1,0:T(8,128)(2,1)S(1)}, bf16[256,128]{1,0:T(8,128)(2,1)S(1)}, u32[]{:S(2)}, u32[]{:S(2)}) collective-permute-start(bf16[256,128]{1,0:T(8,128)(2,1)S(1)} %get-tuple-element.23.own_ref), channel_id=1, source_target_pairs={{0,2},{1,3},{2,0},{3,1},{4,6},{5,7},{6,4},{7,5},{8,10},{9,11},{10,... | collective-permute-start | bytes 196616 | tf_op jit(solution)/shard_map/ppermute | solution.py:362
  72.0 4.5 %collective-permute-start.3 = (bf16[8,256,128]{2,1,0:T(8,128)(2,1)S(1)}, bf16[8,256,128]{2,1,0:T(8,128)(2,1)S(1)}, u32[]{:S(2)}, u32[]{:S(2)}) collective-permute-start(bf16[8,256,128]{2,1,0:T(8,128)(2,1)S(1)} %slice.19), channel_id=1, source_target_pairs={{0,1},{1,0},{2,3},{3,2},{4,5},{5,4},{6,7},{7,6},{8,9},{9,8},{10,11... | collective-permute-start | bytes 1572872 | tf_op jit(solution)/shard_map/ppermute | solution.py:362
  76.5 4.2 %collective-permute-start.4 = (bf16[8,256,128]{2,1,0:T(8,128)(2,1)S(1)}, bf16[8,256,128]{2,1,0:T(8,128)(2,1)S(1)}, u32[]{:S(2)}, u32[]{:S(2)}) collective-permute-start(bf16[8,256,128]{2,1,0:T(8,128)(2,1)S(1)} %get-tuple-element.31), channel_id=1, source_target_pairs={{0,1},{1,0},{2,3},{3,2},{4,5},{5,4},{6,7},{7,6},{8,9},{9,8},{10,11... | collective-permute-start | bytes 1572872 | tf_op jit(solution)/shard_map/ppermute | solution.py:362
  81.7 20.7 %all-to-all-start.2 = ((bf16[8,448,128]{2,1,0:T(8,128)(2,1)}), bf16[8,448,128]{2,1,0:T(8,128)(2,1)S(1)}, u32[]{:S(2)}, u32[]{:S(2)}) async-start(bf16[8,448,128]{2,1,0:T(8,128)(2,1)} %sum.1), calls=%async_computation.2 | async-start | bytes 1835008 | tf_op jit(solution)/shard_map/all_to_all | solution.py:448
  89.7 9.3 %collective-permute-start.5 = (bf16[256,128]{1,0:T(8,128)(2,1)S(1)}, bf16[256,128]{1,0:T(8,128)(2,1)S(1)}, u32[]{:S(2)}, u32[]{:S(2)}) collective-permute-start(bf16[256,128]{1,0:T(8,128)(2,1)S(1)} %get-tuple-element.38), channel_id=1, source_target_pairs={{0,2},{1,3},{2,0},{3,1},{4,6},{5,7},{6,4},{7,5},{8,10},{9,11},{10,... | collective-permute-start | bytes 196616 | tf_op jit(solution)/shard_map/ppermute | solution.py:362
  92.5 7.0 %collective-permute-start.6 = (bf16[256,128]{1,0:T(8,128)(2,1)S(1)}, bf16[256,128]{1,0:T(8,128)(2,1)S(1)}, u32[]{:S(2)}, u32[]{:S(2)}) collective-permute-start(bf16[256,128]{1,0:T(8,128)(2,1)S(1)} %get-tuple-element.39), channel_id=1, source_target_pairs={{0,4},{1,5},{2,6},{3,7},{4,0},{5,1},{6,2},{7,3},{8,12},{9,13},{10,... | collective-permute-start | bytes 196616 | tf_op jit(solution)/shard_map/ppermute | solution.py:362
  95.6 6.8 %collective-permute-start.7 = (bf16[256,128]{1,0:T(8,128)(2,1)S(1)}, bf16[256,128]{1,0:T(8,128)(2,1)S(1)}, u32[]{:S(2)}, u32[]{:S(2)}) collective-permute-start(bf16[256,128]{1,0:T(8,128)(2,1)S(1)} %get-tuple-element.40), channel_id=1, source_target_pairs={{0,6},{1,7},{2,4},{3,5},{4,2},{5,3},{6,0},{7,1},{8,14},{9,15},{10,... | collective-permute-start | bytes 196616 | tf_op jit(solution)/shard_map/ppermute | solution.py:362
  140.8 10.8 %all-to-all-start.4 = ((f32[8,32,128]{2,1,0:T(8,128)}), f32[8,32,128]{2,1,0:T(8,128)S(1)}, u32[]{:S(2)}, u32[]{:S(2)}) async-start(f32[8,32,128]{2,1,0:T(8,128)} %tail.1), calls=%async_computation.4 | async-start | bytes 262144 | tf_op jit(solution)/shard_map/all_to_all | solution.py:464

commit v5 on v4

--- a/solution.py
+++ b/solution.py
@@ -51,13 +51,18 @@
     return jnp.where(n < 128, cell, jnp.where(n < 320, rim, g * 24 + 8 + (corner >> 1) * 8 + (corner & 1) * 7))
 
 
+def by_28(n):
+    part = (n * 2341) >> 16
+    return part, n - part * 28
+
+
 def matrix_row(n):
-    g, m = by_24(n)
+    g, m = by_28(n)
     i, w = (m - 8) >> 3, m & 7
     cell = (m >> 2) * 64 + (m & 3) * 16 + g
     rim = 128 + (w - 1) * 32 + g * 2 + i
-    inner = (w >= 1) & (w <= 6)
-    return jnp.where(m < 8, cell, jnp.where(inner, rim, 320 + g * 4 + i * 2 + (w >> 2)))
+    rim = jnp.where((w >= 1) & (w <= 6), rim, 320 + g * 4 + i * 2 + (w >> 2))
+    return jnp.where(m < 8, cell, jnp.where(m < 24, rim, 384 + g * 4 + m - 24))
 
 
 def quarter_of(rank):
@@ -82,7 +87,7 @@
     return result
 
 
-def first_kernel(slab_ref, scales_ref, cells_ref, rims_ref, weights_ref, out_ref, raw, cells, rims, sems):
+def first_kernel(slab_ref, scales_ref, cells_ref, rims_ref, weights_ref, out_ref, raw, cells, rims, packed, sems):
     copies = [
         pltpu.make_async_copy(cells_ref, raw, sems.at[0]),
         pltpu.make_async_copy(rims_ref, rims.at[:, 16:144], sems.at[1]),
@@ -105,20 +110,34 @@
             parts += [cells[2 * core + i, at : at + 32] for i in range(2)]
             parts += [rims[2 * core + i, at : at + 64] for i in range(2)]
             parts.append(own[core])
-        out_ref[block * 384 : block * 384 + 384] = moved(order, jnp.concatenate(parts, axis=0))
-
-
-def middle_kernel(got_ref, out_ref, corners_ref):
+        part = slice(block * 384, block * 384 + 384)
+        packed[part] = moved(order, jnp.concatenate(parts, axis=0))
+        copies.append(pltpu.make_async_copy(packed.at[part], out_ref.at[part], sems.at[2 + block]))
+        copies[-1].start()
+    for copy in copies[2:]:
+        copy.wait()
+
+
+def middle_kernel(got_ref, out_ref, corners_ref, cells, rims, sems):
     order = select_rows(384, message_row, 384)
+    copies = []
     for block in range(4):
         rows = moved(order, got_ref[block * 384 : block * 384 + 384])
         for i in range(2):
             for y in range(4):
                 piece = rows[i * 64 + y * 16 : i * 64 + y * 16 + 16]
-                for place in range(4):
-                    out_ref[2 * place + i, y * 64 + block * 16 : y * 64 + block * 16 + 16] = piece
-            out_ref[2 * block + i, 256:448] = rows[128:320]
+                cells[i, y * 64 + block * 16 : y * 64 + block * 16 + 16] = piece
+        rims[block] = rows[128:320]
+        for i in range(2):
+            to = 2 * block + i
+            copies.append(pltpu.make_async_copy(rims.at[block], out_ref.at[to, 256:448], sems.at[to]))
+            copies[-1].start()
         corners_ref[block * 64 : block * 64 + 64] = rows[320:384]
+    for to in range(8):
+        copies.append(pltpu.make_async_copy(cells.at[to % 2], out_ref.at[to, 0:256], sems.at[8 + to]))
+        copies[-1].start()
+    for copy in copies:
+        copy.wait()
 
 
 def filter_kernel(rank_ref, own_ref, first_ref, second_ref, third_ref, filter_ref, stacked_ref, quarters):
@@ -239,9 +258,7 @@
         copy.wait()
 
 
-def filter_grad_kernel(
-    rank_ref, got_ref, theirs_ref, own_ref, first_ref, second_ref, third_ref, shifted, image, total
-):
+def filter_grad_kernel(rank_ref, got_ref, theirs_ref, own_ref, send_ref, shifted, image, total):
     shift(got_ref, shifted)
     image[864:896] = jnp.zeros((32, 2048), BF16)
     total[...] = jnp.zeros((1024, 128), F32)
@@ -251,20 +268,18 @@
         cells = jnp.concatenate([plane_of(got_ref, theirs_ref, half * 4 + z) for z in range(4)], axis=1)
         total[:896] += lax.dot_general(image[...], cells, (((1,), (1,)), ((), ())), preferred_element_type=F32)
     rank = rank_ref[0]
-    for n, ref in enumerate((own_ref, first_ref, second_ref, third_ref)):
-        quarter = quarter_of(rank) ^ n
-        part = ((quarter >> 1) ^ (rank & 1)) * 64
+    for n, ref in enumerate((own_ref, send_ref)):
+        part = (((rank >> 1) ^ n ^ rank) & 1) * 64
         order = select_rows(256, lambda n: (n & 3) * 128 + part + (n >> 2), 512)
-        lanes = [
-            total[pl.ds(pl.multiple_of((4 * (quarter & 1) + m) * 128, 128), 128)].astype(BF16) for m in range(4)
-        ]
-        ref[...] = lax.dot_general(
-            order, jnp.concatenate(lanes, axis=1), (((1,), (1,)), ((), ())), preferred_element_type=F32
-        ).astype(BF16)
-
-
-def last_kernel(got_ref, own_ref, first_ref, second_ref, third_ref, out_ref, grads):
-    order = select_rows(384, matrix_row, 384)
+        for h in range(2):
+            lanes = [total[j * 128 : j * 128 + 128].astype(BF16) for j in range(4 * h, 4 * h + 4)]
+            ref[h * 256 : h * 256 + 256] = lax.dot_general(
+                order, jnp.concatenate(lanes, axis=1), (((1,), (1,)), ((), ())), preferred_element_type=F32
+            ).astype(BF16)
+
+
+def last_kernel(got_ref, own_ref, other_ref, out_ref, grads):
+    order = select_rows(448, matrix_row, 448)
     for i in range(2):
         grad = got_ref[i, :256].astype(F32)
         for n in range(1, 4):
@@ -276,20 +291,19 @@
             parts += [grads[i, y * 64 + block * 16 : y * 64 + block * 16 + 16] for y in range(4)]
         rims = [got_ref[2 * block + i, 256:448].astype(F32) for i in range(2)]
         parts.append((rims[0] + rims[1]).astype(BF16))
-        part = slice(block * 64, block * 64 + 64)
-        terms = [ref[part].astype(F32) for ref in (own_ref, first_ref, second_ref, third_ref)]
-        parts.append(sum(terms[1:], terms[0]).astype(BF16))
-        out_ref[block * 384 : block * 384 + 384] = moved(order, jnp.concatenate(parts, axis=0))
+        for h in range(2):
+            part = slice(h * 256 + block * 64, h * 256 + block * 64 + 64)
+            parts.append((own_ref[part].astype(F32) + other_ref[part].astype(F32)).astype(BF16))
+        out_ref[block * 448 : block * 448 + 448] = moved(order, jnp.concatenate(parts, axis=0))
 
 
 def tail_kernel(got_ref, out_ref):
-    row = lax.broadcasted_iota(jnp.int32, (32, 1536), 0)
-    col = lax.broadcasted_iota(jnp.int32, (32, 1536), 1)
-    sender, m = by_24(col)
-    corner = (m >= 8) & (((m & 7) == 0) | ((m & 7) == 7))
-    n = ((m - 8) >> 3) * 2 + ((m & 7) >> 2)
-    quarter = quarter_of(sender)
-    target = (quarter >> 1) * 16 + (sender & 1) * 8 + (quarter & 1) * 4 + n
+    row = lax.broadcasted_iota(jnp.int32, (32, 1792), 0)
+    col = lax.broadcasted_iota(jnp.int32, (32, 1792), 1)
+    sender, m = by_28(col)
+    corner = (m >= 8) & (((m & 7) == 0) | ((m & 7) == 7) | (m >= 24))
+    n = jnp.where(m < 24, ((m - 8) >> 3) * 2 + ((m & 7) >> 2), m - 20)
+    target = ((sender >> 1) & 1) * 16 + (sender & 1) * 8 + n
     order = jnp.where(corner & (target == row), 1.0, 0.0).astype(BF16)
     rows = jnp.dot(order, got_ref[...], preferred_element_type=F32)
     for n in range(8):
@@ -371,8 +385,9 @@
         "first",
         [SCALAR, SCALAR, HBM, HBM, whole(27, 4, 256)],
         [((1536, 128), BF16)],
-        [((4, 128, 128), BF16), ((4, 128, 128), BF16), ((4, 160, 128), BF16), DMA((2,))],
+        [((4, 128, 128), BF16), ((4, 128, 128), BF16), ((4, 160, 128), BF16), ((1536, 128), BF16), DMA((6,))],
         2 * 4 * 384 * 416 * 128,
+        [HBM],
         mib=56,
     )(
         slab,
@@ -388,8 +403,9 @@
         "middle",
         [whole(1536, 128)],
         [((8, 448, 128), BF16), ((256, 128), BF16)],
-        [],
+        [((2, 256, 128), BF16), ((4, 192, 128), BF16), DMA((16,))],
         2 * 4 * 384 * 384 * 128,
+        [HBM, whole(256, 128)],
     )(got.reshape(1536, 128))
     got = lax.all_to_all(both, "space", 0, 0, tiled=True)
     filters = [filters] + [swapped(filters, "filt", 2 * n) for n in range(1, 4)]
@@ -440,27 +456,26 @@
         filter_grad_kernel,
         "filter_grad",
         [SCALAR, whole(8, 448, 128), whole(8, 256, 128)],
-        [((256, 128), BF16)] * 4,
+        [((512, 128), BF16)] * 2,
         [((10, 96, 768), BF16), ((896, 2048), BF16), ((1024, 128), F32)],
         2 * 8 * 896 * 128 * 512,
     )(rank, cells, theirs)
 
     got = lax.all_to_all(both, "space", 0, 0, tiled=True)
-    terms = [terms[0]] + [swapped(terms[n], "filt", 2 * n) for n in range(1, 4)]
     (both,) = call(
         last_kernel,
         "last",
-        [whole(8, 448, 128)] + [whole(256, 128)] * 4,
-        [((1536, 128), BF16)],
+        [whole(8, 448, 128)] + [whole(512, 128)] * 2,
+        [((1792, 128), BF16)],
         [((2, 256, 128), BF16)],
         2 * 4 * 384 * 384 * 128,
-    )(got, *terms)
-    got = lax.all_to_all(both.reshape(64, 24, 128), "filt", 0, 0, tiled=True)
+    )(got, terms[0], swapped(terms[1], "filt", 2))
+    got = lax.all_to_all(both.reshape(448, 4, 128), "filt", 0, 0, tiled=True)
 
     (terms,) = call(
-        tail_kernel, "tail", [whole(1536, 128)], [((8, 32, 128), F32)], [], 2 * 32 * 1536 * 128
-    )(got.reshape(1536, 128))
-    terms, got = lax.optimization_barrier((terms, got.reshape(32, 2, 24, 128)))
+        tail_kernel, "tail", [whole(1792, 128)], [((8, 32, 128), F32)], [], 2 * 32 * 1792 * 128
+    )(got.reshape(1792, 128))
+    terms, got = lax.optimization_barrier((terms, got.reshape(32, 2, 28, 128)))
     terms = lax.all_to_all(terms, "space", 0, 0, tiled=True).reshape(8, 4, 8, 128)
     filter_grad = pl.pallas_call(
         finish_kernel,

time: 153 us -> 151 us (0.987)
  starting transfers between devices: 36.6 us -> 28.4 us
  waiting for transfers between devices: 11.5 us -> 15 us
  blocking collectives: 85.1 us -> 86.9 us
    all_to_all x0 -> x1, blocking collectives: none -> 38.5 us  [local(): got = lax.all_to_all(both.reshape(448, 4, 128), 'filt', 0, 0, tiled=True)]
    all_to_all x2 -> x1, blocking collectives: 85.1 us -> 48.4 us  [local(): got = lax.all_to_all(both.reshape(64, 24, 128), 'filt', 0, 0, tiled=True)]
    ppermute x8 -> x6, starting transfers between devices: 22.9 us -> 16.4 us  [swapped(): return lax.ppermute(array, axis, [(n, n ^ bit) for n in range(count)])]
    all_to_all x2, waiting for transfers between devices: 0.68 us -> 4.46 us  [local(): got = lax.all_to_all(both, 'space', 0, 0, tiled=True)]
    all_to_all x1, starting transfers between devices: 5.07 us -> 3.38 us  [local(): lax.all_to_all(terms, 'space', 0, 0, tiled=True).reshape(8, 4, 8, 128)]
    ppermute x8 -> x6, waiting for transfers between devices: 7.13 us -> 7.12 us  [swapped(): return lax.ppermute(array, axis, [(n, n ^ bit) for n in range(count)])]
  transfers between devices with their start and end apart: 11 -> 9, of which waited for: 6 -> 6; matrix products, arithmetic and copies ran while one was open for 1% -> 1% of each run, Pallas kernels for 5% -> 5%
where the time goes in v5:
time: 151 us; the launch traced here: 150 us
  blocking collectives  86.9 us (58%)
  starting transfers between devices  28.4 us (19%)
  Pallas kernels  16.6 us (11%)
  waiting for transfers between devices  15 us (10%)
  local copies, waits for them, and re-layouts  2.04 us (1%)
    all_to_all x1, blocking collectives, local(): got = lax.all_to_all(both.reshape(64, 24, 128), 'filt', 0, 0, tiled=True)  48.4 us
    all_to_all x1, blocking collectives, local(): got = lax.all_to_all(both.reshape(448, 4, 128), 'filt', 0, 0, tiled=True)  38.5 us
    ppermute x6, starting transfers between devices, swapped(): return lax.ppermute(array, axis, [(n, n ^ bit) for n in range(count)])  16.4 us
    all_to_all x2, starting transfers between devices, local(): got = lax.all_to_all(both, 'space', 0, 0, tiled=True)  8.7 us
    ppermute x6, waiting for transfers between devices, swapped(): return lax.ppermute(array, axis, [(n, n ^ bit) for n in range(count)])  7.12 us
    all_to_all x2, waiting for transfers between devices, local(): got = lax.all_to_all(both, 'space', 0, 0, tiled=True)  4.46 us
    all_to_all x1, waiting for transfers between devices, local(): lax.all_to_all(terms, 'space', 0, 0, tiled=True).reshape(8, 4, 8, 128)  3.43 us
    all_to_all x1, starting transfers between devices, local(): lax.all_to_all(terms, 'space', 0, 0, tiled=True).reshape(8, 4, 8, 128)  3.38 us
  transfers between devices with their start and end apart: 9, of which 6 were waited for; matrix products, arithmetic and copies ran while one was open for 1% of the time, Pallas kernels for 5%

profile of v5, /device:TPU:1, one launch (start us, length us, event | category | flops | bytes accessed | tf_op | source)
XLA Modules:
  0.0 149.9 jit_solution(8517836789820333300)
XLA Ops:
  0.6 3.1 %first.1 = bf16[1536,128]{1,0:T(8,128)(2,1)} custom-call(s32[1]{0:T(128)} %bitcast.1.slab_ref, f32[1,4]{1,0:T(1,128)} %bitcast.42, bf16[4,128,128]{2,1,0:T(8,128)(2,1)} %bitcast.38, bf16[4,128,128]{2,1,0:T(8,128)(2,1)} %bitcast.39, bf16[27,4,256]{2,1,0:T(4,128)(2,1)} %bitcast.41), custom_call_target="tpu_custom_call" | custom-call | flops 163577856 | bytes 4194304 | tf_op jit(solution)/shard_map/first/pallas_call | solution.py:383
  3.8 48.4 %all_to_all.25 = bf16[64,24,128]{2,1,0:T(8,128)(2,1)S(1)} all-to-all(bf16[64,24,128]{2,1,0:T(8,128)(2,1)} %bitcast.33), channel_id=1, replica_groups=mesh['space'=8,'filt'=64] {'filt'}, dimensions={0} | all-to-all | bytes 786432 | tf_op jit(solution)/shard_map/all_to_all | solution.py:399
  52.1 1.5 middle.1
  53.6 4.2 %all-to-all-start.1 = ((bf16[8,448,128]{2,1,0:T(8,128)(2,1)}), bf16[8,448,128]{2,1,0:T(8,128)(2,1)S(1)}, u32[]{:S(2)}, u32[]{:S(2)}) async-start(bf16[8,448,128]{2,1,0:T(8,128)(2,1)} %get-tuple-element.24), calls=%async_computation.1 | async-start | bytes 1835008 | tf_op jit(solution)/shard_map/all_to_all | solution.py:410
  57.9 3.7 %collective-permute-start.2 = (bf16[256,128]{1,0:T(8,128)(2,1)S(1)}, bf16[256,128]{1,0:T(8,128)(2,1)S(1)}, u32[]{:S(2)}, u32[]{:S(2)}) collective-permute-start(bf16[256,128]{1,0:T(8,128)(2,1)S(1)} %get-tuple-element.21.own_ref), channel_id=1, source_target_pairs={{0,6},{1,7},{2,4},{3,5},{4,2},{5,3},{6,0},{7,1},{8,14},{9,15},{10,... | collective-permute-start | bytes 196616 | tf_op jit(solution)/shard_map/ppermute | solution.py:376
  61.5 2.5 %collective-permute-start.1 = (bf16[256,128]{1,0:T(8,128)(2,1)S(1)}, bf16[256,128]{1,0:T(8,128)(2,1)S(1)}, u32[]{:S(2)}, u32[]{:S(2)}) collective-permute-start(bf16[256,128]{1,0:T(8,128)(2,1)S(1)} %get-tuple-element.21.own_ref), channel_id=1, source_target_pairs={{0,4},{1,5},{2,6},{3,7},{4,0},{5,1},{6,2},{7,3},{8,12},{9,13},{10,... | collective-permute-start | bytes 196616 | tf_op jit(solution)/shard_map/ppermute | solution.py:376
  64.0 3.1 %collective-permute-start = (bf16[256,128]{1,0:T(8,128)(2,1)S(1)}, bf16[256,128]{1,0:T(8,128)(2,1)S(1)}, u32[]{:S(2)}, u32[]{:S(2)}) collective-permute-start(bf16[256,128]{1,0:T(8,128)(2,1)S(1)} %get-tuple-element.21.own_ref), channel_id=1, source_target_pairs={{0,2},{1,3},{2,0},{3,1},{4,6},{5,7},{6,4},{7,5},{8,10},{9,11},{10,... | collective-permute-start | bytes 196616 | tf_op jit(solution)/shard_map/ppermute | solution.py:376
  67.2 2.3 %collective-permute-done.1.second_ref = bf16[256,128]{1,0:T(8,128)(2,1)S(1)} collective-permute-done((bf16[256,128]{1,0:T(8,128)(2,1)S(1)}, bf16[256,128]{1,0:T(8,128)(2,1)S(1)}, u32[]{:S(2)}, u32[]{:S(2)}) %collective-permute-start.1) | collective-permute-done | bytes 65568 | tf_op jit(solution)/shard_map/ppermute | solution.py:376
  69.5 1.4 collective-permute-done.first_ref
  70.9 0.5 filters.1
  71.4 0.7 all-to-all-done.1.got_ref.mine_ref
  72.1 2.3 %collective-permute-start.3 = (bf16[8,256,128]{2,1,0:T(8,128)(2,1)S(1)}, bf16[8,256,128]{2,1,0:T(8,128)(2,1)S(1)}, u32[]{:S(2)}, u32[]{:S(2)}) collective-permute-start(bf16[8,256,128]{2,1,0:T(8,128)(2,1)S(1)} %slice.19), channel_id=1, source_target_pairs={{0,1},{1,0},{2,3},{3,2},{4,5},{5,4},{6,7},{7,6},{8,9},{9,8},{10,11... | collective-permute-start | bytes 1572872 | tf_op jit(solution)/shard_map/ppermute | solution.py:376
  74.4 2.2 %backward.1 = (f32[8,256,128]{2,1,0:T(8,128)S(1)}, bf16[8,256,128]{2,1,0:T(8,128)(2,1)S(1)}) custom-call(bf16[8,448,128]{2,1,0:T(8,128)(2,1)S(1)} %all-to-all-done.1.got_ref.mine_ref, bf16[128,896]{1,0:T(8,128)(2,1)S(1)} %get-tuple-element.26.filter_ref), custom_call_target="tpu_custom_call" | custom-call | flops 939524096 | bytes 4194304 | tf_op jit(solution)/shard_map/backward/pallas_call | solution.py:423
  76.5 2.1 %collective-permute-start.4 = (bf16[8,256,128]{2,1,0:T(8,128)(2,1)S(1)}, bf16[8,256,128]{2,1,0:T(8,128)(2,1)S(1)}, u32[]{:S(2)}, u32[]{:S(2)}) collective-permute-start(bf16[8,256,128]{2,1,0:T(8,128)(2,1)S(1)} %get-tuple-element.29), channel_id=1, source_target_pairs={{0,1},{1,0},{2,3},{3,2},{4,5},{5,4},{6,7},{7,6},{8,9},{9,8},{10,11... | collective-permute-start | bytes 1572872 | tf_op jit(solution)/shard_map/ppermute | solution.py:376
  78.6 2.2 %forward.1.out_ref = bf16[8,448,128]{2,1,0:T(8,128)(2,1)} custom-call(bf16[8,448,128]{2,1,0:T(8,128)(2,1)S(1)} %all-to-all-done.1.got_ref.mine_ref, bf16[8,256,128]{2,1,0:T(8,128)(2,1)S(1)} %collective-permute-done.3.theirs_ref, bf16[288,384]{1,0:T(8,128)(2,1)S(1)} %get-tuple-element.31.stacked_ref), custom_call_target="tpu_custom_call" | custom-call | flops 905969664 | bytes 4194304 | tf_op jit(solution)/shard_map/forward/pallas_call | solution.py:434
  80.8 0.9 sum.1
  81.7 4.5 %all-to-all-start.2 = ((bf16[8,448,128]{2,1,0:T(8,128)(2,1)}), bf16[8,448,128]{2,1,0:T(8,128)(2,1)S(1)}, u32[]{:S(2)}, u32[]{:S(2)}) async-start(bf16[8,448,128]{2,1,0:T(8,128)(2,1)} %sum.1), calls=%async_computation.2 | async-start | bytes 1835008 | tf_op jit(solution)/shard_map/all_to_all | solution.py:464
  86.2 3.4 %filter_grad.1 = (bf16[512,128]{1,0:T(8,128)(2,1)S(1)}, bf16[512,128]{1,0:T(8,128)(2,1)S(1)}) custom-call(s32[1]{0:T(128)} %bitcast.rank_ref, bf16[8,448,128]{2,1,0:T(8,128)(2,1)S(1)} %all-to-all-done.1.got_ref.mine_ref, bf16[8,256,128]{2,1,0:T(8,128)(2,1)S(1)} %collective-permute-done.3.theirs_ref), custom_call_target="tpu_custom_call" | custom-call | flops 939524096 | bytes 4194304 | tf_op jit(solution)/shard_map/filter_grad/pallas_call | solution.py:455
  89.5 2.8 %collective-permute-start.5 = (bf16[512,128]{1,0:T(8,128)(2,1)S(1)}, bf16[512,128]{1,0:T(8,128)(2,1)S(1)}, u32[]{:S(2)}, u32[]{:S(2)}) collective-permute-start(bf16[512,128]{1,0:T(8,128)(2,1)S(1)} %get-tuple-element.36), channel_id=1, source_target_pairs={{0,2},{1,3},{2,0},{3,1},{4,6},{5,7},{6,4},{7,5},{8,10},{9,11},{10,... | collective-permute-start | bytes 393224 | tf_op jit(solution)/shard_map/ppermute | solution.py:376
  92.3 3.4 %collective-permute-done.5.other_ref = bf16[512,128]{1,0:T(8,128)(2,1)S(1)} collective-permute-done((bf16[512,128]{1,0:T(8,128)(2,1)S(1)}, bf16[512,128]{1,0:T(8,128)(2,1)S(1)}, u32[]{:S(2)}, u32[]{:S(2)}) %collective-permute-start.5) | collective-permute-done | bytes 131104 | tf_op jit(solution)/shard_map/ppermute | solution.py:376
  95.7 3.8 %all-to-all-done.2.got_ref = bf16[8,448,128]{2,1,0:T(8,128)(2,1)S(1)} async-done(((bf16[8,448,128]{2,1,0:T(8,128)(2,1)}), bf16[8,448,128]{2,1,0:T(8,128)(2,1)S(1)}, u32[]{:S(2)}, u32[]{:S(2)}) %all-to-all-start.2) | async-done | bytes 917536 | tf_op jit(solution)/shard_map/all_to_all | solution.py:464
  99.5 0.9 last.1
  100.4 38.5 %all_to_all.26 = bf16[448,4,128]{2,1,0:T(4,128)(2,1)S(1)} all-to-all(bf16[448,4,128]{2,1,0:T(4,128)(2,1)S(1)} %bitcast.29), channel_id=1, replica_groups=mesh['space'=8,'filt'=64] {'filt'}, dimensions={0} | all-to-all | bytes 917504 | tf_op jit(solution)/shard_map/all_to_all | solution.py:473
  138.9 0.9 tail.1
  139.9 3.4 %all-to-all-start.4 = ((f32[8,32,128]{2,1,0:T(8,128)}), f32[8,32,128]{2,1,0:T(8,128)S(1)}, u32[]{:S(2)}, u32[]{:S(2)}) async-start(f32[8,32,128]{2,1,0:T(8,128)} %tail.1), calls=%async_computation.4 | async-start | bytes 262144 | tf_op jit(solution)/shard_map/all_to_all | solution.py:479
  143.3 0.3 copy.18
  143.7 0.1 add_convert_fusion
  143.8 0.1 slice.27
  143.9 0.7 copy.12
  144.6 0.7 copy.14
  145.4 3.4 %all-to-all-done.4 = f32[8,32,128]{2,1,0:T(8,128)S(1)} async-done(((f32[8,32,128]{2,1,0:T(8,128)}), f32[8,32,128]{2,1,0:T(8,128)S(1)}, u32[]{:S(2)}, u32[]{:S(2)}) %all-to-all-start.4) | async-done | bytes 131104 | tf_op jit(solution)/shard_map/all_to_all | solution.py:479
  148.8 1.1 finish.1
  (9 shorter events, 0.3 us)
Async XLA Ops:
  53.6 18.4 %all-to-all-start.1 = ((bf16[8,448,128]{2,1,0:T(8,128)(2,1)}), bf16[8,448,128]{2,1,0:T(8,128)(2,1)S(1)}, u32[]{:S(2)}, u32[]{:S(2)}) async-start(bf16[8,448,128]{2,1,0:T(8,128)(2,1)} %get-tuple-element.24), calls=%async_computation.1 | async-start | bytes 1835008 | tf_op jit(solution)/shard_map/all_to_all | solution.py:410
  57.9 9.3 %collective-permute-start.2 = (bf16[256,128]{1,0:T(8,128)(2,1)S(1)}, bf16[256,128]{1,0:T(8,128)(2,1)S(1)}, u32[]{:S(2)}, u32[]{:S(2)}) collective-permute-start(bf16[256,128]{1,0:T(8,128)(2,1)S(1)} %get-tuple-element.21.own_ref), channel_id=1, source_target_pairs={{0,6},{1,7},{2,4},{3,5},{4,2},{5,3},{6,0},{7,1},{8,14},{9,15},{10,... | collective-permute-start | bytes 196616 | tf_op jit(solution)/shard_map/ppermute | solution.py:376
  61.5 7.9 %collective-permute-start.1 = (bf16[256,128]{1,0:T(8,128)(2,1)S(1)}, bf16[256,128]{1,0:T(8,128)(2,1)S(1)}, u32[]{:S(2)}, u32[]{:S(2)}) collective-permute-start(bf16[256,128]{1,0:T(8,128)(2,1)S(1)} %get-tuple-element.21.own_ref), channel_id=1, source_target_pairs={{0,4},{1,5},{2,6},{3,7},{4,0},{5,1},{6,2},{7,3},{8,12},{9,13},{10,... | collective-permute-start | bytes 196616 | tf_op jit(solution)/shard_map/ppermute | solution.py:376
  64.0 6.9 %collective-permute-start = (bf16[256,128]{1,0:T(8,128)(2,1)S(1)}, bf16[256,128]{1,0:T(8,128)(2,1)S(1)}, u32[]{:S(2)}, u32[]{:S(2)}) collective-permute-start(bf16[256,128]{1,0:T(8,128)(2,1)S(1)} %get-tuple-element.21.own_ref), channel_id=1, source_target_pairs={{0,2},{1,3},{2,0},{3,1},{4,6},{5,7},{6,4},{7,5},{8,10},{9,11},{10,... | collective-permute-start | bytes 196616 | tf_op jit(solution)/shard_map/ppermute | solution.py:376
  72.1 4.4 %collective-permute-start.3 = (bf16[8,256,128]{2,1,0:T(8,128)(2,1)S(1)}, bf16[8,256,128]{2,1,0:T(8,128)(2,1)S(1)}, u32[]{:S(2)}, u32[]{:S(2)}) collective-permute-start(bf16[8,256,128]{2,1,0:T(8,128)(2,1)S(1)} %slice.19), channel_id=1, source_target_pairs={{0,1},{1,0},{2,3},{3,2},{4,5},{5,4},{6,7},{7,6},{8,9},{9,8},{10,11... | collective-permute-start | bytes 1572872 | tf_op jit(solution)/shard_map/ppermute | solution.py:376
  76.5 4.2 %collective-permute-start.4 = (bf16[8,256,128]{2,1,0:T(8,128)(2,1)S(1)}, bf16[8,256,128]{2,1,0:T(8,128)(2,1)S(1)}, u32[]{:S(2)}, u32[]{:S(2)}) collective-permute-start(bf16[8,256,128]{2,1,0:T(8,128)(2,1)S(1)} %get-tuple-element.29), channel_id=1, source_target_pairs={{0,1},{1,0},{2,3},{3,2},{4,5},{5,4},{6,7},{7,6},{8,9},{9,8},{10,11... | collective-permute-start | bytes 1572872 | tf_op jit(solution)/shard_map/ppermute | solution.py:376
  81.7 17.8 %all-to-all-start.2 = ((bf16[8,448,128]{2,1,0:T(8,128)(2,1)}), bf16[8,448,128]{2,1,0:T(8,128)(2,1)S(1)}, u32[]{:S(2)}, u32[]{:S(2)}) async-start(bf16[8,448,128]{2,1,0:T(8,128)(2,1)} %sum.1), calls=%async_computation.2 | async-start | bytes 1835008 | tf_op jit(solution)/shard_map/all_to_all | solution.py:464
  89.5 6.2 %collective-permute-start.5 = (bf16[512,128]{1,0:T(8,128)(2,1)S(1)}, bf16[512,128]{1,0:T(8,128)(2,1)S(1)}, u32[]{:S(2)}, u32[]{:S(2)}) collective-permute-start(bf16[512,128]{1,0:T(8,128)(2,1)S(1)} %get-tuple-element.36), channel_id=1, source_target_pairs={{0,2},{1,3},{2,0},{3,1},{4,6},{5,7},{6,4},{7,5},{8,10},{9,11},{10,... | collective-permute-start | bytes 393224 | tf_op jit(solution)/shard_map/ppermute | solution.py:376
  139.9 8.9 %all-to-all-start.4 = ((f32[8,32,128]{2,1,0:T(8,128)}), f32[8,32,128]{2,1,0:T(8,128)S(1)}, u32[]{:S(2)}, u32[]{:S(2)}) async-start(f32[8,32,128]{2,1,0:T(8,128)} %tail.1), calls=%async_computation.4 | async-start | bytes 262144 | tf_op jit(solution)/shard_map/all_to_all | solution.py:479

commit v6 on v5

--- a/solution.py
+++ b/solution.py
@@ -11,7 +11,6 @@
 F32 = jnp.float32
 BF16 = jnp.bfloat16
 PARAMS = pltpu.CompilerParams(vmem_limit_bytes=16 * 1024 * 1024)
-UNROLL = 4
 
 
 def select_rows(rows, source, columns):
@@ -87,22 +86,26 @@
     return result
 
 
-def first_kernel(slab_ref, scales_ref, cells_ref, rims_ref, weights_ref, out_ref, raw, cells, rims, packed, sems):
+def first_kernel(
+    scales_ref, cells_ref, rims_ref, weights_ref, out_ref, scales, raw, cells, rims, weights, packed, sems
+):
     copies = [
         pltpu.make_async_copy(cells_ref, raw, sems.at[0]),
         pltpu.make_async_copy(rims_ref, rims.at[:, 16:144], sems.at[1]),
+        pltpu.make_async_copy(scales_ref, scales, sems.at[2]),
+        pltpu.make_async_copy(weights_ref, weights, sems.at[3]),
     ]
     for copy in copies:
         copy.start()
     order = select_rows(384, pack_first, 416)
-    own = own_rows(slab_ref[0], weights_ref)
     for n in range(4):
         rims[n, :16] = jnp.zeros((16, 128), BF16)
         rims[n, 144:] = jnp.zeros((16, 128), BF16)
     for copy in copies:
         copy.wait()
     for n in range(4):
-        cells[n] = (raw[n].astype(F32) * scales_ref[0, n]).astype(BF16)
+        cells[n] = (raw[n].astype(F32) * scales[:, n : n + 1]).astype(BF16)
+    own = own_rows(lax.axis_index("space"), weights)
     for block in range(4):
         at = block * 32
         parts = []
@@ -112,9 +115,9 @@
             parts.append(own[core])
         part = slice(block * 384, block * 384 + 384)
         packed[part] = moved(order, jnp.concatenate(parts, axis=0))
-        copies.append(pltpu.make_async_copy(packed.at[part], out_ref.at[part], sems.at[2 + block]))
+        copies.append(pltpu.make_async_copy(packed.at[part], out_ref.at[part], sems.at[4 + block]))
         copies[-1].start()
-    for copy in copies[2:]:
+    for copy in copies[4:]:
         copy.wait()
 
 
@@ -180,7 +183,7 @@
         planes[z + 1] = plane_of(mine_ref, theirs_ref, z)
     column = lax.broadcasted_iota(jnp.int32, (32, 128), 1)
 
-    def plane(z, _):
+    def plane(z):
         near = jnp.concatenate([planes[z], planes[z + 1], planes[z + 2]], axis=0)
         terms = jnp.dot(stacked_ref[...], near, preferred_element_type=F32)
         for row in range(6):
@@ -197,13 +200,11 @@
             left = jnp.where(column >= 1, pltpu.roll(sums[0], 1, 1), 0.0)
             right = jnp.where(column <= 126, pltpu.roll(sums[2], 127, 1), 0.0)
             rows[z, row * 32 : row * 32 + 32] = (sums[1] + left + right).astype(BF16)
-        return 0
 
     copies = []
-    for half in range(2):
-        lax.fori_loop(half * 4, half * 4 + 4, plane, 0, unroll=UNROLL)
-        part = slice(half * 4, half * 4 + 4)
-        copies.append(pltpu.make_async_copy(rows.at[part], out_ref.at[part, 256:448], sems.at[half]))
+    for z in range(8):
+        plane(z)
+        copies.append(pltpu.make_async_copy(rows.at[z], out_ref.at[z, 256:448], sems.at[z]))
         copies[-1].start()
     for copy in copies:
         copy.wait()
@@ -222,37 +223,31 @@
     shifted[0] = jnp.zeros((96, 768), BF16)
     shifted[9] = jnp.zeros((96, 768), BF16)
 
-    def plane(z, _):
+    for z in range(8):
         rows = got_ref[z, 256:448]
         for e, cells in ((0, moved(rows, before)), (1, rows), (2, moved(rows, after))):
             for y in range(6):
                 shifted[z + 1, e * 32 : e * 32 + 32, y * 128 : y * 128 + 128] = cells[y * 32 : y * 32 + 32]
-        return 0
-
-    lax.fori_loop(0, 8, plane, 0, unroll=UNROLL)
-
-
-def backward_kernel(got_ref, filter_ref, keep_ref, send_ref, shifted, image):
+
+
+def backward_kernel(got_ref, filter_ref, keep_ref, send_ref, shifted, images):
     shift(got_ref, shifted)
-    image[864:896] = jnp.zeros((32, 512), BF16)
-
-    def plane(z, _):
+    images[:, 864:896] = jnp.zeros((2, 32, 512), BF16)
+    for z in range(8):
+        image = images.at[z % 2]
         fill_image(image, shifted, z)
         grad = jnp.dot(filter_ref[...], image[...], preferred_element_type=F32)
         for y in range(4):
             keep_ref[z, y * 64 : y * 64 + 64] = grad[:64, y * 128 : y * 128 + 128]
             send_ref[z, y * 64 : y * 64 + 64] = grad[64:, y * 128 : y * 128 + 128].astype(BF16)
-        return 0
-
-    lax.fori_loop(0, 8, plane, 0, unroll=UNROLL)
 
 
 def sum_kernel(keep_ref, other_ref, out_ref, result_ref, rows_ref, sems):
     copies = []
-    for half in range(2):
-        part = slice(half * 4, half * 4 + 4)
+    for n in range(4):
+        part = slice(n * 2, n * 2 + 2)
         rows_ref[part] = (keep_ref[part] + other_ref[part].astype(F32)).astype(BF16)
-        copies.append(pltpu.make_async_copy(rows_ref.at[part], result_ref.at[part, 0:256], sems.at[half]))
+        copies.append(pltpu.make_async_copy(rows_ref.at[part], result_ref.at[part, 0:256], sems.at[n]))
         copies[-1].start()
     for copy in copies:
         copy.wait()
@@ -311,8 +306,6 @@
 
 
 def finish_kernel(parts_ref, out_ref, by_tap):
-    row = lax.broadcasted_iota(jnp.int32, (256, 128), 0)
-    lane = lax.broadcasted_iota(jnp.int32, (256, 128), 1)
     low = lax.broadcasted_iota(jnp.int32, (8, 128), 1) < 64
     norm = 1.0 / math.sqrt(131072)
     rows = []
@@ -321,10 +314,18 @@
             for y in range(4):
                 rows.append(jnp.concatenate([parts_ref[2 * y + x, 2 * c + k] for k in range(2)], axis=1))
     rows = jnp.concatenate(rows, axis=0) * norm
+    high = rows.astype(BF16)
+    rest = rows - high.astype(F32)
+    middle = rest.astype(BF16)
+    low_bits = (rest - middle.astype(F32)).astype(BF16)
+    row = lax.broadcasted_iota(jnp.int32, (256, 256), 0)
+    lane = lax.broadcasted_iota(jnp.int32, (256, 256), 1)
+    source = ((lane >> 1) & 1) * 128 + (lane >> 6) * 32 + ((lane >> 2) & 15) * 2 + (lane & 1)
+    spread = jnp.where(source == row, 1.0, 0.0).astype(BF16)
+    terms = jnp.dot(jnp.concatenate([high, middle, low_bits], axis=0), spread, preferred_element_type=F32)
+    both = terms[:128] + (terms[128:256] + terms[256:])
     for pair in range(2):
-        source = ((lane >> 1) & 1) * 128 + (2 * pair + (lane >> 6)) * 32 + ((lane >> 2) & 15) * 2 + (lane & 1)
-        spread = jnp.where(source == row, 1.0, 0.0).astype(F32)
-        wide = jnp.dot(rows, spread, preferred_element_type=F32, precision=lax.Precision.HIGHEST)
+        wide = both[:, pair * 128 : pair * 128 + 128]
         for channel in range(4):
             for half in range(2):
                 at = (channel * 4 + half * 2) * 8
@@ -378,19 +379,25 @@
 
 def local(quantized, scales, weights, cotangent):
     rank = lax.axis_index("filt").reshape(1).astype(jnp.int32)
-    slab = lax.axis_index("space").reshape(1).astype(jnp.int32)
 
     (both,) = call(
         first_kernel,
         "first",
-        [SCALAR, SCALAR, HBM, HBM, whole(27, 4, 256)],
+        [HBM] * 4,
         [((1536, 128), BF16)],
-        [((4, 128, 128), BF16), ((4, 128, 128), BF16), ((4, 160, 128), BF16), ((1536, 128), BF16), DMA((6,))],
+        [
+            ((1, 4), F32),
+            ((4, 128, 128), BF16),
+            ((4, 128, 128), BF16),
+            ((4, 160, 128), BF16),
+            ((27, 4, 256), BF16),
+            ((1536, 128), BF16),
+            DMA((8,)),
+        ],
         2 * 4 * 384 * 416 * 128,
         [HBM],
         mib=56,
     )(
-        slab,
         scales.reshape(1, 4),
         quantized.reshape(4, 128, 128),
         cotangent.reshape(4, 128, 128),
@@ -425,7 +432,7 @@
         "backward",
         [whole(8, 448, 128), whole(128, 896)],
         [((8, 256, 128), F32), ((8, 256, 128), BF16)],
-        [((10, 96, 768), BF16), ((896, 512), BF16)],
+        [((10, 96, 768), BF16), ((2, 896, 512), BF16)],
         2 * 8 * 896 * 128 * 512,
     )(got, filters)
     send, theirs = lax.optimization_barrier((send, theirs))
@@ -436,7 +443,7 @@
         "forward",
         [cells, whole(8, 256, 128), whole(288, 384)],
         [((8, 448, 128), BF16)],
-        [((10, 128, 512), BF16), ((8, 192, 128), BF16), DMA((2,))],
+        [((10, 128, 512), BF16), ((8, 192, 128), BF16), DMA((8,))],
         2 * 8 * 288 * 384 * 512,
         [ANY],
     )(got, theirs, stacked)
@@ -445,7 +452,7 @@
         "sum",
         [whole(8, 256, 128), whole(8, 256, 128), ANY],
         [((8, 448, 128), BF16)],
-        [((8, 256, 128), BF16), DMA((2,))],
+        [((8, 256, 128), BF16), DMA((4,))],
         8 * 256 * 128,
         [ANY],
         {2: 0},

time: 151 us -> 150 us (level)
  no operation moved by 1% of the time
where the time goes in v6:
time: 150 us; the launch traced here: 149 us
  blocking collectives  86.2 us (57%)
  starting transfers between devices  28.8 us (19%)
  waiting for transfers between devices  16 us (11%)
  Pallas kernels  15.1 us (10%)
  local copies, waits for them, and re-layouts  2.04 us (1%)
    all_to_all x1, blocking collectives, local(): got = lax.all_to_all(both.reshape(64, 24, 128), 'filt', 0, 0, tiled=True)  48.4 us
    all_to_all x1, blocking collectives, local(): got = lax.all_to_all(both.reshape(448, 4, 128), 'filt', 0, 0, tiled=True)  37.8 us
    ppermute x6, starting transfers between devices, swapped(): return lax.ppermute(array, axis, [(n, n ^ bit) for n in range(count)])  16.6 us
    all_to_all x2, starting transfers between devices, local(): got = lax.all_to_all(both, 'space', 0, 0, tiled=True)  8.82 us
    ppermute x6, waiting for transfers between devices, swapped(): return lax.ppermute(array, axis, [(n, n ^ bit) for n in range(count)])  7.48 us
    all_to_all x2, waiting for transfers between devices, local(): got = lax.all_to_all(both, 'space', 0, 0, tiled=True)  5.08 us
    all_to_all x1, waiting for transfers between devices, local(): lax.all_to_all(terms, 'space', 0, 0, tiled=True).reshape(8, 4, 8, 128)  3.43 us
    all_to_all x1, starting transfers between devices, local(): lax.all_to_all(terms, 'space', 0, 0, tiled=True).reshape(8, 4, 8, 128)  3.38 us
  transfers between devices with their start and end apart: 9, of which 6 were waited for; matrix products, arithmetic and copies ran while one was open for 1% of the time, Pallas kernels for 5%

profile of v6, /device:TPU:1, one launch (start us, length us, event | category | flops | bytes accessed | tf_op | source)
XLA Modules:
  0.0 149.1 jit_solution(3005510010213956361)
XLA Ops:
  0.6 2.7 %first.1 = bf16[1536,128]{1,0:T(8,128)(2,1)} custom-call(f32[1,4]{1,0:T(1,128)} %bitcast.41, bf16[4,128,128]{2,1,0:T(8,128)(2,1)} %bitcast.35, bf16[4,128,128]{2,1,0:T(8,128)(2,1)} %bitcast.36, bf16[27,4,256]{2,1,0:T(4,128)(2,1)} %bitcast.40), custom_call_target="tpu_custom_call" | custom-call | flops 163577856 | bytes 4194304 | tf_op jit(solution)/shard_map/first/pallas_call | solution.py:383
  3.3 48.4 %all_to_all.25 = bf16[64,24,128]{2,1,0:T(8,128)(2,1)S(1)} all-to-all(bf16[64,24,128]{2,1,0:T(8,128)(2,1)} %bitcast.32), channel_id=1, replica_groups=mesh['space'=8,'filt'=64] {'filt'}, dimensions={0} | all-to-all | bytes 786432 | tf_op jit(solution)/shard_map/all_to_all | solution.py:406
  51.7 1.5 middle.1
  53.2 4.2 %all-to-all-start.1 = ((bf16[8,448,128]{2,1,0:T(8,128)(2,1)}), bf16[8,448,128]{2,1,0:T(8,128)(2,1)S(1)}, u32[]{:S(2)}, u32[]{:S(2)}) async-start(bf16[8,448,128]{2,1,0:T(8,128)(2,1)} %get-tuple-element.24), calls=%async_computation.1 | async-start | bytes 1835008 | tf_op jit(solution)/shard_map/all_to_all | solution.py:417
  57.4 3.7 %collective-permute-start.2 = (bf16[256,128]{1,0:T(8,128)(2,1)S(1)}, bf16[256,128]{1,0:T(8,128)(2,1)S(1)}, u32[]{:S(2)}, u32[]{:S(2)}) collective-permute-start(bf16[256,128]{1,0:T(8,128)(2,1)S(1)} %get-tuple-element.21.own_ref), channel_id=1, source_target_pairs={{0,6},{1,7},{2,4},{3,5},{4,2},{5,3},{6,0},{7,1},{8,14},{9,15},{10,... | collective-permute-start | bytes 196616 | tf_op jit(solution)/shard_map/ppermute | solution.py:377
  61.1 2.5 %collective-permute-start.1 = (bf16[256,128]{1,0:T(8,128)(2,1)S(1)}, bf16[256,128]{1,0:T(8,128)(2,1)S(1)}, u32[]{:S(2)}, u32[]{:S(2)}) collective-permute-start(bf16[256,128]{1,0:T(8,128)(2,1)S(1)} %get-tuple-element.21.own_ref), channel_id=1, source_target_pairs={{0,4},{1,5},{2,6},{3,7},{4,0},{5,1},{6,2},{7,3},{8,12},{9,13},{10,... | collective-permute-start | bytes 196616 | tf_op jit(solution)/shard_map/ppermute | solution.py:377
  63.6 3.1 %collective-permute-start = (bf16[256,128]{1,0:T(8,128)(2,1)S(1)}, bf16[256,128]{1,0:T(8,128)(2,1)S(1)}, u32[]{:S(2)}, u32[]{:S(2)}) collective-permute-start(bf16[256,128]{1,0:T(8,128)(2,1)S(1)} %get-tuple-element.21.own_ref), channel_id=1, source_target_pairs={{0,2},{1,3},{2,0},{3,1},{4,6},{5,7},{6,4},{7,5},{8,10},{9,11},{10,... | collective-permute-start | bytes 196616 | tf_op jit(solution)/shard_map/ppermute | solution.py:377
  66.7 2.3 %collective-permute-done.1.second_ref = bf16[256,128]{1,0:T(8,128)(2,1)S(1)} collective-permute-done((bf16[256,128]{1,0:T(8,128)(2,1)S(1)}, bf16[256,128]{1,0:T(8,128)(2,1)S(1)}, u32[]{:S(2)}, u32[]{:S(2)}) %collective-permute-start.1) | collective-permute-done | bytes 65568 | tf_op jit(solution)/shard_map/ppermute | solution.py:377
  69.0 1.4 collective-permute-done.first_ref
  70.4 0.5 filters.1
  70.9 0.7 all-to-all-done.1.got_ref.mine_ref
  71.6 2.3 %collective-permute-start.3 = (bf16[8,256,128]{2,1,0:T(8,128)(2,1)S(1)}, bf16[8,256,128]{2,1,0:T(8,128)(2,1)S(1)}, u32[]{:S(2)}, u32[]{:S(2)}) collective-permute-start(bf16[8,256,128]{2,1,0:T(8,128)(2,1)S(1)} %slice.19), channel_id=1, source_target_pairs={{0,1},{1,0},{2,3},{3,2},{4,5},{5,4},{6,7},{7,6},{8,9},{9,8},{10,11... | collective-permute-start | bytes 1572872 | tf_op jit(solution)/shard_map/ppermute | solution.py:377
  73.9 1.5 %backward.1 = (f32[8,256,128]{2,1,0:T(8,128)S(1)}, bf16[8,256,128]{2,1,0:T(8,128)(2,1)S(1)}) custom-call(bf16[8,448,128]{2,1,0:T(8,128)(2,1)S(1)} %all-to-all-done.1.got_ref.mine_ref, bf16[128,896]{1,0:T(8,128)(2,1)S(1)} %get-tuple-element.26.filter_ref), custom_call_target="tpu_custom_call" | custom-call | flops 939524096 | bytes 4194304 | tf_op jit(solution)/shard_map/backward/pallas_call | solution.py:430
  75.5 2.3 %collective-permute-start.4 = (bf16[8,256,128]{2,1,0:T(8,128)(2,1)S(1)}, bf16[8,256,128]{2,1,0:T(8,128)(2,1)S(1)}, u32[]{:S(2)}, u32[]{:S(2)}) collective-permute-start(bf16[8,256,128]{2,1,0:T(8,128)(2,1)S(1)} %get-tuple-element.29), channel_id=1, source_target_pairs={{0,1},{1,0},{2,3},{3,2},{4,5},{5,4},{6,7},{7,6},{8,9},{9,8},{10,11... | collective-permute-start | bytes 1572872 | tf_op jit(solution)/shard_map/ppermute | solution.py:377
  77.7 2.2 %forward.1.out_ref = bf16[8,448,128]{2,1,0:T(8,128)(2,1)} custom-call(bf16[8,448,128]{2,1,0:T(8,128)(2,1)S(1)} %all-to-all-done.1.got_ref.mine_ref, bf16[8,256,128]{2,1,0:T(8,128)(2,1)S(1)} %collective-permute-done.3.theirs_ref, bf16[288,384]{1,0:T(8,128)(2,1)S(1)} %get-tuple-element.31.stacked_ref), custom_call_target="tpu_custom_call" | custom-call | flops 905969664 | bytes 4194304 | tf_op jit(solution)/shard_map/forward/pallas_call | solution.py:441
  79.9 0.9 sum.1
  80.8 4.6 %all-to-all-start.2 = ((bf16[8,448,128]{2,1,0:T(8,128)(2,1)}), bf16[8,448,128]{2,1,0:T(8,128)(2,1)S(1)}, u32[]{:S(2)}, u32[]{:S(2)}) async-start(bf16[8,448,128]{2,1,0:T(8,128)(2,1)} %sum.1), calls=%async_computation.2 | async-start | bytes 1835008 | tf_op jit(solution)/shard_map/all_to_all | solution.py:471
  85.4 3.1 %filter_grad.1 = (bf16[512,128]{1,0:T(8,128)(2,1)S(1)}, bf16[512,128]{1,0:T(8,128)(2,1)S(1)}) custom-call(s32[1]{0:T(128)} %bitcast.rank_ref, bf16[8,448,128]{2,1,0:T(8,128)(2,1)S(1)} %all-to-all-done.1.got_ref.mine_ref, bf16[8,256,128]{2,1,0:T(8,128)(2,1)S(1)} %collective-permute-done.3.theirs_ref), custom_call_target="tpu_custom_call" | custom-call | flops 939524096 | bytes 4194304 | tf_op jit(solution)/shard_map/filter_grad/pallas_call | solution.py:462
  88.5 2.8 %collective-permute-start.5 = (bf16[512,128]{1,0:T(8,128)(2,1)S(1)}, bf16[512,128]{1,0:T(8,128)(2,1)S(1)}, u32[]{:S(2)}, u32[]{:S(2)}) collective-permute-start(bf16[512,128]{1,0:T(8,128)(2,1)S(1)} %get-tuple-element.36), channel_id=1, source_target_pairs={{0,2},{1,3},{2,0},{3,1},{4,6},{5,7},{6,4},{7,5},{8,10},{9,11},{10,... | collective-permute-start | bytes 393224 | tf_op jit(solution)/shard_map/ppermute | solution.py:377
  91.3 3.7 %collective-permute-done.5.other_ref = bf16[512,128]{1,0:T(8,128)(2,1)S(1)} collective-permute-done((bf16[512,128]{1,0:T(8,128)(2,1)S(1)}, bf16[512,128]{1,0:T(8,128)(2,1)S(1)}, u32[]{:S(2)}, u32[]{:S(2)}) %collective-permute-start.5) | collective-permute-done | bytes 131104 | tf_op jit(solution)/shard_map/ppermute | solution.py:377
  95.0 4.4 %all-to-all-done.2.got_ref = bf16[8,448,128]{2,1,0:T(8,128)(2,1)S(1)} async-done(((bf16[8,448,128]{2,1,0:T(8,128)(2,1)}), bf16[8,448,128]{2,1,0:T(8,128)(2,1)S(1)}, u32[]{:S(2)}, u32[]{:S(2)}) %all-to-all-start.2) | async-done | bytes 917536 | tf_op jit(solution)/shard_map/all_to_all | solution.py:471
  99.4 0.9 last.1
  100.3 37.8 %all_to_all.26 = bf16[448,4,128]{2,1,0:T(4,128)(2,1)S(1)} all-to-all(bf16[448,4,128]{2,1,0:T(4,128)(2,1)S(1)} %bitcast.28), channel_id=1, replica_groups=mesh['space'=8,'filt'=64] {'filt'}, dimensions={0} | all-to-all | bytes 917504 | tf_op jit(solution)/shard_map/all_to_all | solution.py:480
  138.2 0.9 tail.1
  139.2 3.4 %all-to-all-start.4 = ((f32[8,32,128]{2,1,0:T(8,128)}), f32[8,32,128]{2,1,0:T(8,128)S(1)}, u32[]{:S(2)}, u32[]{:S(2)}) async-start(f32[8,32,128]{2,1,0:T(8,128)} %tail.1), calls=%async_computation.4 | async-start | bytes 262144 | tf_op jit(solution)/shard_map/all_to_all | solution.py:486
  142.6 0.3 copy.18
  143.0 0.1 add_convert_fusion
  143.1 0.1 slice.27
  143.2 0.7 copy.12
  143.9 0.7 copy.14
  144.6 3.4 %all-to-all-done.4 = f32[8,32,128]{2,1,0:T(8,128)S(1)} async-done(((f32[8,32,128]{2,1,0:T(8,128)}), f32[8,32,128]{2,1,0:T(8,128)S(1)}, u32[]{:S(2)}, u32[]{:S(2)}) %all-to-all-start.4) | async-done | bytes 131104 | tf_op jit(solution)/shard_map/all_to_all | solution.py:486
  148.1 1.0 finish.1
  (9 shorter events, 0.3 us)
Async XLA Ops:
  53.2 18.4 %all-to-all-start.1 = ((bf16[8,448,128]{2,1,0:T(8,128)(2,1)}), bf16[8,448,128]{2,1,0:T(8,128)(2,1)S(1)}, u32[]{:S(2)}, u32[]{:S(2)}) async-start(bf16[8,448,128]{2,1,0:T(8,128)(2,1)} %get-tuple-element.24), calls=%async_computation.1 | async-start | bytes 1835008 | tf_op jit(solution)/shard_map/all_to_all | solution.py:417
  57.4 9.3 %collective-permute-start.2 = (bf16[256,128]{1,0:T(8,128)(2,1)S(1)}, bf16[256,128]{1,0:T(8,128)(2,1)S(1)}, u32[]{:S(2)}, u32[]{:S(2)}) collective-permute-start(bf16[256,128]{1,0:T(8,128)(2,1)S(1)} %get-tuple-element.21.own_ref), channel_id=1, source_target_pairs={{0,6},{1,7},{2,4},{3,5},{4,2},{5,3},{6,0},{7,1},{8,14},{9,15},{10,... | collective-permute-start | bytes 196616 | tf_op jit(solution)/shard_map/ppermute | solution.py:377
  61.1 7.9 %collective-permute-start.1 = (bf16[256,128]{1,0:T(8,128)(2,1)S(1)}, bf16[256,128]{1,0:T(8,128)(2,1)S(1)}, u32[]{:S(2)}, u32[]{:S(2)}) collective-permute-start(bf16[256,128]{1,0:T(8,128)(2,1)S(1)} %get-tuple-element.21.own_ref), channel_id=1, source_target_pairs={{0,4},{1,5},{2,6},{3,7},{4,0},{5,1},{6,2},{7,3},{8,12},{9,13},{10,... | collective-permute-start | bytes 196616 | tf_op jit(solution)/shard_map/ppermute | solution.py:377
  63.6 6.9 %collective-permute-start = (bf16[256,128]{1,0:T(8,128)(2,1)S(1)}, bf16[256,128]{1,0:T(8,128)(2,1)S(1)}, u32[]{:S(2)}, u32[]{:S(2)}) collective-permute-start(bf16[256,128]{1,0:T(8,128)(2,1)S(1)} %get-tuple-element.21.own_ref), channel_id=1, source_target_pairs={{0,2},{1,3},{2,0},{3,1},{4,6},{5,7},{6,4},{7,5},{8,10},{9,11},{10,... | collective-permute-start | bytes 196616 | tf_op jit(solution)/shard_map/ppermute | solution.py:377
  71.6 3.8 %collective-permute-start.3 = (bf16[8,256,128]{2,1,0:T(8,128)(2,1)S(1)}, bf16[8,256,128]{2,1,0:T(8,128)(2,1)S(1)}, u32[]{:S(2)}, u32[]{:S(2)}) collective-permute-start(bf16[8,256,128]{2,1,0:T(8,128)(2,1)S(1)} %slice.19), channel_id=1, source_target_pairs={{0,1},{1,0},{2,3},{3,2},{4,5},{5,4},{6,7},{7,6},{8,9},{9,8},{10,11... | collective-permute-start | bytes 1572872 | tf_op jit(solution)/shard_map/ppermute | solution.py:377
  75.5 4.4 %collective-permute-start.4 = (bf16[8,256,128]{2,1,0:T(8,128)(2,1)S(1)}, bf16[8,256,128]{2,1,0:T(8,128)(2,1)S(1)}, u32[]{:S(2)}, u32[]{:S(2)}) collective-permute-start(bf16[8,256,128]{2,1,0:T(8,128)(2,1)S(1)} %get-tuple-element.29), channel_id=1, source_target_pairs={{0,1},{1,0},{2,3},{3,2},{4,5},{5,4},{6,7},{7,6},{8,9},{9,8},{10,11... | collective-permute-start | bytes 1572872 | tf_op jit(solution)/shard_map/ppermute | solution.py:377
  80.8 18.6 %all-to-all-start.2 = ((bf16[8,448,128]{2,1,0:T(8,128)(2,1)}), bf16[8,448,128]{2,1,0:T(8,128)(2,1)S(1)}, u32[]{:S(2)}, u32[]{:S(2)}) async-start(bf16[8,448,128]{2,1,0:T(8,128)(2,1)} %sum.1), calls=%async_computation.2 | async-start | bytes 1835008 | tf_op jit(solution)/shard_map/all_to_all | solution.py:471
  88.5 6.5 %collective-permute-start.5 = (bf16[512,128]{1,0:T(8,128)(2,1)S(1)}, bf16[512,128]{1,0:T(8,128)(2,1)S(1)}, u32[]{:S(2)}, u32[]{:S(2)}) collective-permute-start(bf16[512,128]{1,0:T(8,128)(2,1)S(1)} %get-tuple-element.36), channel_id=1, source_target_pairs={{0,2},{1,3},{2,0},{3,1},{4,6},{5,7},{6,4},{7,5},{8,10},{9,11},{10,... | collective-permute-start | bytes 393224 | tf_op jit(solution)/shard_map/ppermute | solution.py:377
  139.2 8.9 %all-to-all-start.4 = ((f32[8,32,128]{2,1,0:T(8,128)}), f32[8,32,128]{2,1,0:T(8,128)S(1)}, u32[]{:S(2)}, u32[]{:S(2)}) async-start(f32[8,32,128]{2,1,0:T(8,128)} %tail.1), calls=%async_computation.4 | async-start | bytes 262144 | tf_op jit(solution)/shard_map/all_to_all | solution.py:486

commit v7 on v6

--- a/solution.py
+++ b/solution.py
@@ -122,23 +122,26 @@
 
 
 def middle_kernel(got_ref, out_ref, corners_ref, cells, rims, sems):
-    order = select_rows(384, message_row, 384)
     copies = []
+    order = select_rows(128, message_row, 384)
     for block in range(4):
         rows = moved(order, got_ref[block * 384 : block * 384 + 384])
         for i in range(2):
             for y in range(4):
                 piece = rows[i * 64 + y * 16 : i * 64 + y * 16 + 16]
                 cells[i, y * 64 + block * 16 : y * 64 + block * 16 + 16] = piece
-        rims[block] = rows[128:320]
+    for to in range(8):
+        copies.append(pltpu.make_async_copy(cells.at[to % 2], out_ref.at[to, 0:256], sems.at[8 + to]))
+        copies[-1].start()
+    order = select_rows(256, lambda n: message_row(n + 128), 384)
+    for block in range(4):
+        rows = moved(order, got_ref[block * 384 : block * 384 + 384])
+        rims[block] = rows[:192]
         for i in range(2):
             to = 2 * block + i
             copies.append(pltpu.make_async_copy(rims.at[block], out_ref.at[to, 256:448], sems.at[to]))
             copies[-1].start()
-        corners_ref[block * 64 : block * 64 + 64] = rows[320:384]
-    for to in range(8):
-        copies.append(pltpu.make_async_copy(cells.at[to % 2], out_ref.at[to, 0:256], sems.at[8 + to]))
-        copies[-1].start()
+        corners_ref[block * 64 : block * 64 + 64] = rows[192:]
     for copy in copies:
         copy.wait()
 
@@ -176,7 +179,7 @@
     return jnp.concatenate(halves, axis=0)
 
 
-def forward_kernel(mine_ref, theirs_ref, stacked_ref, out_ref, planes, rows, sems):
+def forward_kernel(mine_ref, theirs_ref, stacked_ref, out_ref, planes):
     planes[0] = jnp.zeros((128, 512), BF16)
     planes[9] = jnp.zeros((128, 512), BF16)
     for z in range(8):
@@ -199,15 +202,10 @@
                 sums.append(total)
             left = jnp.where(column >= 1, pltpu.roll(sums[0], 1, 1), 0.0)
             right = jnp.where(column <= 126, pltpu.roll(sums[2], 127, 1), 0.0)
-            rows[z, row * 32 : row * 32 + 32] = (sums[1] + left + right).astype(BF16)
-
-    copies = []
+            out_ref[z, row * 32 : row * 32 + 32] = (sums[1] + left + right).astype(BF16)
+
     for z in range(8):
         plane(z)
-        copies.append(pltpu.make_async_copy(rows.at[z], out_ref.at[z, 256:448], sems.at[z]))
-        copies[-1].start()
-    for copy in copies:
-        copy.wait()
 
 
 def fill_image(image, shifted, z):
@@ -242,12 +240,13 @@
             send_ref[z, y * 64 : y * 64 + 64] = grad[64:, y * 128 : y * 128 + 128].astype(BF16)
 
 
-def sum_kernel(keep_ref, other_ref, out_ref, result_ref, rows_ref, sems):
-    copies = []
+def sum_kernel(keep_ref, other_ref, rims_ref, out_ref, rows_ref, sems):
+    copies = [pltpu.make_async_copy(rims_ref, out_ref.at[:, 256:448], sems.at[4])]
+    copies[0].start()
     for n in range(4):
         part = slice(n * 2, n * 2 + 2)
         rows_ref[part] = (keep_ref[part] + other_ref[part].astype(F32)).astype(BF16)
-        copies.append(pltpu.make_async_copy(rows_ref.at[part], result_ref.at[part, 0:256], sems.at[n]))
+        copies.append(pltpu.make_async_copy(rows_ref.at[part], out_ref.at[part, 0:256], sems.at[n]))
         copies[-1].start()
     for copy in copies:
         copy.wait()
@@ -352,12 +351,11 @@
 
 
 SCALAR = pl.BlockSpec(memory_space=pltpu.SMEM)
-ANY = pl.BlockSpec(memory_space=pl.ANY)
 HBM = pl.BlockSpec(memory_space=pltpu.HBM)
 DMA = pltpu.SemaphoreType.DMA
 
 
-def call(kernel, name, ins, outs, scratch, flops, out_specs=None, aliases={}, mib=16):
+def call(kernel, name, ins, outs, scratch, flops, out_specs=None, mib=16):
     return pl.pallas_call(
         kernel,
         grid=(1,),
@@ -365,7 +363,6 @@
         out_shape=[jax.ShapeDtypeStruct(shape, dtype) for shape, dtype in outs],
         out_specs=out_specs or [whole(*shape) for shape, _ in outs],
         scratch_shapes=[pltpu.VMEM(*s) if isinstance(s, tuple) else s for s in scratch],
-        input_output_aliases=aliases,
         compiler_params=pltpu.CompilerParams(vmem_limit_bytes=mib * 1024 * 1024),
         cost_estimate=pl.CostEstimate(flops=flops, bytes_accessed=4 << 20, transcendentals=0),
         name=name,
@@ -442,20 +439,18 @@
         forward_kernel,
         "forward",
         [cells, whole(8, 256, 128), whole(288, 384)],
-        [((8, 448, 128), BF16)],
-        [((10, 128, 512), BF16), ((8, 192, 128), BF16), DMA((8,))],
+        [((8, 192, 128), BF16)],
+        [((10, 128, 512), BF16)],
         2 * 8 * 288 * 384 * 512,
-        [ANY],
     )(got, theirs, stacked)
     (both,) = call(
         sum_kernel,
         "sum",
-        [whole(8, 256, 128), whole(8, 256, 128), ANY],
+        [whole(8, 256, 128), whole(8, 256, 128), whole(8, 192, 128)],
         [((8, 448, 128), BF16)],
-        [((8, 256, 128), BF16), DMA((4,))],
+        [((8, 256, 128), BF16), DMA((5,))],
         8 * 256 * 128,
-        [ANY],
-        {2: 0},
+        [HBM],
     )(keep, other, out)
     both, cells, theirs = lax.optimization_barrier((both, got, theirs))
 

time: 150 us -> 149 us (level)
  transfers between devices with their start and end apart: 9 -> 9, of which waited for: 6 -> 7; matrix products, arithmetic and copies ran while one was open for 1% -> 1% of each run, Pallas kernels for 5% -> 4%
where the time goes in v7:
time: 149 us; the launch traced here: 148 us
  blocking collectives  86.4 us (58%)
  starting transfers between devices  28.8 us (19%)
  waiting for transfers between devices  15.8 us (11%)
  Pallas kernels  14.4 us (10%)
  local copies, waits for them, and re-layouts  2.04 us (1%)
    all_to_all x1, blocking collectives, local(): got = lax.all_to_all(both.reshape(64, 24, 128), 'filt', 0, 0, tiled=True)  48.4 us
    all_to_all x1, blocking collectives, local(): got = lax.all_to_all(both.reshape(448, 4, 128), 'filt', 0, 0, tiled=True)  38.1 us
    ppermute x6, starting transfers between devices, swapped(): return lax.ppermute(array, axis, [(n, n ^ bit) for n in range(count)])  16.6 us
    all_to_all x2, starting transfers between devices, local(): got = lax.all_to_all(both, 'space', 0, 0, tiled=True)  8.82 us
    ppermute x6, waiting for transfers between devices, swapped(): return lax.ppermute(array, axis, [(n, n ^ bit) for n in range(count)])  7.3 us
    all_to_all x2, waiting for transfers between devices, local(): got = lax.all_to_all(both, 'space', 0, 0, tiled=True)  5.08 us
    all_to_all x1, waiting for transfers between devices, local(): lax.all_to_all(terms, 'space', 0, 0, tiled=True).reshape(8, 4, 8, 128)  3.43 us
    all_to_all x1, starting transfers between devices, local(): lax.all_to_all(terms, 'space', 0, 0, tiled=True).reshape(8, 4, 8, 128)  3.38 us
  transfers between devices with their start and end apart: 9, of which 7 were waited for; matrix products, arithmetic and copies ran while one was open for 1% of the time, Pallas kernels for 4%

profile of v7, /device:TPU:1, one launch (start us, length us, event | category | flops | bytes accessed | tf_op | source)
XLA Modules:
  0.0 148.4 jit_solution(17223776147831599532)
XLA Ops:
  0.6 2.7 %first.1 = bf16[1536,128]{1,0:T(8,128)(2,1)} custom-call(f32[1,4]{1,0:T(1,128)} %bitcast.41, bf16[4,128,128]{2,1,0:T(8,128)(2,1)} %bitcast.35, bf16[4,128,128]{2,1,0:T(8,128)(2,1)} %bitcast.36, bf16[27,4,256]{2,1,0:T(4,128)(2,1)} %bitcast.40), custom_call_target="tpu_custom_call" | custom-call | flops 163577856 | bytes 4194304 | tf_op jit(solution)/shard_map/first/pallas_call | solution.py:380
  3.3 48.4 %all_to_all.25 = bf16[64,24,128]{2,1,0:T(8,128)(2,1)S(1)} all-to-all(bf16[64,24,128]{2,1,0:T(8,128)(2,1)} %bitcast.32), channel_id=1, replica_groups=mesh['space'=8,'filt'=64] {'filt'}, dimensions={0} | all-to-all | bytes 786432 | tf_op jit(solution)/shard_map/all_to_all | solution.py:403
  51.7 1.4 middle.1
  53.1 4.2 %all-to-all-start.1 = ((bf16[8,448,128]{2,1,0:T(8,128)(2,1)}), bf16[8,448,128]{2,1,0:T(8,128)(2,1)S(1)}, u32[]{:S(2)}, u32[]{:S(2)}) async-start(bf16[8,448,128]{2,1,0:T(8,128)(2,1)} %get-tuple-element.24), calls=%async_computation.1 | async-start | bytes 1835008 | tf_op jit(solution)/shard_map/all_to_all | solution.py:414
  57.3 3.7 %collective-permute-start.2 = (bf16[256,128]{1,0:T(8,128)(2,1)S(1)}, bf16[256,128]{1,0:T(8,128)(2,1)S(1)}, u32[]{:S(2)}, u32[]{:S(2)}) collective-permute-start(bf16[256,128]{1,0:T(8,128)(2,1)S(1)} %get-tuple-element.21.own_ref), channel_id=1, source_target_pairs={{0,6},{1,7},{2,4},{3,5},{4,2},{5,3},{6,0},{7,1},{8,14},{9,15},{10,... | collective-permute-start | bytes 196616 | tf_op jit(solution)/shard_map/ppermute | solution.py:374
  61.0 2.5 %collective-permute-start.1 = (bf16[256,128]{1,0:T(8,128)(2,1)S(1)}, bf16[256,128]{1,0:T(8,128)(2,1)S(1)}, u32[]{:S(2)}, u32[]{:S(2)}) collective-permute-start(bf16[256,128]{1,0:T(8,128)(2,1)S(1)} %get-tuple-element.21.own_ref), channel_id=1, source_target_pairs={{0,4},{1,5},{2,6},{3,7},{4,0},{5,1},{6,2},{7,3},{8,12},{9,13},{10,... | collective-permute-start | bytes 196616 | tf_op jit(solution)/shard_map/ppermute | solution.py:374
  63.5 3.1 %collective-permute-start = (bf16[256,128]{1,0:T(8,128)(2,1)S(1)}, bf16[256,128]{1,0:T(8,128)(2,1)S(1)}, u32[]{:S(2)}, u32[]{:S(2)}) collective-permute-start(bf16[256,128]{1,0:T(8,128)(2,1)S(1)} %get-tuple-element.21.own_ref), channel_id=1, source_target_pairs={{0,2},{1,3},{2,0},{3,1},{4,6},{5,7},{6,4},{7,5},{8,10},{9,11},{10,... | collective-permute-start | bytes 196616 | tf_op jit(solution)/shard_map/ppermute | solution.py:374
  66.6 2.3 %collective-permute-done.1.second_ref = bf16[256,128]{1,0:T(8,128)(2,1)S(1)} collective-permute-done((bf16[256,128]{1,0:T(8,128)(2,1)S(1)}, bf16[256,128]{1,0:T(8,128)(2,1)S(1)}, u32[]{:S(2)}, u32[]{:S(2)}) %collective-permute-start.1) | collective-permute-done | bytes 65568 | tf_op jit(solution)/shard_map/ppermute | solution.py:374
  68.9 1.4 collective-permute-done.first_ref
  70.3 0.5 filters.1
  70.8 0.7 all-to-all-done.1.got_ref.mine_ref
  71.5 2.3 %collective-permute-start.3 = (bf16[8,256,128]{2,1,0:T(8,128)(2,1)S(1)}, bf16[8,256,128]{2,1,0:T(8,128)(2,1)S(1)}, u32[]{:S(2)}, u32[]{:S(2)}) collective-permute-start(bf16[8,256,128]{2,1,0:T(8,128)(2,1)S(1)} %slice.19), channel_id=1, source_target_pairs={{0,1},{1,0},{2,3},{3,2},{4,5},{5,4},{6,7},{7,6},{8,9},{9,8},{10,11... | collective-permute-start | bytes 1572872 | tf_op jit(solution)/shard_map/ppermute | solution.py:374
  73.8 1.5 %backward.1 = (f32[8,256,128]{2,1,0:T(8,128)S(1)}, bf16[8,256,128]{2,1,0:T(8,128)(2,1)S(1)}) custom-call(bf16[8,448,128]{2,1,0:T(8,128)(2,1)S(1)} %all-to-all-done.1.got_ref.mine_ref, bf16[128,896]{1,0:T(8,128)(2,1)S(1)} %get-tuple-element.26.filter_ref), custom_call_target="tpu_custom_call" | custom-call | flops 939524096 | bytes 4194304 | tf_op jit(solution)/shard_map/backward/pallas_call | solution.py:427
  75.3 2.3 %collective-permute-start.4 = (bf16[8,256,128]{2,1,0:T(8,128)(2,1)S(1)}, bf16[8,256,128]{2,1,0:T(8,128)(2,1)S(1)}, u32[]{:S(2)}, u32[]{:S(2)}) collective-permute-start(bf16[8,256,128]{2,1,0:T(8,128)(2,1)S(1)} %get-tuple-element.29), channel_id=1, source_target_pairs={{0,1},{1,0},{2,3},{3,2},{4,5},{5,4},{6,7},{7,6},{8,9},{9,8},{10,11... | collective-permute-start | bytes 1572872 | tf_op jit(solution)/shard_map/ppermute | solution.py:374
  77.6 1.5 forward.1.rims_ref
  79.2 1.0 sum.1
  80.2 4.6 %all-to-all-start.2 = ((bf16[8,448,128]{2,1,0:T(8,128)(2,1)}), bf16[8,448,128]{2,1,0:T(8,128)(2,1)S(1)}, u32[]{:S(2)}, u32[]{:S(2)}) async-start(bf16[8,448,128]{2,1,0:T(8,128)(2,1)} %sum.1), calls=%async_computation.2 | async-start | bytes 1835008 | tf_op jit(solution)/shard_map/all_to_all | solution.py:466
  84.7 3.1 %filter_grad.1 = (bf16[512,128]{1,0:T(8,128)(2,1)S(1)}, bf16[512,128]{1,0:T(8,128)(2,1)S(1)}) custom-call(s32[1]{0:T(128)} %bitcast.rank_ref, bf16[8,448,128]{2,1,0:T(8,128)(2,1)S(1)} %all-to-all-done.1.got_ref.mine_ref, bf16[8,256,128]{2,1,0:T(8,128)(2,1)S(1)} %collective-permute-done.3.theirs_ref), custom_call_target="tpu_custom_call" | custom-call | flops 939524096 | bytes 4194304 | tf_op jit(solution)/shard_map/filter_grad/pallas_call | solution.py:457
  87.8 2.8 %collective-permute-start.5 = (bf16[512,128]{1,0:T(8,128)(2,1)S(1)}, bf16[512,128]{1,0:T(8,128)(2,1)S(1)}, u32[]{:S(2)}, u32[]{:S(2)}) collective-permute-start(bf16[512,128]{1,0:T(8,128)(2,1)S(1)} %get-tuple-element.36), channel_id=1, source_target_pairs={{0,2},{1,3},{2,0},{3,1},{4,6},{5,7},{6,4},{7,5},{8,10},{9,11},{10,... | collective-permute-start | bytes 393224 | tf_op jit(solution)/shard_map/ppermute | solution.py:374
  90.6 3.5 %collective-permute-done.5.other_ref = bf16[512,128]{1,0:T(8,128)(2,1)S(1)} collective-permute-done((bf16[512,128]{1,0:T(8,128)(2,1)S(1)}, bf16[512,128]{1,0:T(8,128)(2,1)S(1)}, u32[]{:S(2)}, u32[]{:S(2)}) %collective-permute-start.5) | collective-permute-done | bytes 131104 | tf_op jit(solution)/shard_map/ppermute | solution.py:374
  94.1 4.4 %all-to-all-done.2.got_ref = bf16[8,448,128]{2,1,0:T(8,128)(2,1)S(1)} async-done(((bf16[8,448,128]{2,1,0:T(8,128)(2,1)}), bf16[8,448,128]{2,1,0:T(8,128)(2,1)S(1)}, u32[]{:S(2)}, u32[]{:S(2)}) %all-to-all-start.2) | async-done | bytes 917536 | tf_op jit(solution)/shard_map/all_to_all | solution.py:466
  98.5 0.9 last.1
  99.4 38.1 %all_to_all.26 = bf16[448,4,128]{2,1,0:T(4,128)(2,1)S(1)} all-to-all(bf16[448,4,128]{2,1,0:T(4,128)(2,1)S(1)} %bitcast.28), channel_id=1, replica_groups=mesh['space'=8,'filt'=64] {'filt'}, dimensions={0} | all-to-all | bytes 917504 | tf_op jit(solution)/shard_map/all_to_all | solution.py:475
  137.5 0.9 tail.1
  138.5 3.4 %all-to-all-start.4 = ((f32[8,32,128]{2,1,0:T(8,128)}), f32[8,32,128]{2,1,0:T(8,128)S(1)}, u32[]{:S(2)}, u32[]{:S(2)}) async-start(f32[8,32,128]{2,1,0:T(8,128)} %tail.1), calls=%async_computation.4 | async-start | bytes 262144 | tf_op jit(solution)/shard_map/all_to_all | solution.py:481
  141.9 0.3 copy.17
  142.3 0.1 add_convert_fusion
  142.4 0.1 slice.27
  142.5 0.7 copy.11
  143.3 0.7 copy.13
  144.0 3.4 %all-to-all-done.4 = f32[8,32,128]{2,1,0:T(8,128)S(1)} async-done(((f32[8,32,128]{2,1,0:T(8,128)}), f32[8,32,128]{2,1,0:T(8,128)S(1)}, u32[]{:S(2)}, u32[]{:S(2)}) %all-to-all-start.4) | async-done | bytes 131104 | tf_op jit(solution)/shard_map/all_to_all | solution.py:481
  147.4 1.0 finish.1
  (9 shorter events, 0.4 us)
Async XLA Ops:
  53.1 18.4 %all-to-all-start.1 = ((bf16[8,448,128]{2,1,0:T(8,128)(2,1)}), bf16[8,448,128]{2,1,0:T(8,128)(2,1)S(1)}, u32[]{:S(2)}, u32[]{:S(2)}) async-start(bf16[8,448,128]{2,1,0:T(8,128)(2,1)} %get-tuple-element.24), calls=%async_computation.1 | async-start | bytes 1835008 | tf_op jit(solution)/shard_map/all_to_all | solution.py:414
  57.3 9.3 %collective-permute-start.2 = (bf16[256,128]{1,0:T(8,128)(2,1)S(1)}, bf16[256,128]{1,0:T(8,128)(2,1)S(1)}, u32[]{:S(2)}, u32[]{:S(2)}) collective-permute-start(bf16[256,128]{1,0:T(8,128)(2,1)S(1)} %get-tuple-element.21.own_ref), channel_id=1, source_target_pairs={{0,6},{1,7},{2,4},{3,5},{4,2},{5,3},{6,0},{7,1},{8,14},{9,15},{10,... | collective-permute-start | bytes 196616 | tf_op jit(solution)/shard_map/ppermute | solution.py:374
  61.0 7.9 %collective-permute-start.1 = (bf16[256,128]{1,0:T(8,128)(2,1)S(1)}, bf16[256,128]{1,0:T(8,128)(2,1)S(1)}, u32[]{:S(2)}, u32[]{:S(2)}) collective-permute-start(bf16[256,128]{1,0:T(8,128)(2,1)S(1)} %get-tuple-element.21.own_ref), channel_id=1, source_target_pairs={{0,4},{1,5},{2,6},{3,7},{4,0},{5,1},{6,2},{7,3},{8,12},{9,13},{10,... | collective-permute-start | bytes 196616 | tf_op jit(solution)/shard_map/ppermute | solution.py:374
  63.5 6.9 %collective-permute-start = (bf16[256,128]{1,0:T(8,128)(2,1)S(1)}, bf16[256,128]{1,0:T(8,128)(2,1)S(1)}, u32[]{:S(2)}, u32[]{:S(2)}) collective-permute-start(bf16[256,128]{1,0:T(8,128)(2,1)S(1)} %get-tuple-element.21.own_ref), channel_id=1, source_target_pairs={{0,2},{1,3},{2,0},{3,1},{4,6},{5,7},{6,4},{7,5},{8,10},{9,11},{10,... | collective-permute-start | bytes 196616 | tf_op jit(solution)/shard_map/ppermute | solution.py:374
  71.5 3.8 %collective-permute-start.3 = (bf16[8,256,128]{2,1,0:T(8,128)(2,1)S(1)}, bf16[8,256,128]{2,1,0:T(8,128)(2,1)S(1)}, u32[]{:S(2)}, u32[]{:S(2)}) collective-permute-start(bf16[8,256,128]{2,1,0:T(8,128)(2,1)S(1)} %slice.19), channel_id=1, source_target_pairs={{0,1},{1,0},{2,3},{3,2},{4,5},{5,4},{6,7},{7,6},{8,9},{9,8},{10,11... | collective-permute-start | bytes 1572872 | tf_op jit(solution)/shard_map/ppermute | solution.py:374
  75.3 3.8 %collective-permute-start.4 = (bf16[8,256,128]{2,1,0:T(8,128)(2,1)S(1)}, bf16[8,256,128]{2,1,0:T(8,128)(2,1)S(1)}, u32[]{:S(2)}, u32[]{:S(2)}) collective-permute-start(bf16[8,256,128]{2,1,0:T(8,128)(2,1)S(1)} %get-tuple-element.29), channel_id=1, source_target_pairs={{0,1},{1,0},{2,3},{3,2},{4,5},{5,4},{6,7},{7,6},{8,9},{9,8},{10,11... | collective-permute-start | bytes 1572872 | tf_op jit(solution)/shard_map/ppermute | solution.py:374
  80.2 18.4 %all-to-all-start.2 = ((bf16[8,448,128]{2,1,0:T(8,128)(2,1)}), bf16[8,448,128]{2,1,0:T(8,128)(2,1)S(1)}, u32[]{:S(2)}, u32[]{:S(2)}) async-start(bf16[8,448,128]{2,1,0:T(8,128)(2,1)} %sum.1), calls=%async_computation.2 | async-start | bytes 1835008 | tf_op jit(solution)/shard_map/all_to_all | solution.py:466
  87.8 6.3 %collective-permute-start.5 = (bf16[512,128]{1,0:T(8,128)(2,1)S(1)}, bf16[512,128]{1,0:T(8,128)(2,1)S(1)}, u32[]{:S(2)}, u32[]{:S(2)}) collective-permute-start(bf16[512,128]{1,0:T(8,128)(2,1)S(1)} %get-tuple-element.36), channel_id=1, source_target_pairs={{0,2},{1,3},{2,0},{3,1},{4,6},{5,7},{6,4},{7,5},{8,10},{9,11},{10,... | collective-permute-start | bytes 393224 | tf_op jit(solution)/shard_map/ppermute | solution.py:374
  138.5 8.9 %all-to-all-start.4 = ((f32[8,32,128]{2,1,0:T(8,128)}), f32[8,32,128]{2,1,0:T(8,128)S(1)}, u32[]{:S(2)}, u32[]{:S(2)}) async-start(f32[8,32,128]{2,1,0:T(8,128)} %tail.1), calls=%async_computation.4 | async-start | bytes 262144 | tf_op jit(solution)/shard_map/all_to_all | solution.py:481

commit v8 on v7

--- a/solution.py
+++ b/solution.py
@@ -432,7 +432,6 @@
         [((10, 96, 768), BF16), ((2, 896, 512), BF16)],
         2 * 8 * 896 * 128 * 512,
     )(got, filters)
-    send, theirs = lax.optimization_barrier((send, theirs))
     other = swapped(send, "filt", 1)
     cells = pl.BlockSpec((8, 256, 128), lambda n: (0, 0, 0))
     (out,) = call(

time: 149 us -> 149 us (level)
  no operation moved by 1% of the time
where the time goes in v8:
time: 149 us; the launch traced here: 148 us
  blocking collectives  86.2 us (58%)
  starting transfers between devices  28.6 us (19%)
  waiting for transfers between devices  16.2 us (11%)
  Pallas kernels  14.4 us (10%)
  local copies, waits for them, and re-layouts  2.04 us (1%)
    all_to_all x1, blocking collectives, local(): got = lax.all_to_all(both.reshape(64, 24, 128), 'filt', 0, 0, tiled=True)  48.4 us
    all_to_all x1, blocking collectives, local(): got = lax.all_to_all(both.reshape(448, 4, 128), 'filt', 0, 0, tiled=True)  37.8 us
    ppermute x6, starting transfers between devices, swapped(): return lax.ppermute(array, axis, [(n, n ^ bit) for n in range(count)])  16.4 us
    all_to_all x2, starting transfers between devices, local(): got = lax.all_to_all(both, 'space', 0, 0, tiled=True)  8.82 us
    ppermute x6, waiting for transfers between devices, swapped(): return lax.ppermute(array, axis, [(n, n ^ bit) for n in range(count)])  7.72 us
    all_to_all x2, waiting for transfers between devices, local(): got = lax.all_to_all(both, 'space', 0, 0, tiled=True)  5.08 us
    all_to_all x1, waiting for transfers between devices, local(): lax.all_to_all(terms, 'space', 0, 0, tiled=True).reshape(8, 4, 8, 128)  3.43 us
    all_to_all x1, starting transfers between devices, local(): lax.all_to_all(terms, 'space', 0, 0, tiled=True).reshape(8, 4, 8, 128)  3.38 us
  transfers between devices with their start and end apart: 9, of which 7 were waited for; matrix products, arithmetic and copies ran while one was open for 1% of the time, Pallas kernels for 4%

profile of v8, /device:TPU:1, one launch (start us, length us, event | category | flops | bytes accessed | tf_op | source)
XLA Modules:
  0.0 148.4 jit_solution(12913508931524135515)
XLA Ops:
  0.6 2.7 %first.1 = bf16[1536,128]{1,0:T(8,128)(2,1)} custom-call(f32[1,4]{1,0:T(1,128)} %bitcast.41, bf16[4,128,128]{2,1,0:T(8,128)(2,1)} %bitcast.35, bf16[4,128,128]{2,1,0:T(8,128)(2,1)} %bitcast.36, bf16[27,4,256]{2,1,0:T(4,128)(2,1)} %bitcast.40), custom_call_target="tpu_custom_call" | custom-call | flops 163577856 | bytes 4194304 | tf_op jit(solution)/shard_map/first/pallas_call | solution.py:380
  3.3 48.4 %all_to_all.25 = bf16[64,24,128]{2,1,0:T(8,128)(2,1)S(1)} all-to-all(bf16[64,24,128]{2,1,0:T(8,128)(2,1)} %bitcast.32), channel_id=1, replica_groups=mesh['space'=8,'filt'=64] {'filt'}, dimensions={0} | all-to-all | bytes 786432 | tf_op jit(solution)/shard_map/all_to_all | solution.py:403
  51.7 1.4 middle.1
  53.1 4.2 %all-to-all-start.1 = ((bf16[8,448,128]{2,1,0:T(8,128)(2,1)}), bf16[8,448,128]{2,1,0:T(8,128)(2,1)S(1)}, u32[]{:S(2)}, u32[]{:S(2)}) async-start(bf16[8,448,128]{2,1,0:T(8,128)(2,1)} %get-tuple-element.22), calls=%async_computation.1 | async-start | bytes 1835008 | tf_op jit(solution)/shard_map/all_to_all | solution.py:414
  57.3 3.7 %collective-permute-start.2 = (bf16[256,128]{1,0:T(8,128)(2,1)S(1)}, bf16[256,128]{1,0:T(8,128)(2,1)S(1)}, u32[]{:S(2)}, u32[]{:S(2)}) collective-permute-start(bf16[256,128]{1,0:T(8,128)(2,1)S(1)} %get-tuple-element.19.own_ref), channel_id=1, source_target_pairs={{0,6},{1,7},{2,4},{3,5},{4,2},{5,3},{6,0},{7,1},{8,14},{9,15},{10,... | collective-permute-start | bytes 196616 | tf_op jit(solution)/shard_map/ppermute | solution.py:374
  61.0 2.5 %collective-permute-start.1 = (bf16[256,128]{1,0:T(8,128)(2,1)S(1)}, bf16[256,128]{1,0:T(8,128)(2,1)S(1)}, u32[]{:S(2)}, u32[]{:S(2)}) collective-permute-start(bf16[256,128]{1,0:T(8,128)(2,1)S(1)} %get-tuple-element.19.own_ref), channel_id=1, source_target_pairs={{0,4},{1,5},{2,6},{3,7},{4,0},{5,1},{6,2},{7,3},{8,12},{9,13},{10,... | collective-permute-start | bytes 196616 | tf_op jit(solution)/shard_map/ppermute | solution.py:374
  63.5 3.1 %collective-permute-start = (bf16[256,128]{1,0:T(8,128)(2,1)S(1)}, bf16[256,128]{1,0:T(8,128)(2,1)S(1)}, u32[]{:S(2)}, u32[]{:S(2)}) collective-permute-start(bf16[256,128]{1,0:T(8,128)(2,1)S(1)} %get-tuple-element.19.own_ref), channel_id=1, source_target_pairs={{0,2},{1,3},{2,0},{3,1},{4,6},{5,7},{6,4},{7,5},{8,10},{9,11},{10,... | collective-permute-start | bytes 196616 | tf_op jit(solution)/shard_map/ppermute | solution.py:374
  66.6 2.3 %collective-permute-done.1.second_ref = bf16[256,128]{1,0:T(8,128)(2,1)S(1)} collective-permute-done((bf16[256,128]{1,0:T(8,128)(2,1)S(1)}, bf16[256,128]{1,0:T(8,128)(2,1)S(1)}, u32[]{:S(2)}, u32[]{:S(2)}) %collective-permute-start.1) | collective-permute-done | bytes 65568 | tf_op jit(solution)/shard_map/ppermute | solution.py:374
  68.9 1.4 collective-permute-done.first_ref
  70.3 0.5 filters.1
  70.8 0.7 all-to-all-done.1.got_ref.mine_ref
  71.5 2.3 %collective-permute-start.4 = (bf16[8,256,128]{2,1,0:T(8,128)(2,1)S(1)}, bf16[8,256,128]{2,1,0:T(8,128)(2,1)S(1)}, u32[]{:S(2)}, u32[]{:S(2)}) collective-permute-start(bf16[8,256,128]{2,1,0:T(8,128)(2,1)S(1)} %slice.19), channel_id=1, source_target_pairs={{0,1},{1,0},{2,3},{3,2},{4,5},{5,4},{6,7},{7,6},{8,9},{9,8},{10,11... | collective-permute-start | bytes 1572872 | tf_op jit(solution)/shard_map/ppermute | solution.py:374
  73.8 1.5 %backward.1 = (f32[8,256,128]{2,1,0:T(8,128)S(1)}, bf16[8,256,128]{2,1,0:T(8,128)(2,1)S(1)}) custom-call(bf16[8,448,128]{2,1,0:T(8,128)(2,1)S(1)} %all-to-all-done.1.got_ref.mine_ref, bf16[128,896]{1,0:T(8,128)(2,1)S(1)} %get-tuple-element.24.filter_ref), custom_call_target="tpu_custom_call" | custom-call | flops 939524096 | bytes 4194304 | tf_op jit(solution)/shard_map/backward/pallas_call | solution.py:427
  75.3 2.0 %collective-permute-start.3 = (bf16[8,256,128]{2,1,0:T(8,128)(2,1)S(1)}, bf16[8,256,128]{2,1,0:T(8,128)(2,1)S(1)}, u32[]{:S(2)}, u32[]{:S(2)}) collective-permute-start(bf16[8,256,128]{2,1,0:T(8,128)(2,1)S(1)} %get-tuple-element.26), channel_id=1, source_target_pairs={{0,1},{1,0},{2,3},{3,2},{4,5},{5,4},{6,7},{7,6},{8,9},{9,8},{10,11... | collective-permute-start | bytes 1572872 | tf_op jit(solution)/shard_map/ppermute | solution.py:374
  77.4 1.5 forward.1.rims_ref
  78.9 0.3 collective-permute-done.3.other_ref
  79.1 1.0 sum.1
  80.1 4.6 %all-to-all-start.2 = ((bf16[8,448,128]{2,1,0:T(8,128)(2,1)}), bf16[8,448,128]{2,1,0:T(8,128)(2,1)S(1)}, u32[]{:S(2)}, u32[]{:S(2)}) async-start(bf16[8,448,128]{2,1,0:T(8,128)(2,1)} %sum.1), calls=%async_computation.2 | async-start | bytes 1835008 | tf_op jit(solution)/shard_map/all_to_all | solution.py:465
  84.7 3.1 %filter_grad.1 = (bf16[512,128]{1,0:T(8,128)(2,1)S(1)}, bf16[512,128]{1,0:T(8,128)(2,1)S(1)}) custom-call(s32[1]{0:T(128)} %bitcast.rank_ref, bf16[8,448,128]{2,1,0:T(8,128)(2,1)S(1)} %all-to-all-done.1.got_ref.mine_ref, bf16[8,256,128]{2,1,0:T(8,128)(2,1)S(1)} %collective-permute-done.4.theirs_ref), custom_call_target="tpu_custom_call" | custom-call | flops 939524096 | bytes 4194304 | tf_op jit(solution)/shard_map/filter_grad/pallas_call | solution.py:456
  87.8 2.8 %collective-permute-start.5 = (bf16[512,128]{1,0:T(8,128)(2,1)S(1)}, bf16[512,128]{1,0:T(8,128)(2,1)S(1)}, u32[]{:S(2)}, u32[]{:S(2)}) collective-permute-start(bf16[512,128]{1,0:T(8,128)(2,1)S(1)} %get-tuple-element.32), channel_id=1, source_target_pairs={{0,2},{1,3},{2,0},{3,1},{4,6},{5,7},{6,4},{7,5},{8,10},{9,11},{10,... | collective-permute-start | bytes 393224 | tf_op jit(solution)/shard_map/ppermute | solution.py:374
  90.6 3.7 %collective-permute-done.5.other_ref = bf16[512,128]{1,0:T(8,128)(2,1)S(1)} collective-permute-done((bf16[512,128]{1,0:T(8,128)(2,1)S(1)}, bf16[512,128]{1,0:T(8,128)(2,1)S(1)}, u32[]{:S(2)}, u32[]{:S(2)}) %collective-permute-start.5) | collective-permute-done | bytes 131104 | tf_op jit(solution)/shard_map/ppermute | solution.py:374
  94.3 4.4 %all-to-all-done.2.got_ref = bf16[8,448,128]{2,1,0:T(8,128)(2,1)S(1)} async-done(((bf16[8,448,128]{2,1,0:T(8,128)(2,1)}), bf16[8,448,128]{2,1,0:T(8,128)(2,1)S(1)}, u32[]{:S(2)}, u32[]{:S(2)}) %all-to-all-start.2) | async-done | bytes 917536 | tf_op jit(solution)/shard_map/all_to_all | solution.py:465
  98.8 0.9 last.1
  99.7 37.8 %all_to_all.26 = bf16[448,4,128]{2,1,0:T(4,128)(2,1)S(1)} all-to-all(bf16[448,4,128]{2,1,0:T(4,128)(2,1)S(1)} %bitcast.28), channel_id=1, replica_groups=mesh['space'=8,'filt'=64] {'filt'}, dimensions={0} | all-to-all | bytes 917504 | tf_op jit(solution)/shard_map/all_to_all | solution.py:474
  137.5 0.9 tail.1
  138.5 3.4 %all-to-all-start.4 = ((f32[8,32,128]{2,1,0:T(8,128)}), f32[8,32,128]{2,1,0:T(8,128)S(1)}, u32[]{:S(2)}, u32[]{:S(2)}) async-start(f32[8,32,128]{2,1,0:T(8,128)} %tail.1), calls=%async_computation.4 | async-start | bytes 262144 | tf_op jit(solution)/shard_map/all_to_all | solution.py:480
  141.9 0.3 copy.17
  142.3 0.1 add_convert_fusion
  142.5 0.7 copy.11
  143.2 0.7 copy.13
  144.0 3.4 %all-to-all-done.4 = f32[8,32,128]{2,1,0:T(8,128)S(1)} async-done(((f32[8,32,128]{2,1,0:T(8,128)}), f32[8,32,128]{2,1,0:T(8,128)S(1)}, u32[]{:S(2)}, u32[]{:S(2)}) %all-to-all-start.4) | async-done | bytes 131104 | tf_op jit(solution)/shard_map/all_to_all | solution.py:480
  147.4 1.0 finish.1
  (9 shorter events, 0.4 us)
Async XLA Ops:
  53.1 18.4 %all-to-all-start.1 = ((bf16[8,448,128]{2,1,0:T(8,128)(2,1)}), bf16[8,448,128]{2,1,0:T(8,128)(2,1)S(1)}, u32[]{:S(2)}, u32[]{:S(2)}) async-start(bf16[8,448,128]{2,1,0:T(8,128)(2,1)} %get-tuple-element.22), calls=%async_computation.1 | async-start | bytes 1835008 | tf_op jit(solution)/shard_map/all_to_all | solution.py:414
  57.3 9.3 %collective-permute-start.2 = (bf16[256,128]{1,0:T(8,128)(2,1)S(1)}, bf16[256,128]{1,0:T(8,128)(2,1)S(1)}, u32[]{:S(2)}, u32[]{:S(2)}) collective-permute-start(bf16[256,128]{1,0:T(8,128)(2,1)S(1)} %get-tuple-element.19.own_ref), channel_id=1, source_target_pairs={{0,6},{1,7},{2,4},{3,5},{4,2},{5,3},{6,0},{7,1},{8,14},{9,15},{10,... | collective-permute-start | bytes 196616 | tf_op jit(solution)/shard_map/ppermute | solution.py:374
  61.0 7.9 %collective-permute-start.1 = (bf16[256,128]{1,0:T(8,128)(2,1)S(1)}, bf16[256,128]{1,0:T(8,128)(2,1)S(1)}, u32[]{:S(2)}, u32[]{:S(2)}) collective-permute-start(bf16[256,128]{1,0:T(8,128)(2,1)S(1)} %get-tuple-element.19.own_ref), channel_id=1, source_target_pairs={{0,4},{1,5},{2,6},{3,7},{4,0},{5,1},{6,2},{7,3},{8,12},{9,13},{10,... | collective-permute-start | bytes 196616 | tf_op jit(solution)/shard_map/ppermute | solution.py:374
  63.5 6.9 %collective-permute-start = (bf16[256,128]{1,0:T(8,128)(2,1)S(1)}, bf16[256,128]{1,0:T(8,128)(2,1)S(1)}, u32[]{:S(2)}, u32[]{:S(2)}) collective-permute-start(bf16[256,128]{1,0:T(8,128)(2,1)S(1)} %get-tuple-element.19.own_ref), channel_id=1, source_target_pairs={{0,2},{1,3},{2,0},{3,1},{4,6},{5,7},{6,4},{7,5},{8,10},{9,11},{10,... | collective-permute-start | bytes 196616 | tf_op jit(solution)/shard_map/ppermute | solution.py:374
  71.5 5.9 %collective-permute-start.4 = (bf16[8,256,128]{2,1,0:T(8,128)(2,1)S(1)}, bf16[8,256,128]{2,1,0:T(8,128)(2,1)S(1)}, u32[]{:S(2)}, u32[]{:S(2)}) collective-permute-start(bf16[8,256,128]{2,1,0:T(8,128)(2,1)S(1)} %slice.19), channel_id=1, source_target_pairs={{0,1},{1,0},{2,3},{3,2},{4,5},{5,4},{6,7},{7,6},{8,9},{9,8},{10,11... | collective-permute-start | bytes 1572872 | tf_op jit(solution)/shard_map/ppermute | solution.py:374
  75.3 3.8 %collective-permute-start.3 = (bf16[8,256,128]{2,1,0:T(8,128)(2,1)S(1)}, bf16[8,256,128]{2,1,0:T(8,128)(2,1)S(1)}, u32[]{:S(2)}, u32[]{:S(2)}) collective-permute-start(bf16[8,256,128]{2,1,0:T(8,128)(2,1)S(1)} %get-tuple-element.26), channel_id=1, source_target_pairs={{0,1},{1,0},{2,3},{3,2},{4,5},{5,4},{6,7},{7,6},{8,9},{9,8},{10,11... | collective-permute-start | bytes 1572872 | tf_op jit(solution)/shard_map/ppermute | solution.py:374
  80.1 18.6 %all-to-all-start.2 = ((bf16[8,448,128]{2,1,0:T(8,128)(2,1)}), bf16[8,448,128]{2,1,0:T(8,128)(2,1)S(1)}, u32[]{:S(2)}, u32[]{:S(2)}) async-start(bf16[8,448,128]{2,1,0:T(8,128)(2,1)} %sum.1), calls=%async_computation.2 | async-start | bytes 1835008 | tf_op jit(solution)/shard_map/all_to_all | solution.py:465
  87.8 6.5 %collective-permute-start.5 = (bf16[512,128]{1,0:T(8,128)(2,1)S(1)}, bf16[512,128]{1,0:T(8,128)(2,1)S(1)}, u32[]{:S(2)}, u32[]{:S(2)}) collective-permute-start(bf16[512,128]{1,0:T(8,128)(2,1)S(1)} %get-tuple-element.32), channel_id=1, source_target_pairs={{0,2},{1,3},{2,0},{3,1},{4,6},{5,7},{6,4},{7,5},{8,10},{9,11},{10,... | collective-permute-start | bytes 393224 | tf_op jit(solution)/shard_map/ppermute | solution.py:374
  138.5 8.9 %all-to-all-start.4 = ((f32[8,32,128]{2,1,0:T(8,128)}), f32[8,32,128]{2,1,0:T(8,128)S(1)}, u32[]{:S(2)}, u32[]{:S(2)}) async-start(f32[8,32,128]{2,1,0:T(8,128)} %tail.1), calls=%async_computation.4 | async-start | bytes 262144 | tf_op jit(solution)/shard_map/all_to_all | solution.py:480

commit v9 on v8

--- a/solution.py
+++ b/solution.py
@@ -180,15 +180,15 @@
 
 
 def forward_kernel(mine_ref, theirs_ref, stacked_ref, out_ref, planes):
-    planes[0] = jnp.zeros((128, 512), BF16)
-    planes[9] = jnp.zeros((128, 512), BF16)
     for z in range(8):
         planes[z + 1] = plane_of(mine_ref, theirs_ref, z)
     column = lax.broadcasted_iota(jnp.int32, (32, 128), 1)
 
     def plane(z):
-        near = jnp.concatenate([planes[z], planes[z + 1], planes[z + 2]], axis=0)
-        terms = jnp.dot(stacked_ref[...], near, preferred_element_type=F32)
+        taps = range(1 if z == 0 else 0, 2 if z == 7 else 3)
+        near = jnp.concatenate([planes[z + tap] for tap in taps], axis=0)
+        used = stacked_ref[:, taps[0] * 128 : taps[-1] * 128 + 128]
+        terms = jnp.dot(used, near, preferred_element_type=F32)
         for row in range(6):
             sums = []
             for e in range(3):

time: 149 us -> 149 us (level)
  no operation moved by 1% of the time
where the time goes in v9:
time: 149 us; the launch traced here: 148 us
  blocking collectives  86.2 us (58%)
  starting transfers between devices  28.6 us (19%)
  waiting for transfers between devices  16.4 us (11%)
  Pallas kernels  14.2 us (10%)
  local copies, waits for them, and re-layouts  2.04 us (1%)
    all_to_all x1, blocking collectives, local(): got = lax.all_to_all(both.reshape(64, 24, 128), 'filt', 0, 0, tiled=True)  48.4 us
    all_to_all x1, blocking collectives, local(): got = lax.all_to_all(both.reshape(448, 4, 128), 'filt', 0, 0, tiled=True)  37.8 us
    ppermute x6, starting transfers between devices, swapped(): return lax.ppermute(array, axis, [(n, n ^ bit) for n in range(count)])  16.4 us
    all_to_all x2, starting transfers between devices, local(): got = lax.all_to_all(both, 'space', 0, 0, tiled=True)  8.82 us
    ppermute x6, waiting for transfers between devices, swapped(): return lax.ppermute(array, axis, [(n, n ^ bit) for n in range(count)])  7.85 us
    all_to_all x2, waiting for transfers between devices, local(): got = lax.all_to_all(both, 'space', 0, 0, tiled=True)  5.08 us
    all_to_all x1, waiting for transfers between devices, local(): lax.all_to_all(terms, 'space', 0, 0, tiled=True).reshape(8, 4, 8, 128)  3.43 us
    all_to_all x1, starting transfers between devices, local(): lax.all_to_all(terms, 'space', 0, 0, tiled=True).reshape(8, 4, 8, 128)  3.38 us
  transfers between devices with their start and end apart: 9, of which 7 were waited for; matrix products, arithmetic and copies ran while one was open for 1% of the time, Pallas kernels for 4%

profile of v9, /device:TPU:1, one launch (start us, length us, event | category | flops | bytes accessed | tf_op | source)
XLA Modules:
  0.0 148.4 jit_solution(13106464327545597193)
XLA Ops:
  0.6 2.7 %first.1 = bf16[1536,128]{1,0:T(8,128)(2,1)} custom-call(f32[1,4]{1,0:T(1,128)} %bitcast.41, bf16[4,128,128]{2,1,0:T(8,128)(2,1)} %bitcast.35, bf16[4,128,128]{2,1,0:T(8,128)(2,1)} %bitcast.36, bf16[27,4,256]{2,1,0:T(4,128)(2,1)} %bitcast.40), custom_call_target="tpu_custom_call" | custom-call | flops 163577856 | bytes 4194304 | tf_op jit(solution)/shard_map/first/pallas_call | solution.py:380
  3.3 48.4 %all_to_all.25 = bf16[64,24,128]{2,1,0:T(8,128)(2,1)S(1)} all-to-all(bf16[64,24,128]{2,1,0:T(8,128)(2,1)} %bitcast.32), channel_id=1, replica_groups=mesh['space'=8,'filt'=64] {'filt'}, dimensions={0} | all-to-all | bytes 786432 | tf_op jit(solution)/shard_map/all_to_all | solution.py:403
  51.7 1.4 middle.1
  53.1 4.2 %all-to-all-start.1 = ((bf16[8,448,128]{2,1,0:T(8,128)(2,1)}), bf16[8,448,128]{2,1,0:T(8,128)(2,1)S(1)}, u32[]{:S(2)}, u32[]{:S(2)}) async-start(bf16[8,448,128]{2,1,0:T(8,128)(2,1)} %get-tuple-element.22), calls=%async_computation.1 | async-start | bytes 1835008 | tf_op jit(solution)/shard_map/all_to_all | solution.py:414
  57.3 3.7 %collective-permute-start.2 = (bf16[256,128]{1,0:T(8,128)(2,1)S(1)}, bf16[256,128]{1,0:T(8,128)(2,1)S(1)}, u32[]{:S(2)}, u32[]{:S(2)}) collective-permute-start(bf16[256,128]{1,0:T(8,128)(2,1)S(1)} %get-tuple-element.19.own_ref), channel_id=1, source_target_pairs={{0,6},{1,7},{2,4},{3,5},{4,2},{5,3},{6,0},{7,1},{8,14},{9,15},{10,... | collective-permute-start | bytes 196616 | tf_op jit(solution)/shard_map/ppermute | solution.py:374
  61.0 2.5 %collective-permute-start.1 = (bf16[256,128]{1,0:T(8,128)(2,1)S(1)}, bf16[256,128]{1,0:T(8,128)(2,1)S(1)}, u32[]{:S(2)}, u32[]{:S(2)}) collective-permute-start(bf16[256,128]{1,0:T(8,128)(2,1)S(1)} %get-tuple-element.19.own_ref), channel_id=1, source_target_pairs={{0,4},{1,5},{2,6},{3,7},{4,0},{5,1},{6,2},{7,3},{8,12},{9,13},{10,... | collective-permute-start | bytes 196616 | tf_op jit(solution)/shard_map/ppermute | solution.py:374
  63.5 3.1 %collective-permute-start = (bf16[256,128]{1,0:T(8,128)(2,1)S(1)}, bf16[256,128]{1,0:T(8,128)(2,1)S(1)}, u32[]{:S(2)}, u32[]{:S(2)}) collective-permute-start(bf16[256,128]{1,0:T(8,128)(2,1)S(1)} %get-tuple-element.19.own_ref), channel_id=1, source_target_pairs={{0,2},{1,3},{2,0},{3,1},{4,6},{5,7},{6,4},{7,5},{8,10},{9,11},{10,... | collective-permute-start | bytes 196616 | tf_op jit(solution)/shard_map/ppermute | solution.py:374
  66.6 2.3 %collective-permute-done.1.second_ref = bf16[256,128]{1,0:T(8,128)(2,1)S(1)} collective-permute-done((bf16[256,128]{1,0:T(8,128)(2,1)S(1)}, bf16[256,128]{1,0:T(8,128)(2,1)S(1)}, u32[]{:S(2)}, u32[]{:S(2)}) %collective-permute-start.1) | collective-permute-done | bytes 65568 | tf_op jit(solution)/shard_map/ppermute | solution.py:374
  68.9 1.4 collective-permute-done.first_ref
  70.3 0.5 filters.1
  70.8 0.7 all-to-all-done.1.got_ref.mine_ref
  71.5 2.3 %collective-permute-start.4 = (bf16[8,256,128]{2,1,0:T(8,128)(2,1)S(1)}, bf16[8,256,128]{2,1,0:T(8,128)(2,1)S(1)}, u32[]{:S(2)}, u32[]{:S(2)}) collective-permute-start(bf16[8,256,128]{2,1,0:T(8,128)(2,1)S(1)} %slice.19), channel_id=1, source_target_pairs={{0,1},{1,0},{2,3},{3,2},{4,5},{5,4},{6,7},{7,6},{8,9},{9,8},{10,11... | collective-permute-start | bytes 1572872 | tf_op jit(solution)/shard_map/ppermute | solution.py:374
  73.8 1.5 %backward.1 = (f32[8,256,128]{2,1,0:T(8,128)S(1)}, bf16[8,256,128]{2,1,0:T(8,128)(2,1)S(1)}) custom-call(bf16[8,448,128]{2,1,0:T(8,128)(2,1)S(1)} %all-to-all-done.1.got_ref.mine_ref, bf16[128,896]{1,0:T(8,128)(2,1)S(1)} %get-tuple-element.24.filter_ref), custom_call_target="tpu_custom_call" | custom-call | flops 939524096 | bytes 4194304 | tf_op jit(solution)/shard_map/backward/pallas_call | solution.py:427
  75.3 2.0 %collective-permute-start.3 = (bf16[8,256,128]{2,1,0:T(8,128)(2,1)S(1)}, bf16[8,256,128]{2,1,0:T(8,128)(2,1)S(1)}, u32[]{:S(2)}, u32[]{:S(2)}) collective-permute-start(bf16[8,256,128]{2,1,0:T(8,128)(2,1)S(1)} %get-tuple-element.26), channel_id=1, source_target_pairs={{0,1},{1,0},{2,3},{3,2},{4,5},{5,4},{6,7},{7,6},{8,9},{9,8},{10,11... | collective-permute-start | bytes 1572872 | tf_op jit(solution)/shard_map/ppermute | solution.py:374
  77.4 1.3 forward.1.rims_ref
  78.8 0.4 collective-permute-done.3.other_ref
  79.1 1.0 sum.1
  80.1 4.6 %all-to-all-start.2 = ((bf16[8,448,128]{2,1,0:T(8,128)(2,1)}), bf16[8,448,128]{2,1,0:T(8,128)(2,1)S(1)}, u32[]{:S(2)}, u32[]{:S(2)}) async-start(bf16[8,448,128]{2,1,0:T(8,128)(2,1)} %sum.1), calls=%async_computation.2 | async-start | bytes 1835008 | tf_op jit(solution)/shard_map/all_to_all | solution.py:465
  84.7 3.1 %filter_grad.1 = (bf16[512,128]{1,0:T(8,128)(2,1)S(1)}, bf16[512,128]{1,0:T(8,128)(2,1)S(1)}) custom-call(s32[1]{0:T(128)} %bitcast.rank_ref, bf16[8,448,128]{2,1,0:T(8,128)(2,1)S(1)} %all-to-all-done.1.got_ref.mine_ref, bf16[8,256,128]{2,1,0:T(8,128)(2,1)S(1)} %collective-permute-done.4.theirs_ref), custom_call_target="tpu_custom_call" | custom-call | flops 939524096 | bytes 4194304 | tf_op jit(solution)/shard_map/filter_grad/pallas_call | solution.py:456
  87.8 2.8 %collective-permute-start.5 = (bf16[512,128]{1,0:T(8,128)(2,1)S(1)}, bf16[512,128]{1,0:T(8,128)(2,1)S(1)}, u32[]{:S(2)}, u32[]{:S(2)}) collective-permute-start(bf16[512,128]{1,0:T(8,128)(2,1)S(1)} %get-tuple-element.32), channel_id=1, source_target_pairs={{0,2},{1,3},{2,0},{3,1},{4,6},{5,7},{6,4},{7,5},{8,10},{9,11},{10,... | collective-permute-start | bytes 393224 | tf_op jit(solution)/shard_map/ppermute | solution.py:374
  90.6 3.7 %collective-permute-done.5.other_ref = bf16[512,128]{1,0:T(8,128)(2,1)S(1)} collective-permute-done((bf16[512,128]{1,0:T(8,128)(2,1)S(1)}, bf16[512,128]{1,0:T(8,128)(2,1)S(1)}, u32[]{:S(2)}, u32[]{:S(2)}) %collective-permute-start.5) | collective-permute-done | bytes 131104 | tf_op jit(solution)/shard_map/ppermute | solution.py:374
  94.3 4.4 %all-to-all-done.2.got_ref = bf16[8,448,128]{2,1,0:T(8,128)(2,1)S(1)} async-done(((bf16[8,448,128]{2,1,0:T(8,128)(2,1)}), bf16[8,448,128]{2,1,0:T(8,128)(2,1)S(1)}, u32[]{:S(2)}, u32[]{:S(2)}) %all-to-all-start.2) | async-done | bytes 917536 | tf_op jit(solution)/shard_map/all_to_all | solution.py:465
  98.8 0.9 last.1
  99.7 37.8 %all_to_all.26 = bf16[448,4,128]{2,1,0:T(4,128)(2,1)S(1)} all-to-all(bf16[448,4,128]{2,1,0:T(4,128)(2,1)S(1)} %bitcast.28), channel_id=1, replica_groups=mesh['space'=8,'filt'=64] {'filt'}, dimensions={0} | all-to-all | bytes 917504 | tf_op jit(solution)/shard_map/all_to_all | solution.py:474
  137.5 0.9 tail.1
  138.5 3.4 %all-to-all-start.4 = ((f32[8,32,128]{2,1,0:T(8,128)}), f32[8,32,128]{2,1,0:T(8,128)S(1)}, u32[]{:S(2)}, u32[]{:S(2)}) async-start(f32[8,32,128]{2,1,0:T(8,128)} %tail.1), calls=%async_computation.4 | async-start | bytes 262144 | tf_op jit(solution)/shard_map/all_to_all | solution.py:480
  141.9 0.3 copy.17
  142.3 0.1 add_convert_fusion
  142.5 0.7 copy.11
  143.2 0.7 copy.13
  144.0 3.4 %all-to-all-done.4 = f32[8,32,128]{2,1,0:T(8,128)S(1)} async-done(((f32[8,32,128]{2,1,0:T(8,128)}), f32[8,32,128]{2,1,0:T(8,128)S(1)}, u32[]{:S(2)}, u32[]{:S(2)}) %all-to-all-start.4) | async-done | bytes 131104 | tf_op jit(solution)/shard_map/all_to_all | solution.py:480
  147.4 1.0 finish.1
  (9 shorter events, 0.4 us)
Async XLA Ops:
  53.1 18.4 %all-to-all-start.1 = ((bf16[8,448,128]{2,1,0:T(8,128)(2,1)}), bf16[8,448,128]{2,1,0:T(8,128)(2,1)S(1)}, u32[]{:S(2)}, u32[]{:S(2)}) async-start(bf16[8,448,128]{2,1,0:T(8,128)(2,1)} %get-tuple-element.22), calls=%async_computation.1 | async-start | bytes 1835008 | tf_op jit(solution)/shard_map/all_to_all | solution.py:414
  57.3 9.3 %collective-permute-start.2 = (bf16[256,128]{1,0:T(8,128)(2,1)S(1)}, bf16[256,128]{1,0:T(8,128)(2,1)S(1)}, u32[]{:S(2)}, u32[]{:S(2)}) collective-permute-start(bf16[256,128]{1,0:T(8,128)(2,1)S(1)} %get-tuple-element.19.own_ref), channel_id=1, source_target_pairs={{0,6},{1,7},{2,4},{3,5},{4,2},{5,3},{6,0},{7,1},{8,14},{9,15},{10,... | collective-permute-start | bytes 196616 | tf_op jit(solution)/shard_map/ppermute | solution.py:374
  61.0 7.9 %collective-permute-start.1 = (bf16[256,128]{1,0:T(8,128)(2,1)S(1)}, bf16[256,128]{1,0:T(8,128)(2,1)S(1)}, u32[]{:S(2)}, u32[]{:S(2)}) collective-permute-start(bf16[256,128]{1,0:T(8,128)(2,1)S(1)} %get-tuple-element.19.own_ref), channel_id=1, source_target_pairs={{0,4},{1,5},{2,6},{3,7},{4,0},{5,1},{6,2},{7,3},{8,12},{9,13},{10,... | collective-permute-start | bytes 196616 | tf_op jit(solution)/shard_map/ppermute | solution.py:374
  63.5 6.9 %collective-permute-start = (bf16[256,128]{1,0:T(8,128)(2,1)S(1)}, bf16[256,128]{1,0:T(8,128)(2,1)S(1)}, u32[]{:S(2)}, u32[]{:S(2)}) collective-permute-start(bf16[256,128]{1,0:T(8,128)(2,1)S(1)} %get-tuple-element.19.own_ref), channel_id=1, source_target_pairs={{0,2},{1,3},{2,0},{3,1},{4,6},{5,7},{6,4},{7,5},{8,10},{9,11},{10,... | collective-permute-start | bytes 196616 | tf_op jit(solution)/shard_map/ppermute | solution.py:374
  71.5 5.9 %collective-permute-start.4 = (bf16[8,256,128]{2,1,0:T(8,128)(2,1)S(1)}, bf16[8,256,128]{2,1,0:T(8,128)(2,1)S(1)}, u32[]{:S(2)}, u32[]{:S(2)}) collective-permute-start(bf16[8,256,128]{2,1,0:T(8,128)(2,1)S(1)} %slice.19), channel_id=1, source_target_pairs={{0,1},{1,0},{2,3},{3,2},{4,5},{5,4},{6,7},{7,6},{8,9},{9,8},{10,11... | collective-permute-start | bytes 1572872 | tf_op jit(solution)/shard_map/ppermute | solution.py:374
  75.3 3.8 %collective-permute-start.3 = (bf16[8,256,128]{2,1,0:T(8,128)(2,1)S(1)}, bf16[8,256,128]{2,1,0:T(8,128)(2,1)S(1)}, u32[]{:S(2)}, u32[]{:S(2)}) collective-permute-start(bf16[8,256,128]{2,1,0:T(8,128)(2,1)S(1)} %get-tuple-element.26), channel_id=1, source_target_pairs={{0,1},{1,0},{2,3},{3,2},{4,5},{5,4},{6,7},{7,6},{8,9},{9,8},{10,11... | collective-permute-start | bytes 1572872 | tf_op jit(solution)/shard_map/ppermute | solution.py:374
  80.1 18.6 %all-to-all-start.2 = ((bf16[8,448,128]{2,1,0:T(8,128)(2,1)}), bf16[8,448,128]{2,1,0:T(8,128)(2,1)S(1)}, u32[]{:S(2)}, u32[]{:S(2)}) async-start(bf16[8,448,128]{2,1,0:T(8,128)(2,1)} %sum.1), calls=%async_computation.2 | async-start | bytes 1835008 | tf_op jit(solution)/shard_map/all_to_all | solution.py:465
  87.8 6.5 %collective-permute-start.5 = (bf16[512,128]{1,0:T(8,128)(2,1)S(1)}, bf16[512,128]{1,0:T(8,128)(2,1)S(1)}, u32[]{:S(2)}, u32[]{:S(2)}) collective-permute-start(bf16[512,128]{1,0:T(8,128)(2,1)S(1)} %get-tuple-element.32), channel_id=1, source_target_pairs={{0,2},{1,3},{2,0},{3,1},{4,6},{5,7},{6,4},{7,5},{8,10},{9,11},{10,... | collective-permute-start | bytes 393224 | tf_op jit(solution)/shard_map/ppermute | solution.py:374
  138.5 8.9 %all-to-all-start.4 = ((f32[8,32,128]{2,1,0:T(8,128)}), f32[8,32,128]{2,1,0:T(8,128)S(1)}, u32[]{:S(2)}, u32[]{:S(2)}) async-start(f32[8,32,128]{2,1,0:T(8,128)} %tail.1), calls=%async_computation.4 | async-start | bytes 262144 | tf_op jit(solution)/shard_map/all_to_all | solution.py:480
